TPU v7x, 32 devices: a whole 2x2x4 slice. The times are simulated.
32 devices in a mesh: dp: 8 (over y, x, core), fsdp: 4 (over z).
Axes of the slice: x: 2, y: 2, z: 4, core: 2. Of those that a mesh axis runs over, the one named last changes fastest.
Arguments:
- inputs: bfloat16 [32, 448, 1024], P(('dp', 'fsdp')), may hold values from -10 to 10
- encoder: bfloat16 [32, 1500, 1024], P(('dp', 'fsdp')), may hold values from -7 to 7
- cotangent: bfloat16 [32, 448, 1024], P(('dp', 'fsdp')), may hold values from -6 to 6
- attention_master: float32 [8, 1024, 1024], P(None, ('dp', 'fsdp')), may hold values from -2 to 2
- expand_master: float32 [1024, 4096], P(('dp', 'fsdp')), may hold values from -0.1875 to 0.1875
- contract_master: float32 [4096, 1024], P(('dp', 'fsdp')), may hold values from -0.09375 to 0.09375
- vectors_master: float32 [17, 1024], P(None, ('dp', 'fsdp')), may hold values from -1.5 to 1.5
- attention_first: bfloat16 [8, 1024, 1024], P(None, ('dp', 'fsdp')), may hold values from -20 to 20
- expand_first: bfloat16 [1024, 4096], P(('dp', 'fsdp')), may hold values from -20 to 20
- contract_first: bfloat16 [4096, 1024], P(('dp', 'fsdp')), may hold values from -20 to 20
- vectors_first: bfloat16 [17, 1024], P(None, ('dp', 'fsdp')), may hold values from -20 to 20
- attention_second: float32 [8, 1024, 1024], P(None, ('dp', 'fsdp')), may hold values from 1.4336 to 143.36
- expand_second: float32 [1024, 4096], P(('dp', 'fsdp')), may hold values from 1.4336 to 143.36
- contract_second: float32 [4096, 1024], P(('dp', 'fsdp')), may hold values from 1.4336 to 143.36
- vectors_second: float32 [17, 1024], P(None, ('dp', 'fsdp')), may hold values from 1.4336 to 143.36
Outputs:
- output: bfloat16 [32, 448, 1024], P(('dp', 'fsdp'))
- grad_input: float32 [32, 448, 1024], P(('dp', 'fsdp'))
- grad_encoder: float32 [32, 1500, 1024], P(('dp', 'fsdp'))
- grad_attention: float32 [8, 1024, 1024], P(None, ('dp', 'fsdp'))
- grad_expand: float32 [1024, 4096], P(('dp', 'fsdp'))
- grad_contract: float32 [4096, 1024], P(('dp', 'fsdp'))
- grad_vectors: float32 [17, 1024], P(None, ('dp', 'fsdp'))
- first_attention: float32 [8, 1024, 1024], P(None, ('dp', 'fsdp'))
- first_expand: float32 [1024, 4096], P(('dp', 'fsdp'))
- first_contract: float32 [4096, 1024], P(('dp', 'fsdp'))
- first_vectors: float32 [17, 1024], P(None, ('dp', 'fsdp'))
- second_attention: float32 [8, 1024, 1024], P(None, ('dp', 'fsdp'))
- second_expand: float32 [1024, 4096], P(('dp', 'fsdp'))
- second_contract: float32 [4096, 1024], P(('dp', 'fsdp'))
- second_vectors: float32 [17, 1024], P(None, ('dp', 'fsdp'))
- master_attention: float32 [8, 1024, 1024], P(None, ('dp', 'fsdp'))
- master_expand: float32 [1024, 4096], P(('dp', 'fsdp'))
- master_contract: float32 [4096, 1024], P(('dp', 'fsdp'))
- master_vectors: float32 [17, 1024], P(None, ('dp', 'fsdp'))
All inputs are finite; a program needn't handle non-finite values.
Results may differ from a plain program's by a relative error of at most 0.02.
The roundings to bfloat16 on the way count: a program that leaves them out, or rounds other values in their place, can miss the bound.
Values may be sent and summed in bfloat16 or wider, within the bound.
No kernel may reach another device: no remote copies, remote signals or barrier semaphores. Data moves between devices by JAX's collectives and lax.ppermute only.
A program may use at most 320 MiB of HBM per device.

v0:
```python
import jax
import jax.numpy as jnp
from jax import lax
from jax.sharding import PartitionSpec as P

HD = 64
ADAM_STEP = 4


eps_norm = 1e-05
clip_limit = 1.0
learn_rate = 0.05
beta_first = 0.9
beta_second = 0.999
eps_adam = 1e-08
weight_decay = 0.1
head_block = 4


def matmul(left, right):
    return jnp.dot(left, right, preferred_element_type=jnp.float32)


def matmul_tn(left, right):
    return lax.dot_general(
        left, right, (((0,), (0,)), ((), ())), preferred_element_type=jnp.float32
    )


def matmul_nt(left, right):
    return lax.dot_general(
        left, right, (((1,), (1,)), ((), ())), preferred_element_type=jnp.float32
    )


def gelu_exact(values):
    return jax.nn.gelu(values, approximate=False)


def norm_forward(values, gain, shift):
    centered = values - jnp.mean(values, axis=-1, keepdims=True)
    inv_std = lax.rsqrt(jnp.mean(centered * centered, axis=-1, keepdims=True) + eps_norm)
    normed = centered * inv_std
    return (normed * gain + shift, normed, inv_std)


def norm_backward(grad_out, normed, inv_std, gain):
    scaled = grad_out * gain
    return inv_std * (
        scaled
        - jnp.mean(scaled, axis=-1, keepdims=True)
        - normed * jnp.mean(scaled * normed, axis=-1, keepdims=True)
    )


def split_heads(tensor, sequences):
    row_count = tensor.shape[0] // sequences
    group_count = tensor.shape[1] // (head_block * HD)
    return tensor.reshape(sequences, row_count, group_count, head_block, HD).transpose(
        2, 3, 0, 1, 4
    )


def join_heads(tensor):
    group_count, block_heads, seq_count, row_count, head_size = tensor.shape
    return tensor.transpose(2, 3, 0, 1, 4).reshape(
        seq_count * row_count, group_count * block_heads * head_size
    )


def causal_mask(query_rows, key_rows):
    return jnp.arange(key_rows)[None, :] <= jnp.arange(query_rows)[:, None]


def attention_forward(query_in, key_in, value_in, sequences, causal):
    score_scale = HD ** (-0.5)
    blocks = (
        split_heads(query_in, sequences),
        split_heads(key_in, sequences),
        split_heads(value_in, sequences),
    )

    def one_block(block_in):
        query_b, key_b, value_b = block_in
        scores = (
            jnp.einsum("gsqd,gskd->gsqk", query_b, key_b, preferred_element_type=jnp.float32)
            * score_scale
        )
        if causal:
            scores = jnp.where(causal_mask(scores.shape[2], scores.shape[3]), scores, -1e30)
        row_max = jnp.max(scores, axis=-1, keepdims=True)
        exp_scores = jnp.exp(scores - row_max)
        row_sum = jnp.sum(exp_scores, axis=-1, keepdims=True)
        attn_probs = (exp_scores / row_sum).astype(jnp.bfloat16)
        mixed_out = jnp.einsum(
            "gsqk,gskd->gsqd", attn_probs, value_b, preferred_element_type=jnp.float32
        )
        return (mixed_out, (row_max + jnp.log(row_sum))[..., 0], jnp.max(row_max, axis=(1, 2, 3)))

    mixed_out, log_sums, head_max = lax.map(one_block, blocks)
    return (join_heads(mixed_out).astype(jnp.bfloat16), log_sums, head_max.reshape(-1))


def attention_backward(query_in, key_in, value_in, log_sums, grad_mixed, sequences, causal):
    score_scale = HD ** (-0.5)
    blocks = (
        split_heads(query_in, sequences),
        split_heads(key_in, sequences),
        split_heads(value_in, sequences),
        log_sums,
        split_heads(grad_mixed, sequences),
    )

    def one_block(block_in):
        query_b, key_b, value_b, lse_b, grad_b = block_in
        scores = (
            jnp.einsum("gsqd,gskd->gsqk", query_b, key_b, preferred_element_type=jnp.float32)
            * score_scale
        )
        if causal:
            scores = jnp.where(causal_mask(scores.shape[2], scores.shape[3]), scores, -1e30)
        attn_probs = jnp.exp(scores - lse_b[..., None])
        grad_probs = jnp.einsum(
            "gsqd,gskd->gsqk", grad_b, value_b, preferred_element_type=jnp.float32
        )
        row_dot = jnp.sum(attn_probs * grad_probs, axis=-1, keepdims=True)
        grad_scores = (attn_probs * (grad_probs - row_dot)).astype(jnp.bfloat16)
        grad_query = (
            jnp.einsum("gsqk,gskd->gsqd", grad_scores, key_b, preferred_element_type=jnp.float32)
            * score_scale
        )
        grad_key = (
            jnp.einsum("gsqk,gsqd->gskd", grad_scores, query_b, preferred_element_type=jnp.float32)
            * score_scale
        )
        grad_value = jnp.einsum(
            "gsqk,gsqd->gskd",
            attn_probs.astype(jnp.bfloat16),
            grad_b,
            preferred_element_type=jnp.float32,
        )
        return (
            grad_query.astype(jnp.bfloat16),
            grad_key.astype(jnp.bfloat16),
            grad_value.astype(jnp.bfloat16),
        )

    grad_query, grad_key, grad_value = lax.map(one_block, blocks)
    return (join_heads(grad_query), join_heads(grad_key), join_heads(grad_value))


def column_sums(values):
    return jnp.sum(values.astype(jnp.float32), axis=0)


def adam_update(master, gradient, first, second, step_value, clip_scale):
    first_new = beta_first * first.astype(jnp.float32) + (1.0 - beta_first) * gradient
    second_new = beta_second * second + (1.0 - beta_second) * gradient * gradient
    direction = (
        first_new
        / (1.0 - beta_first**step_value)
        / (jnp.sqrt(second_new / (1.0 - beta_second**step_value)) + eps_adam)
    )
    master_new = (master - learn_rate * (direction + weight_decay * master)) * clip_scale
    return (first_new, second_new, master_new)


def local(
    inputs,
    encoder,
    cotangent,
    attention_master,
    expand_master,
    contract_master,
    vectors_master,
    attention_first,
    expand_first,
    contract_first,
    vectors_first,
    attention_second,
    expand_second,
    contract_second,
    vectors_second,
):
    owned_weights = (
        attention_master.astype(jnp.bfloat16),
        expand_master.astype(jnp.bfloat16),
        contract_master.astype(jnp.bfloat16),
        vectors_master.astype(jnp.bfloat16),
    )
    w_attention, w_expand, w_contract, w_vectors = (
        lax.all_gather(owned_weights[0], ("dp", "fsdp"), axis=1, tiled=True),
        lax.all_gather(owned_weights[1], ("dp", "fsdp"), axis=0, tiled=True),
        lax.all_gather(owned_weights[2], ("dp", "fsdp"), axis=0, tiled=True),
        lax.all_gather(owned_weights[3], ("dp", "fsdp"), axis=1, tiled=True),
    )
    vectors = w_vectors.astype(jnp.float32)
    sequences, seq_length, model_width = inputs.shape
    frame_count = encoder.shape[1]
    token_rows = sequences * seq_length
    hidden_in = inputs.reshape(token_rows, model_width).astype(jnp.float32)
    enc_rows = encoder.reshape(sequences * frame_count, model_width)
    norm_one, normed_one, inv_one = norm_forward(hidden_in, vectors[0], vectors[1])
    act_one = norm_one.astype(jnp.bfloat16)
    q_self = (matmul(act_one, w_attention[0]) + vectors[6]).astype(jnp.bfloat16)
    k_self = matmul(act_one, w_attention[1]).astype(jnp.bfloat16)
    v_self = (matmul(act_one, w_attention[2]) + vectors[7]).astype(jnp.bfloat16)
    mixed_self, lse_self, max_self = attention_forward(q_self, k_self, v_self, sequences, True)
    resid_one = hidden_in + (matmul(mixed_self, w_attention[3]) + vectors[8])
    norm_two, normed_two, inv_two = norm_forward(resid_one, vectors[2], vectors[3])
    act_two = norm_two.astype(jnp.bfloat16)
    q_cross = (matmul(act_two, w_attention[4]) + vectors[9]).astype(jnp.bfloat16)
    k_cross = matmul(enc_rows, w_attention[5]).astype(jnp.bfloat16)
    v_cross = (matmul(enc_rows, w_attention[6]) + vectors[10]).astype(jnp.bfloat16)
    mixed_cross, lse_cross, max_cross = attention_forward(
        q_cross, k_cross, v_cross, sequences, False
    )
    resid_two = resid_one + (matmul(mixed_cross, w_attention[7]) + vectors[11])
    norm_three, normed_three, inv_three = norm_forward(resid_two, vectors[4], vectors[5])
    act_three = norm_three.astype(jnp.bfloat16)
    pre_gelu = matmul(act_three, w_expand) + vectors[13:].reshape(-1)
    gelu_out, gelu_back = jax.vjp(gelu_exact, pre_gelu)
    hidden_act = gelu_out.astype(jnp.bfloat16)
    result = resid_two + (matmul(hidden_act, w_contract) + vectors[12])
    maxima = lax.pmax(jnp.stack([max_self, max_cross]), ("dp", "fsdp"))
    w_attention, w_expand, w_contract, w_vectors = (
        lax.all_gather(owned_weights[0], ("dp", "fsdp"), axis=1, tiled=True),
        lax.all_gather(owned_weights[1], ("dp", "fsdp"), axis=0, tiled=True),
        lax.all_gather(owned_weights[2], ("dp", "fsdp"), axis=0, tiled=True),
        lax.all_gather(owned_weights[3], ("dp", "fsdp"), axis=1, tiled=True),
    )
    vectors = w_vectors.astype(jnp.float32)
    grad_top = cotangent.reshape(token_rows, model_width).astype(jnp.float32)
    grad_mlp_out = grad_top.astype(jnp.bfloat16)
    g_contract = matmul_tn(hidden_act, grad_mlp_out)
    b_contract = column_sums(grad_mlp_out)
    grad_pre = gelu_back(matmul_nt(grad_mlp_out, w_contract))[0].astype(jnp.bfloat16)
    g_expand = matmul_tn(act_three, grad_pre)
    b_expand = column_sums(grad_pre)
    grad_act_three = matmul_nt(grad_pre, w_expand)
    gain_three = jnp.sum(grad_act_three * normed_three, axis=0)
    shift_three = jnp.sum(grad_act_three, axis=0)
    grad_two = grad_top + norm_backward(grad_act_three, normed_three, inv_three, vectors[4])
    grad_cross_out = grad_two.astype(jnp.bfloat16)
    g_cross_o = matmul_tn(mixed_cross, grad_cross_out)
    b_cross_o = column_sums(grad_cross_out)
    grad_mixed_cross = matmul_nt(grad_cross_out, w_attention[7]).astype(jnp.bfloat16)
    dq_cross, dk_cross, dv_cross = attention_backward(
        q_cross, k_cross, v_cross, lse_cross, grad_mixed_cross, sequences, False
    )
    g_cross_q = matmul_tn(act_two, dq_cross)
    b_cross_q = column_sums(dq_cross)
    g_cross_k = matmul_tn(enc_rows, dk_cross)
    g_cross_v = matmul_tn(enc_rows, dv_cross)
    b_cross_v = column_sums(dv_cross)
    grad_encoder = (
        matmul_nt(dk_cross, w_attention[5]) + matmul_nt(dv_cross, w_attention[6])
    ).reshape(sequences, frame_count, model_width)
    grad_act_two = matmul_nt(dq_cross, w_attention[4])
    gain_two = jnp.sum(grad_act_two * normed_two, axis=0)
    shift_two = jnp.sum(grad_act_two, axis=0)
    grad_one = grad_two + norm_backward(grad_act_two, normed_two, inv_two, vectors[2])
    grad_self_out = grad_one.astype(jnp.bfloat16)
    g_self_o = matmul_tn(mixed_self, grad_self_out)
    b_self_o = column_sums(grad_self_out)
    grad_mixed_self = matmul_nt(grad_self_out, w_attention[3]).astype(jnp.bfloat16)
    dq_self, dk_self, dv_self = attention_backward(
        q_self, k_self, v_self, lse_self, grad_mixed_self, sequences, True
    )
    g_self_q = matmul_tn(act_one, dq_self)
    b_self_q = column_sums(dq_self)
    g_self_k = matmul_tn(act_one, dk_self)
    g_self_v = matmul_tn(act_one, dv_self)
    b_self_v = column_sums(dv_self)
    grad_act_one = (
        matmul_nt(dq_self, w_attention[0])
        + matmul_nt(dk_self, w_attention[1])
        + matmul_nt(dv_self, w_attention[2])
    )
    gain_one = jnp.sum(grad_act_one * normed_one, axis=0)
    shift_one = jnp.sum(grad_act_one, axis=0)
    grad_input = grad_one + norm_backward(grad_act_one, normed_one, inv_one, vectors[0])
    g_attention = jnp.stack(
        [g_self_q, g_self_k, g_self_v, g_self_o, g_cross_q, g_cross_k, g_cross_v, g_cross_o]
    )
    g_vectors = jnp.concatenate(
        [
            jnp.stack(
                [
                    gain_one,
                    shift_one,
                    gain_two,
                    shift_two,
                    gain_three,
                    shift_three,
                    b_self_q,
                    b_self_v,
                    b_self_o,
                    b_cross_q,
                    b_cross_v,
                    b_cross_o,
                    b_contract,
                ]
            ),
            b_expand.reshape(-1, model_width),
        ],
        axis=0,
    )
    grad_shards = (
        lax.psum_scatter(g_attention, ("dp", "fsdp"), scatter_dimension=1, tiled=True),
        lax.psum_scatter(g_expand, ("dp", "fsdp"), scatter_dimension=0, tiled=True),
        lax.psum_scatter(g_contract, ("dp", "fsdp"), scatter_dimension=0, tiled=True),
        lax.psum_scatter(g_vectors, ("dp", "fsdp"), scatter_dimension=1, tiled=True),
    )
    clip_cols = jnp.repeat(jnp.sqrt(clip_limit / jnp.maximum(maxima, clip_limit)), HD, axis=1)
    unit_row = jnp.ones_like(clip_cols[0])
    clip_attention = jnp.stack(
        [
            clip_cols[0],
            clip_cols[0],
            unit_row,
            unit_row,
            clip_cols[1],
            clip_cols[1],
            unit_row,
            unit_row,
        ]
    )[:, None, :]
    shard_cols = vectors_master.shape[1]
    local_cols = lax.dynamic_slice_in_dim(
        clip_cols, lax.axis_index(("dp", "fsdp")) * shard_cols, shard_cols, 1
    )
    clip_vectors = jnp.ones_like(vectors_master).at[6].set(local_cols[0]).at[9].set(local_cols[1])
    step_value = float(ADAM_STEP)
    new_attention = adam_update(
        attention_master,
        grad_shards[0],
        attention_first,
        attention_second,
        step_value,
        clip_attention,
    )
    new_expand = adam_update(
        expand_master, grad_shards[1], expand_first, expand_second, step_value, 1.0
    )
    new_contract = adam_update(
        contract_master, grad_shards[2], contract_first, contract_second, step_value, 1.0
    )
    new_vectors = adam_update(
        vectors_master, grad_shards[3], vectors_first, vectors_second, step_value, clip_vectors
    )
    return (
        result.reshape(sequences, seq_length, model_width).astype(jnp.bfloat16),
        grad_input.reshape(sequences, seq_length, model_width),
        grad_encoder,
        grad_shards[0],
        grad_shards[1],
        grad_shards[2],
        grad_shards[3],
        new_attention[0],
        new_expand[0],
        new_contract[0],
        new_vectors[0],
        new_attention[1],
        new_expand[1],
        new_contract[1],
        new_vectors[1],
        new_attention[2],
        new_expand[2],
        new_contract[2],
        new_vectors[2],
    )


def solution(mesh):
    in_specs = (
        P(("dp", "fsdp"), None, None),
        P(("dp", "fsdp"), None, None),
        P(("dp", "fsdp"), None, None),
        P(None, ("dp", "fsdp"), None),
        P(("dp", "fsdp"), None),
        P(("dp", "fsdp"), None),
        P(None, ("dp", "fsdp")),
        P(None, ("dp", "fsdp"), None),
        P(("dp", "fsdp"), None),
        P(("dp", "fsdp"), None),
        P(None, ("dp", "fsdp")),
        P(None, ("dp", "fsdp"), None),
        P(("dp", "fsdp"), None),
        P(("dp", "fsdp"), None),
        P(None, ("dp", "fsdp")),
    )
    out_specs = (
        P(("dp", "fsdp"), None, None),
        P(("dp", "fsdp"), None, None),
        P(("dp", "fsdp"), None, None),
        P(None, ("dp", "fsdp"), None),
        P(("dp", "fsdp"), None),
        P(("dp", "fsdp"), None),
        P(None, ("dp", "fsdp")),
        P(None, ("dp", "fsdp"), None),
        P(("dp", "fsdp"), None),
        P(("dp", "fsdp"), None),
        P(None, ("dp", "fsdp")),
        P(None, ("dp", "fsdp"), None),
        P(("dp", "fsdp"), None),
        P(("dp", "fsdp"), None),
        P(None, ("dp", "fsdp")),
        P(None, ("dp", "fsdp"), None),
        P(("dp", "fsdp"), None),
        P(("dp", "fsdp"), None),
        P(None, ("dp", "fsdp")),
    )
    return jax.shard_map(local, mesh=mesh, in_specs=in_specs, out_specs=out_specs, check_vma=False)
```

profile of v0, /device:TPU:0, one launch (start us, length us, event | category | flops | bytes accessed | tf_op | source)
XLA Modules:
  0.0 2159.6 jit_solution(5261098819585136216)
XLA Ops:
  11.5 73.0 %all-gather = bf16[32,32,17]{1,2,0:T(8,128)(2,1)S(1)} all-gather(bf16[1,32,17]{1,2,0:T(8,128)(2,1)S(1)} %convert_bitcast_fusion.1), channel_id=1, replica_groups=mesh['dp'=8,'fsdp'=4] {'dp','fsdp'}, dimensions={0}, use_global_device_ids=true | all-gather | bytes 35904 | tf_op jit(solution)/shard_map/all_gather | solution.py:195
  88.9 41.2 %all-gather.5.cloned.1.call-done = bf16[8,1024,1024]{2,1,0:T(8,128)(2,1)} async-done(((bf16[8,32,1024]{2,1,0:T(8,128)(2,1)}), bf16[8,1024,1024]{2,1,0:T(8,128)(2,1)}) %all-gather.5.cloned.1.call-update) | async-done | bytes 16777232 | tf_op jit(solution)/shard_map/all_gather | solution.py:192
  150.1 26.4 %while.58 = (s32[]{:T(128)}, bf16[4,4,1,448,64]{3,4,1,2,0:T(8,128)(2,1)}, f32[4,4,1,448]{3,1,2,0:T(4,128)S(1)}, f32[4,4]{1,0:T(4,128)S(1)}, bf16[4,4,1,448,64]{3...) while((s32[]{:T(128)}, ...), condition=%wide.region_6.7_spmd, body=%wide.region_2.6_spmd.sunk | while | flops 216156416 | bytes 19639508 | solution.py:100
  187.1 6.3 add_convert_fusion.1
  198.1 6.3 convolution_convert_fusion
  210.2 44.8 %while.59 = (s32[]{:T(128)}, bf16[4,4,1,448,64]{3,4,1,2,0:T(8,128)(2,1)}, f32[4,4,1,448]{3,1,2,0:T(4,128)S(1)}, f32[4,4]{1,0:T(4,128)S(1)}, bf16[4,4,1,448,64]{3...) while((s32[]{:T(128)}, ...), condition=%wide.region_13.14_spmd, body=%wide.region_9.13_spmd.sunk | while | flops 715006208 | bytes 42278100 | solution.py:100
  260.4 24.0 %multiply_convert_fusion.2 = (bf16[448,4096]{1,0:T(8,128)(2,1)S(1)}, f32[448,4096]{1,0:T(8,128)}, f32[448,4096]{1,0:T(8,128)}) fusion(f32[4096]{0:T(1024)S(1)} %bitcast.510, bf16[1024,4096]{1,0:T(8,128)(2,1)} %all-gather.7.cloned.1.call-done, f32[448,1024]{1,0:T(8,128)} %copy-done.23, f32[1024]{0:T(1024)S(1)} %bitcast.535, f32[1024]{0:T(1024)S(1)} %bitcast.520, ...), kind=kOutput, calls=%fused_computation.124 | convolution fusion | flops 3881500672 | bytes 28601856 | tf_op jit(solution)/shard_map/dot_general | solution.py:21
  286.2 8.2 fusion.163
  294.5 363.3 %reduce-scatter.11.cloned.1.call-done = f32[128,1024]{1,0:T(8,128)} async-done(((f32[4096,1024]{1,0:T(8,128)}), f32[128,1024]{1,0:T(8,128)}) %reduce-scatter.11.cloned.1.call-update) | async-done | bytes 524304 | tf_op jit(solution)/shard_map/reduce_scatter | solution.py:312
  660.9 75.6 %all-gather.9.cloned.1.call-done = bf16[4096,1024]{1,0:T(8,128)(2,1)} async-done(((bf16[128,1024]{1,0:T(8,128)(2,1)}), bf16[4096,1024]{1,0:T(8,128)(2,1)}) %all-gather.9.cloned.1.call-update) | async-done | bytes 8388624 | tf_op jit(solution)/shard_map/all_gather | solution.py:194
  736.5 13.9 convert_reduce_fusion
  751.0 10.1 multiply_reduce_fusion.4
  770.9 91.7 %while.60 = (s32[]{:T(128)}, bf16[4,4,1,448,64]{3,4,1,2,0:T(8,128)(2,1)}, bf16[4,4,1,1500,64]{3,4,1,2,0:T(8,128)(2,1)}, bf16[4,4,1,1500,64]{3,4,1,2,0:T(8,128)(2...) while((s32[]{:T(128)}, ...), condition=%wide.region_20.21_spmd, body=%wide.region_18.20_spmd.sunk | while | flops 1753955584 | bytes 111759520 | solution.py:148
  785.7 5.3 fusion.266
  808.6 5.3 fusion.266
  882.3 40.5 %while.61 = (s32[]{:T(128)}, bf16[4,4,1,448,64]{3,4,1,2,0:T(8,128)(2,1)}, bf16[4,4,1,448,64]{3,4,1,2,0:T(8,128)(2,1)}, bf16[4,4,1,448,64]{3,4,1,2,0:T(8,128)(2,1...) while((s32[]{:T(128)}, ...), condition=%wide.region_25.26_spmd, body=%wide.region_23.25_spmd.sunk | while | flops 521799936 | bytes 35435688 | solution.py:148
  938.9 13.0 fusion.176
  985.6 39.8 %pmax.7 = f32[2,16]{1,0:T(2,128)S(1)} all-reduce(f32[2,16]{1,0:T(2,128)S(1)} %pad_maximum_fusion), channel_id=1, replica_groups=mesh['dp'=8,'fsdp'=4] {'dp','fsdp'}, use_global_device_ids=true, to_apply=%region_46.47 | all-reduce | flops 32 | bytes 256 | tf_op jit(solution)/shard_map/pmax | solution.py:225
  1026.1 6.3 fusion.143
  1032.4 5.4 add_bitcast_fusion
  1037.9 12.3 copy.138
  1058.4 13.8 reduce-scatter.13.cloned.1.call-done
  1073.7 361.6 %reduce-scatter.9.cloned.1.call-done = f32[32,4096]{1,0:T(8,128)} async-done(((f32[1024,4096]{1,0:T(8,128)}), f32[32,4096]{1,0:T(8,128)}) %reduce-scatter.9.cloned.1.call-update) | async-done | bytes 524304 | tf_op jit(solution)/shard_map/reduce_scatter | solution.py:311
  1438.0 710.1 %reduce-scatter.7.cloned.1.call-done = f32[8,32,1024]{2,1,0:T(8,128)} async-done(((f32[8,1024,1024]{2,1,0:T(8,128)}), f32[8,32,1024]{2,1,0:T(8,128)}) %reduce-scatter.7.cloned.1.call-update) | async-done | bytes 1048592 | tf_op jit(solution)/shard_map/reduce_scatter | solution.py:310
  (436 shorter events, 348.3 us)
Async XLA Ops:
  7.2 179.9 %copy-start = (bf16[1,1500,1024]{2,1,0:T(8,128)(2,1)S(1)}, bf16[1,1500,1024]{2,1,0:T(8,128)(2,1)}, u32[]{:S(2)}) copy-start(bf16[1,1500,1024]{2,1,0:T(8,128)(2,1)} %param.28) | copy-start | bytes 9216004
  7.2 122.9 %all-gather.5.cloned.1.call-start = ((), (), s32[]{:S(2)}) async-start(), calls=%async_computation.4 | async-start | bytes 17301504 | tf_op jit(solution)/shard_map/all_gather | solution.py:192
  9.5 250.8 %all-gather.7.cloned.1.call-start = ((), (), s32[]{:S(2)}) async-start(), calls=%async_computation.5 | async-start | bytes 8650752 | tf_op jit(solution)/shard_map/all_gather | solution.py:193
  11.4 646.4 %reduce-scatter.11.cloned.1.call-start = ((), (), s32[]{:S(2)}) async-start(), calls=%async_computation.9 | async-start | bytes 17301504 | tf_op jit(solution)/shard_map/reduce_scatter | solution.py:312
  85.3 57.4 %copy-start.52 = (f32[1,1024]{1,0:T(1,128)}, f32[1,1024]{1,0:T(1,128)S(1)}, u32[]{:S(2)}) copy-start(f32[1,1024]{1,0:T(1,128)S(1)} %get-tuple-element.523) | copy-start | bytes 12292
  85.3 57.4 %copy-start.73 = (f32[1,1024]{1,0:T(1,128)}, f32[1,1024]{1,0:T(1,128)S(1)}, u32[]{:S(2)}) copy-start(f32[1,1024]{1,0:T(1,128)S(1)} %get-tuple-element.522) | copy-start | bytes 12292
  85.3 95.0 %copy-start.49 = (f32[1,1024]{1,0:T(1,128)}, f32[1,1024]{1,0:T(1,128)S(1)}, u32[]{:S(2)}) copy-start(f32[1,1024]{1,0:T(1,128)S(1)} %get-tuple-element.518) | copy-start | bytes 12292
  85.3 95.0 %copy-start.71 = (f32[1,1024]{1,0:T(1,128)}, f32[1,1024]{1,0:T(1,128)S(1)}, u32[]{:S(2)}) copy-start(f32[1,1024]{1,0:T(1,128)S(1)} %get-tuple-element.517) | copy-start | bytes 12292
  86.7 56.0 %copy-start.43 = (f32[448]{0:T(512)}, f32[448]{0:T(512)S(1)}, u32[]{:S(2)}) copy-start(f32[448]{0:T(512)S(1)} %broadcast_multiply_fusion.8) | copy-start | bytes 5380
  88.3 54.4 %copy-start.59 = (f32[448]{0:T(512)}, f32[448]{0:T(512)S(1)}, u32[]{:S(2)}) copy-start(f32[448]{0:T(512)S(1)} %add_rsqrt_fusion.2) | copy-start | bytes 5380
  210.2 44.8 %copy-start.77 = (f32[1,1024]{1,0:T(1,128)S(1)}, f32[1,1024]{1,0:T(1,128)}, u32[]{:S(2)}) copy-start(f32[1,1024]{1,0:T(1,128)} %get-tuple-element.514) | copy-start | bytes 12292
  258.8 502.4 %copy-start.47 = (f32[448]{0:T(512)}, f32[448]{0:T(512)S(1)}, u32[]{:S(2)}) copy-start(f32[448]{0:T(512)S(1)} %broadcast_multiply_fusion.6) | copy-start | bytes 5380
  260.3 500.8 %copy-start.63 = (f32[448]{0:T(512)}, f32[448]{0:T(512)S(1)}, u32[]{:S(2)}) copy-start(f32[448]{0:T(512)S(1)} %add_rsqrt_fusion) | copy-start | bytes 5380
  260.4 25.8 %copy-start.34 = (bf16[1,448,1024]{2,1,0:T(8,128)(2,1)S(1)}, bf16[1,448,1024]{2,1,0:T(8,128)(2,1)}, u32[]{:S(2)}) copy-start(bf16[1,448,1024]{2,1,0:T(8,128)(2,1)} %param.29) | copy-start | bytes 2752516
  294.4 363.4 %copy-start.36 = (bf16[128,1024]{1,0:T(8,128)(2,1)S(1)}, bf16[128,1024]{1,0:T(8,128)(2,1)}, u32[]{:S(2)}) copy-start(bf16[128,1024]{1,0:T(8,128)(2,1)} %param.36) | copy-start | bytes 786436
  294.4 442.1 %all-gather.9.cloned.1.call-start = ((), (), s32[]{:S(2)}) async-start(), calls=%async_computation.6 | async-start | bytes 8650752 | tf_op jit(solution)/shard_map/all_gather | solution.py:194
  660.9 411.3 %reduce-scatter.13.cloned.1.call-start = ((), (), s32[]{:S(2)}) async-start(), calls=%async_computation.10 | async-start | bytes 540672
  938.9 496.4 %reduce-scatter.9.cloned.1.call-start = ((), (), s32[]{:S(2)}) async-start(), calls=%async_computation.8 | async-start | bytes 17301504 | tf_op jit(solution)/shard_map/reduce_scatter | solution.py:311
  952.0 1196.1 %reduce-scatter.7.cloned.1.call-start = ((), (), s32[]{:S(2)}) async-start(), calls=%async_computation.7 | async-start | bytes 34603008 | tf_op jit(solution)/shard_map/reduce_scatter | solution.py:310
  1026.1 25.9 %slice-start = ((s8[8388608]{0:T(1024)(128)(4,1)}), s8[4194304]{0:T(1024)(128)(4,1)S(1)}, s32[]{:S(2)}) async-start(s8[8388608]{0:T(1024)(128)(4,1)} %bitcast.549), calls=%async_computation.11 | async-start | bytes 8388608
  1032.4 19.6 slice-start.1
  1053.4 19.6 copy-start.69
  1053.4 381.8 %copy-start.37 = (bf16[32,4096]{1,0:T(8,128)(2,1)S(1)}, bf16[32,4096]{1,0:T(8,128)(2,1)}, u32[]{:S(2)}) copy-start(bf16[32,4096]{1,0:T(8,128)(2,1)} %param.35) | copy-start | bytes 786436
  1073.0 1079.5 %copy-start.40 = (f32[17,32]{1,0:T(8,128)}, f32[17,32]{1,0:T(8,128)S(1)}, u32[]{:S(2)}) copy-start(f32[17,32]{1,0:T(8,128)S(1)} %copy.146) | copy-start | bytes 6532
  (92 other events, 379.8 us)
Sparse Core Ops, SparseCore 0:
  11.7 118.3 all-gather.4
  133.6 75.6 all-gather.6
  294.5 363.1 reduce-scatter.10
  661.1 75.3 all-gather.8
  939.0 133.1 reduce-scatter.12
  1075.0 360.1 reduce-scatter.8
  1438.2 709.8 reduce-scatter.6
where the time goes:
time: 2160 us
  waiting for transfers between devices  1570 us (73%)
  matrix products  326 us (15%)
  blocking collectives  113 us (5%)
  other arithmetic  69.7 us (3%)
  local copies, waits for them, and re-layouts  67.8 us (3%)
    reduce_scatter x1, waiting for transfers between devices, local(): lax.psum_scatter(g_attention, ('dp', 'fsdp'), scatter_dimension=1, tiled=...  710 us
    reduce_scatter x1, waiting for transfers between devices, local(): lax.psum_scatter(g_contract, ('dp', 'fsdp'), scatter_dimension=0, tiled=T...  363 us
    reduce_scatter x1, waiting for transfers between devices, local(): lax.psum_scatter(g_expand, ('dp', 'fsdp'), scatter_dimension=0, tiled=True)  362 us
    all_gather x1, waiting for transfers between devices, local(): lax.all_gather(owned_weights[2], ('dp', 'fsdp'), axis=0, tiled=True)  75.6 us
    all_gather x1, blocking collectives, local(): lax.all_gather(owned_weights[3], ('dp', 'fsdp'), axis=1, tiled=True)  73 us
    dot_general x10, matrix products, matmul(): return jnp.dot(left, right, preferred_element_type=jnp.float32)  64.3 us
    dot_general x10, matrix products, matmul_nt(): lax.dot_general(left, right, (((1,), (1,)), ((), ())), preferred_element_...  59 us
    dot_general x10, matrix products, matmul_tn(): lax.dot_general(left, right, (((0,), (0,)), ((), ())), preferred_element_...  53.3 us
  transfers between devices with their start and end apart: 7, of which 6 were waited for; matrix products, arithmetic and copies ran while one was open for 10% of the time, Pallas kernels for 0%

commit v1 on v0

v1 whole, which is shorter than its diff:
```python
import functools
import math

import jax
import jax.numpy as jnp
from jax import lax
from jax.experimental import pallas as pl
from jax.experimental.pallas import tpu as pltpu
from jax.sharding import Mesh
from jax.sharding import PartitionSpec as P

HD = 64
ADAM_STEP = 4

eps_norm = 1e-05
clip_limit = 1.0
learn_rate = 0.05
beta_first = 0.9
beta_second = 0.999
eps_adam = 1e-08
weight_decay = 0.1

BF = jnp.bfloat16
F32 = jnp.float32
ALL = ("y", "x", "c", "z")
TILE = 256
KEY_CHUNK = 256
VEC_ROWS = 17
MIB = 1024 * 1024


def dot(left, right):
    return jnp.dot(left, right, preferred_element_type=F32)


def dot_tn(left, right):
    return lax.dot_general(left, right, (((0,), (0,)), ((), ())), preferred_element_type=F32)


def dot_nt(left, right):
    return lax.dot_general(left, right, (((1,), (1,)), ((), ())), preferred_element_type=F32)


def params(limit=48):
    return pltpu.CompilerParams(vmem_limit_bytes=limit * MIB)


def vmem():
    return pl.BlockSpec(memory_space=pltpu.VMEM)


def hbm():
    return pl.BlockSpec(memory_space=pl.ANY)


def smem():
    return pl.BlockSpec(memory_space=pltpu.SMEM)


def shape(dims, dtype):
    return jax.ShapeDtypeStruct(tuple(dims), dtype)


def cost(flops, nbytes):
    return pl.CostEstimate(flops=int(flops), bytes_accessed=int(nbytes), transcendentals=0)


def weight_copy(pack, row, buf, sem):
    return pltpu.make_async_copy(pack.at[:, pl.ds(row, buf.shape[1]), :], buf, sem)


def times(act_ref, buf, put):
    depth = buf.shape[0] * buf.shape[1]

    @pl.loop(0, buf.shape[2] // TILE)
    def _(n):
        start = pl.multiple_of(n * TILE, TILE)
        put(start, dot(act_ref[...], buf[:, :, pl.ds(start, TILE)].reshape(depth, TILE)))


def times_t(act_ref, buf, put):
    per = TILE // buf.shape[1]

    @pl.loop(0, buf.shape[0] // per)
    def _(n):
        start = pl.multiple_of(n * TILE, TILE)
        rows = buf[pl.ds(n * per, per)].reshape(TILE, buf.shape[2])
        put(start, dot_nt(act_ref[...], rows))


def grad_weight(act_ref, grad_ref, out):
    @pl.loop(0, 4)
    def _(n):
        start = pl.multiple_of(n * TILE, TILE)
        tile = dot_tn(act_ref[:, pl.ds(start, TILE)], grad_ref[...])
        out[pl.ds(2 * n, 2)] = tile.astype(BF).reshape((2,) + out.shape[1:])


def block_copies(sel, grad, keep, send, row, sems):
    out = []
    for j in range(8):
        across, plane = j // 4, j % 4
        block = jnp.bitwise_xor(sel, plane * 2 + across)
        target = (send if across else keep).at[plane, :, pl.ds(row, grad.shape[2]), :]
        out.append(pltpu.make_async_copy(grad.at[block], target, sems.at[j]))
    return out


def start_all(copies):
    for one in copies:
        one.start()


def wait_all(copies):
    for one in copies:
        one.wait()


def row_chunks(count, size=64):
    return [slice(a, min(a + size, count)) for a in range(0, count, size)]


def normalise(values):
    centered = values - jnp.mean(values, axis=-1, keepdims=True)
    inv = lax.rsqrt(jnp.mean(centered * centered, axis=-1, keepdims=True) + eps_norm)
    return centered * inv, inv


def norm_into(src, gain, shift, out_ref):
    for rows in row_chunks(src.shape[0]):
        normed, _ = normalise(src[rows, :].astype(F32))
        out_ref[rows, :] = (normed * gain + shift).astype(BF)


def norm_grad(src, grad_ref, gain, put):
    gain_sum = jnp.zeros((1, src.shape[1]), F32)
    shift_sum = jnp.zeros((1, src.shape[1]), F32)
    for rows in row_chunks(src.shape[0]):
        normed, inv = normalise(src[rows, :].astype(F32))
        grad = grad_ref[rows, :]
        gain_sum += jnp.sum(grad * normed, axis=0, keepdims=True)
        shift_sum += jnp.sum(grad, axis=0, keepdims=True)
        scaled = grad * gain
        mean_one = jnp.mean(scaled, axis=-1, keepdims=True)
        mean_two = jnp.mean(scaled * normed, axis=-1, keepdims=True)
        put(rows, inv * (scaled - mean_one - normed * mean_two))
    return gain_sum, shift_sum


def column_sum(ref):
    total = jnp.zeros((1, ref.shape[1]), F32)
    for rows in row_chunks(ref.shape[0], 128):
        total += jnp.sum(ref[rows, :].astype(F32), axis=0, keepdims=True)
    return total


def self_in_kernel(x_ref, vec_ref, pack, a_ref, q_ref, k_ref, v_ref, bufs, sems):
    copies = [weight_copy(pack, 32 * n, bufs.at[n], sems.at[n]) for n in range(3)]
    start_all(copies)
    norm_into(x_ref, vec_ref[0:1, :], vec_ref[1:2, :], a_ref)
    for n, (out, bias) in enumerate(((q_ref, 6), (k_ref, None), (v_ref, 7))):
        copies[n].wait()

        def put(start, value, out=out, bias=bias):
            if bias is not None:
                value = value + vec_ref[bias : bias + 1, pl.ds(start, TILE)]
            out[:, pl.ds(start, TILE)] = value.astype(BF)

        times(a_ref, bufs.at[n], put)


def self_in(x, vec, pack):
    rows, width = x.shape
    full = shape((rows, width), BF)
    return pl.pallas_call(
        self_in_kernel,
        out_shape=[full] * 4,
        in_specs=[vmem(), vmem(), hbm()],
        out_specs=[vmem()] * 4,
        scratch_shapes=[pltpu.VMEM((3, 32, 32, width), BF), pltpu.SemaphoreType.DMA((3,))],
        compiler_params=params(),
        cost_estimate=cost(6 * rows * width * width, 10 * MIB),
        name="self_in",
    )(x, vec, pack)


def masked_pair(value):
    lane = lax.broadcasted_iota(jnp.int32, value.shape, 1)
    zero = jnp.zeros_like(value)
    return jnp.concatenate([jnp.where(lane < HD, value, zero), jnp.where(lane < HD, zero, value)], axis=0)


def pair_back(both, rows):
    line = lax.broadcasted_iota(jnp.int32, (2 * HD, rows), 0)
    return jnp.where(line < HD, both[:, :rows], both[:, rows:]).T


def key_chunks(count):
    return [(a, min(a + KEY_CHUNK, count)) for a in range(0, count, KEY_CHUNK)]


def exclude(scores, start, rows, causal, valid):
    key = lax.broadcasted_iota(jnp.int32, scores.shape, 0) + start
    if causal:
        query = lax.broadcasted_iota(jnp.int32, scores.shape, 1)
        query = jnp.where(query >= rows, query - rows, query)
        return jnp.where(key <= query, scores, -1e30)
    if start + scores.shape[0] > valid:
        return jnp.where(key < valid, scores, -1e30)
    return scores


def attend_kernel(causal, valid, q_ref, k_ref, v_ref, o_ref, lse_ref, top_ref, held):
    rows = q_ref.shape[0]
    query = masked_pair(q_ref[...] * jnp.asarray(HD**-0.5, BF))
    top = jnp.full((1, 2 * rows), -1e30, F32)
    for a, b in key_chunks(k_ref.shape[0]):
        scores = exclude(dot_nt(k_ref[a:b, :], query), a, rows, causal, valid)
        held[a:b, :] = scores
        top = jnp.maximum(top, jnp.max(scores, axis=0, keepdims=True))
    total = jnp.zeros((1, 2 * rows), F32)
    mixed = jnp.zeros((2 * HD, 2 * rows), F32)
    for a, b in key_chunks(k_ref.shape[0]):
        probs = jnp.exp(held[a:b, :] - top)
        total += jnp.sum(probs, axis=0, keepdims=True)
        mixed += dot_tn(v_ref[a:b, :], probs.astype(BF))
    o_ref[...] = pair_back(mixed * (1.0 / total), rows).astype(BF)
    top_ref[0] = top
    lse_ref[0] = top + jnp.log(total)


def attend(query, key, value, causal, valid):
    rows, width = query.shape
    keys = key.shape[0]
    pairs = width // (2 * HD)

    def column(count):
        return pl.BlockSpec((count, 2 * HD), lambda h: (0, h))

    line = pl.BlockSpec((1, 1, 2 * rows), lambda h: (h, 0, 0))
    return pl.pallas_call(
        functools.partial(attend_kernel, causal, valid),
        grid=(pairs,),
        out_shape=[shape((rows, width), BF)] + [shape((pairs, 1, 2 * rows), F32)] * 2,
        in_specs=[column(rows), column(keys), column(keys)],
        out_specs=[column(rows), line, line],
        scratch_shapes=[pltpu.VMEM((keys, 2 * rows), F32)],
        compiler_params=params(),
        cost_estimate=cost(16 * rows * keys * width, 4 * keys * width),
        name="attend_causal" if causal else "attend",
    )(query, key, value)


def self_out_kernel(o_ref, x_ref, vec_ref, pack, x1_ref, a_ref, q_ref, bufs, sems):
    copies = [weight_copy(pack, 32 * (3 + n), bufs.at[n], sems.at[n]) for n in range(2)]
    start_all(copies)
    copies[0].wait()

    def put_residual(start, value):
        cols = pl.ds(start, TILE)
        x1_ref[:, cols] = x_ref[:, cols].astype(F32) + (value + vec_ref[8:9, cols])

    times(o_ref, bufs.at[0], put_residual)
    norm_into(x1_ref, vec_ref[2:3, :], vec_ref[3:4, :], a_ref)
    copies[1].wait()

    def put_query(start, value):
        cols = pl.ds(start, TILE)
        q_ref[:, cols] = (value + vec_ref[9:10, cols]).astype(BF)

    times(a_ref, bufs.at[1], put_query)


def self_out(mixed, x, vec, pack):
    rows, width = x.shape
    return pl.pallas_call(
        self_out_kernel,
        out_shape=[shape((rows, width), F32), shape((rows, width), BF), shape((rows, width), BF)],
        in_specs=[vmem()] * 3 + [hbm()],
        out_specs=[vmem()] * 3,
        scratch_shapes=[pltpu.VMEM((2, 32, 32, width), BF), pltpu.SemaphoreType.DMA((2,))],
        compiler_params=params(),
        cost_estimate=cost(4 * rows * width * width, 10 * MIB),
        name="self_out",
    )(mixed, x, vec, pack)


def cross_in_kernel(e_ref, vec_ref, pack, k_ref, v_ref, bufs, sems):
    copies = [weight_copy(pack, 32 * (5 + n), bufs.at[n], sems.at[n]) for n in range(2)]
    start_all(copies)
    for n, (out, bias) in enumerate(((k_ref, None), (v_ref, 10))):
        copies[n].wait()

        def put(start, value, out=out, bias=bias):
            if bias is not None:
                value = value + vec_ref[bias : bias + 1, pl.ds(start, TILE)]
            out[:, pl.ds(start, TILE)] = value.astype(BF)

        times(e_ref, bufs.at[n], put)


def cross_in(enc, vec, pack):
    frames, width = enc.shape
    return pl.pallas_call(
        cross_in_kernel,
        out_shape=[shape((frames, width), BF)] * 2,
        in_specs=[vmem()] * 2 + [hbm()],
        out_specs=[vmem()] * 2,
        scratch_shapes=[pltpu.VMEM((2, 32, 32, width), BF), pltpu.SemaphoreType.DMA((2,))],
        compiler_params=params(),
        cost_estimate=cost(4 * frames * width * width, 14 * MIB),
        name="cross_in",
    )(enc, vec, pack)


def cross_out_kernel(o_ref, x1_ref, vec_ref, pack, x2_ref, a_ref, buf, sem):
    copy = weight_copy(pack, 32 * 7, buf, sem)
    copy.start()
    copy.wait()

    def put(start, value):
        cols = pl.ds(start, TILE)
        x2_ref[:, cols] = x1_ref[:, cols] + (value + vec_ref[11:12, cols])

    times(o_ref, buf, put)
    norm_into(x2_ref, vec_ref[4:5, :], vec_ref[5:6, :], a_ref)


def cross_out(mixed, x1, vec, pack):
    rows, width = x1.shape
    return pl.pallas_call(
        cross_out_kernel,
        out_shape=[shape((rows, width), F32), shape((rows, width), BF)],
        in_specs=[vmem()] * 3 + [hbm()],
        out_specs=[vmem()] * 2,
        scratch_shapes=[pltpu.VMEM((32, 32, width), BF), pltpu.SemaphoreType.DMA],
        compiler_params=params(),
        cost_estimate=cost(2 * rows * width * width, 8 * MIB),
        name="cross_out",
    )(mixed, x1, vec, pack)


def feed_kernel(
    sel_ref, a_ref, x2_ref, e_ref, vec_ref, bias_ref, w1_ref, w2_ref,
    out_ref, da_ref, gb1_ref, gb2_ref, keep1, send1, keep2, send2,
    total, g1, g2, sems1, sems2,
):
    step = pl.program_id(0)
    steps = pl.num_programs(0)
    sel = sel_ref[0]
    slot = lax.rem(step, 2)
    wide = w1_ref.shape[2]
    depth = a_ref.shape[1]

    def copies_one(at_step, at_slot):
        cols = pl.ds(pl.multiple_of(at_step * wide, wide), wide)
        return block_copies(sel, g1.at[at_slot], keep1.at[:, :, :, cols], send1.at[:, :, :, cols], 0, sems1.at[at_slot])

    def copy_two(at_step, at_slot, ref):
        place = jnp.bitwise_xor(sel, at_step)
        return pltpu.make_async_copy(g2.at[at_slot], ref.at[lax.div(place, 2)], sems2.at[at_slot])

    @pl.when(step >= 2)
    def _():
        wait_all(copies_one(step - 2, slot))
        copy_two(step - 2, slot, keep2).wait()

    w1 = w1_ref[...].reshape(depth, wide)
    w2 = w2_ref[...].reshape(wide, depth)
    pre = dot(a_ref[...], w1) + bias_ref[0]
    cdf = 0.5 * (1.0 + lax.erf(pre * math.sqrt(0.5)))
    act = (pre * cdf).astype(BF)
    slope = cdf + pre * (jnp.exp(-0.5 * (pre * pre)) * (1.0 / math.sqrt(2.0 * math.pi)))
    grad_pre = (dot_nt(e_ref[...], w2) * slope).astype(BF)
    gb1_ref[0] = jnp.sum(grad_pre.astype(F32), axis=0, keepdims=True)
    g2[slot] = dot_tn(act, e_ref[...]).astype(BF).reshape(g2.shape[1:])

    place = jnp.bitwise_xor(sel, step)

    @pl.when(lax.rem(place, 2) == 0)
    def _():
        copy_two(step, slot, keep2).start()

    @pl.when(lax.rem(place, 2) == 1)
    def _():
        copy_two(step, slot, send2).start()

    g1[slot] = dot_tn(a_ref[...], grad_pre).astype(BF).reshape(g1.shape[1:])
    start_all(copies_one(step, slot))

    @pl.when(step == 0)
    def _():
        total[...] = x2_ref[...] + vec_ref[12:13, :]
        da_ref[...] = jnp.zeros_like(da_ref)
        gb2_ref[...] = column_sum(e_ref)

    total[...] += dot(act, w2)
    da_ref[...] += dot_nt(grad_pre, w1)

    @pl.when(step == steps - 1)
    def _():
        out_ref[...] = total[...].astype(BF)
        wait_all(copies_one(step - 1, 1 - slot))
        copy_two(step - 1, 1 - slot, keep2).wait()
        wait_all(copies_one(step, slot))
        copy_two(step, slot, keep2).wait()


def feed(sel, a3, x2, cot, vec, pack):
    rows, width = a3.shape
    hidden = 4 * width
    wide = hidden // 8
    bias = vec[13:].reshape(8, 1, wide)

    def whole(dims):
        return pl.BlockSpec(dims, lambda n: (0,) * len(dims))

    return pl.pallas_call(
        feed_kernel,
        grid=(8,),
        out_shape=[
            shape((rows, width), BF),
            shape((rows, width), F32),
            shape((8, 1, wide), F32),
            shape((1, width), F32),
            shape((4, 4, 32, hidden), BF),
            shape((4, 4, 32, hidden), BF),
            shape((4, 4, 128, width), BF),
            shape((4, 4, 128, width), BF),
        ],
        in_specs=[
            smem(),
            whole((rows, width)),
            whole((rows, width)),
            whole((rows, width)),
            whole(vec.shape),
            pl.BlockSpec((1, 1, wide), lambda n: (n, 0, 0)),
            pl.BlockSpec((32, 32, wide), lambda n: (0, n // 2, n % 2)),
            pl.BlockSpec((4, 128, width), lambda n: (n, 1, 0)),
        ],
        out_specs=[
            whole((rows, width)),
            whole((rows, width)),
            pl.BlockSpec((1, 1, wide), lambda n: (n, 0, 0)),
            whole((1, width)),
            hbm(), hbm(), hbm(), hbm(),
        ],
        scratch_shapes=[
            pltpu.VMEM((rows, width), F32),
            pltpu.VMEM((2, 8, 4, 32, wide), BF),
            pltpu.VMEM((2, 4, 128, width), BF),
            pltpu.SemaphoreType.DMA((2, 8)),
            pltpu.SemaphoreType.DMA((2,)),
        ],
        compiler_params=params(),
        cost_estimate=cost(12 * rows * width * hidden, 40 * MIB),
        name="feed",
    )(sel, a3, x2, cot, vec, bias, pack, pack)


def cross_out_grad_kernel(
    sel_ref, da_ref, x2_ref, cot_ref, o_ref, vec_ref, pack,
    dx_ref, do_ref, sums_ref, keep, send, buf, e_ref, grad, sem, sems,
):
    copy = weight_copy(pack, 32 * 7, buf, sem)
    copy.start()

    def put(rows, value):
        total = cot_ref[rows, :].astype(F32) + value
        dx_ref[rows, :] = total
        e_ref[rows, :] = total.astype(BF)

    gain, shift = norm_grad(x2_ref, da_ref, vec_ref[4:5, :], put)
    sums_ref[0:1, :] = gain
    sums_ref[1:2, :] = shift
    sums_ref[2:3, :] = column_sum(e_ref)
    grad_weight(o_ref, e_ref, grad)
    out = block_copies(sel_ref[0], grad, keep, send, 0, sems)
    start_all(out)
    copy.wait()

    def put_mixed(start, value):
        do_ref[:, pl.ds(start, TILE)] = value.astype(BF)

    times_t(e_ref, buf, put_mixed)
    wait_all(out)


def cross_out_grad(sel, da3, x2, cot, mixed, vec, pack):
    rows, width = x2.shape
    return pl.pallas_call(
        cross_out_grad_kernel,
        out_shape=[
            shape((rows, width), F32), shape((rows, width), BF), shape((3, width), F32),
            shape((4, 4, 32, width), BF), shape((4, 4, 32, width), BF),
        ],
        in_specs=[smem()] + [vmem()] * 5 + [hbm()],
        out_specs=[vmem()] * 3 + [hbm()] * 2,
        scratch_shapes=[
            pltpu.VMEM((32, 32, width), BF), pltpu.VMEM((rows, width), BF), pltpu.VMEM((8, 4, 32, width), BF),
            pltpu.SemaphoreType.DMA, pltpu.SemaphoreType.DMA((8,)),
        ],
        compiler_params=params(),
        cost_estimate=cost(4 * rows * width * width, 14 * MIB),
        name="cross_out_grad",
    )(sel, da3, x2, cot, mixed, vec, pack)


def attend_grad_kernel(causal, valid, q_ref, k_ref, v_ref, o_ref, do_ref, lse_ref, dq_ref, dk_ref, dv_ref):
    rows = q_ref.shape[0]
    scale = jnp.asarray(HD**-0.5, BF)
    query = masked_pair(q_ref[...] * scale)
    grad_out = masked_pair(do_ref[...])
    product = (do_ref[...].astype(F32) * o_ref[...].astype(F32)).T
    delta = jnp.concatenate(
        [jnp.sum(product[:HD], axis=0, keepdims=True), jnp.sum(product[HD:], axis=0, keepdims=True)], axis=1
    )
    lse = lse_ref[0]
    grad_query = jnp.zeros((2 * HD, 2 * rows), F32)
    for a, b in key_chunks(k_ref.shape[0]):
        key = k_ref[a:b, :]
        scores = exclude(dot_nt(key, query), a, rows, causal, valid)
        probs = jnp.exp(scores - lse)
        grad_probs = dot_nt(v_ref[a:b, :], grad_out)
        grad_scores = (probs * (grad_probs - delta)).astype(BF)
        dv_ref[a:b, :] = dot(probs.astype(BF), grad_out).astype(BF)
        dk_ref[a:b, :] = dot(grad_scores, query).astype(BF)
        grad_query += dot_tn(key, grad_scores)
    dq_ref[...] = (pair_back(grad_query, rows) * HD**-0.5).astype(BF)


def attend_grad(query, key, value, mixed, grad_mixed, lse, causal, valid):
    rows, width = query.shape
    keys = key.shape[0]
    pairs = width // (2 * HD)

    def column(count):
        return pl.BlockSpec((count, 2 * HD), lambda h: (0, h))

    line = pl.BlockSpec((1, 1, 2 * rows), lambda h: (h, 0, 0))
    return pl.pallas_call(
        functools.partial(attend_grad_kernel, causal, valid),
        grid=(pairs,),
        out_shape=[shape((rows, width), BF)] + [shape((keys, width), BF)] * 2,
        in_specs=[column(rows), column(keys), column(keys), column(rows), column(rows), line],
        out_specs=[column(rows), column(keys), column(keys)],
        compiler_params=params(),
        cost_estimate=cost(40 * rows * keys * width, 8 * keys * width),
        name="attend_causal_grad" if causal else "attend_grad",
    )(query, key, value, mixed, grad_mixed, lse)


def cross_query_grad_kernel(
    sel_ref, a_ref, dq_ref, x1_ref, dx2_ref, o_ref, vec_ref, pack,
    dx_ref, do_ref, sums_ref, keep, send, bufs, da_ref, e_ref, grads, sem, sems,
):
    copies = [weight_copy(pack, 32 * (4 - n), bufs.at[n], sem.at[n]) for n in range(2)]
    start_all(copies)
    sel = sel_ref[0]
    grad_weight(a_ref, dq_ref, grads.at[0])
    out = block_copies(sel, grads.at[0], keep, send, 32, sems.at[0])
    start_all(out)
    sums_ref[0:1, :] = column_sum(dq_ref)
    copies[0].wait()

    def put_act(start, value):
        da_ref[:, pl.ds(start, TILE)] = value

    times_t(dq_ref, bufs.at[0], put_act)

    def put(rows, value):
        total = dx2_ref[rows, :] + value
        dx_ref[rows, :] = total
        e_ref[rows, :] = total.astype(BF)

    gain, shift = norm_grad(x1_ref, da_ref, vec_ref[2:3, :], put)
    sums_ref[1:2, :] = gain
    sums_ref[2:3, :] = shift
    sums_ref[3:4, :] = column_sum(e_ref)
    grad_weight(o_ref, e_ref, grads.at[1])
    more = block_copies(sel, grads.at[1], keep, send, 0, sems.at[1])
    start_all(more)
    copies[1].wait()

    def put_mixed(start, value):
        do_ref[:, pl.ds(start, TILE)] = value.astype(BF)

    times_t(e_ref, bufs.at[1], put_mixed)
    wait_all(out)
    wait_all(more)


def cross_query_grad(sel, a2, dq2, x1, dx2, mixed, vec, pack):
    rows, width = x1.shape
    return pl.pallas_call(
        cross_query_grad_kernel,
        out_shape=[
            shape((rows, width), F32), shape((rows, width), BF), shape((4, width), F32),
            shape((4, 4, 64, width), BF), shape((4, 4, 64, width), BF),
        ],
        in_specs=[smem()] + [vmem()] * 6 + [hbm()],
        out_specs=[vmem()] * 3 + [hbm()] * 2,
        scratch_shapes=[
            pltpu.VMEM((2, 32, 32, width), BF), pltpu.VMEM((rows, width), F32), pltpu.VMEM((rows, width), BF),
            pltpu.VMEM((2, 8, 4, 32, width), BF), pltpu.SemaphoreType.DMA((2,)), pltpu.SemaphoreType.DMA((2, 8)),
        ],
        compiler_params=params(),
        cost_estimate=cost(8 * rows * width * width, 20 * MIB),
        name="cross_query_grad",
    )(sel, a2, dq2, x1, dx2, mixed, vec, pack)


def cross_key_grad_kernel(sel_ref, e_ref, dk_ref, dv_ref, sums_ref, keep, send, grads, sems):
    sel = sel_ref[0]
    copies = []
    for n, ref in enumerate((dk_ref, dv_ref)):
        grad_weight(e_ref, ref, grads.at[n])
        out = block_copies(sel, grads.at[n], keep, send, 32 * n, sems.at[n])
        start_all(out)
        copies += out
    sums_ref[...] = column_sum(dv_ref)
    wait_all(copies)


def cross_key_grad(sel, enc, dk2, dv2):
    frames, width = enc.shape
    return pl.pallas_call(
        cross_key_grad_kernel,
        out_shape=[shape((1, width), F32), shape((4, 4, 64, width), BF), shape((4, 4, 64, width), BF)],
        in_specs=[smem()] + [vmem()] * 3,
        out_specs=[vmem()] + [hbm()] * 2,
        scratch_shapes=[pltpu.VMEM((2, 8, 4, 32, width), BF), pltpu.SemaphoreType.DMA((2, 8))],
        compiler_params=params(),
        cost_estimate=cost(4 * frames * width * width, 14 * MIB),
        name="cross_key_grad",
    )(sel, enc, dk2, dv2)


def encoder_grad_kernel(dk_ref, dv_ref, pack, out_ref, bufs, sems):
    copies = [weight_copy(pack, 32 * (5 + n), bufs.at[n], sems.at[n]) for n in range(2)]
    start_all(copies)
    wait_all(copies)

    def put(start, value):
        out_ref[:, pl.ds(start, TILE)] = value

    times_t(dk_ref, bufs.at[0], put)

    def add(start, value):
        out_ref[:, pl.ds(start, TILE)] += value

    times_t(dv_ref, bufs.at[1], add)


def encoder_grad(dk2, dv2, pack):
    frames, width = dk2.shape
    return pl.pallas_call(
        encoder_grad_kernel,
        out_shape=shape((frames, width), F32),
        in_specs=[vmem()] * 2 + [hbm()],
        out_specs=vmem(),
        scratch_shapes=[pltpu.VMEM((2, 32, 32, width), BF), pltpu.SemaphoreType.DMA((2,))],
        compiler_params=params(),
        cost_estimate=cost(4 * frames * width * width, 16 * MIB),
        name="encoder_grad",
    )(dk2, dv2, pack)


def self_in_grad_kernel(
    sel_ref, a_ref, dq_ref, dk_ref, dv_ref, x_ref, dx1_ref, vec_ref, pack,
    dx_ref, sums_ref, keep, send, bufs, da_ref, grads, sem, sems,
):
    copies = [weight_copy(pack, 32 * n, bufs.at[n], sem.at[n]) for n in range(3)]
    start_all(copies)
    sel = sel_ref[0]
    out = []
    grad_refs = (dq_ref, dk_ref, dv_ref)
    for n, ref in enumerate(grad_refs):
        grad_weight(a_ref, ref, grads.at[n])
        more = block_copies(sel, grads.at[n], keep, send, 32 * n, sems.at[n])
        start_all(more)
        out += more
    sums_ref[0:1, :] = column_sum(dq_ref)
    sums_ref[1:2, :] = column_sum(dv_ref)
    for n, ref in enumerate(grad_refs):
        copies[n].wait()

        def put_act(start, value, n=n):
            if n:
                da_ref[:, pl.ds(start, TILE)] += value
            else:
                da_ref[:, pl.ds(start, TILE)] = value

        times_t(ref, bufs.at[n], put_act)

    def put(rows, value):
        dx_ref[rows, :] = dx1_ref[rows, :] + value

    gain, shift = norm_grad(x_ref, da_ref, vec_ref[0:1, :], put)
    sums_ref[2:3, :] = gain
    sums_ref[3:4, :] = shift
    wait_all(out)


def self_in_grad(sel, a1, dq1, dk1, dv1, x, dx1, vec, pack):
    rows, width = x.shape
    return pl.pallas_call(
        self_in_grad_kernel,
        out_shape=[
            shape((rows, width), F32), shape((4, width), F32),
            shape((4, 4, 96, width), BF), shape((4, 4, 96, width), BF),
        ],
        in_specs=[smem()] + [vmem()] * 7 + [hbm()],
        out_specs=[vmem()] * 2 + [hbm()] * 2,
        scratch_shapes=[
            pltpu.VMEM((3, 32, 32, width), BF), pltpu.VMEM((rows, width), F32),
            pltpu.VMEM((3, 8, 4, 32, width), BF), pltpu.SemaphoreType.DMA((3,)), pltpu.SemaphoreType.DMA((3, 8)),
        ],
        compiler_params=params(),
        cost_estimate=cost(12 * rows * width * width, 24 * MIB),
        name="self_in_grad",
    )(sel, a1, dq1, dk1, dv1, x, dx1, vec, pack)


SWAP = [(0, 1), (1, 0)]


def add_rounded(left, right):
    return (left.astype(F32) + right.astype(F32)).astype(BF)


def reduce_chain(part, received, first, second):
    def side(value, axis, at):
        return lax.index_in_dim(value, at, axis=0 if axis == "y" else 1, keepdims=True)

    out = add_rounded(side(part, first, 1), side(received, first, 1))
    mine = add_rounded(side(part, first, 0), side(received, first, 0))
    other = lax.ppermute(out, first, SWAP)
    out = add_rounded(side(mine, second, 1), side(other, second, 1))
    mine = add_rounded(side(mine, second, 0), side(other, second, 0))
    other = lax.ppermute(out, second, SWAP)
    return add_rounded(mine, other)[0, 0]


def reduce_fast(keep, send):
    rows, columns = keep.shape[2:]
    received = lax.ppermute(send, "c", SWAP)
    keep = keep.reshape((2, 2, 4, rows, columns))
    received = received.reshape(keep.shape)
    half = rows // 2
    parts = [
        reduce_chain(keep[:, :, :, :half], received[:, :, :, :half], "x", "y"),
        reduce_chain(keep[:, :, :, half:], received[:, :, :, half:], "y", "x"),
    ]
    both = jnp.concatenate(parts, axis=1)
    here = lax.axis_index("z")
    total = lax.dynamic_index_in_dim(both, here, 0, keepdims=False).astype(F32)
    for step in (1, 3, 2):
        piece = lax.dynamic_index_in_dim(both, lax.rem(here + step, 4), 0, keepdims=False)
        total += lax.ppermute(piece, "z", [(n, (n + step) % 4) for n in range(4)]).astype(F32)
    return total


def reduce_plain(keep, send):
    count = lax.axis_size(ALL)
    rows, columns = keep.shape[2:]
    whole = jnp.stack([keep, send], axis=1).reshape(32, rows, columns)
    if rows == 128:
        whole = whole.reshape(32 * rows, columns)
        return lax.psum_scatter(whole.astype(F32), ALL, scatter_dimension=0, tiled=True)
    many = rows // 32
    whole = whole.reshape(32, many, 32, columns).swapaxes(0, 1).reshape(many, 1024, columns)
    mine = lax.psum_scatter(whole.astype(F32), ALL, scatter_dimension=1, tiled=True)
    return mine.reshape(many * (1024 // count), columns)


def exchange(value, combine, axes):
    for axis in axes:
        size = lax.axis_size(axis)
        moved = [lax.ppermute(value, axis, [(n, (n + step) % size) for n in range(size)]) for step in range(1, size)]
        for other in moved:
            value = combine(value, other)
    return value


def gather_fast(attention, expand, contract, vectors):
    width = attention.shape[2]
    line = jnp.pad(vectors.reshape(1, -1), ((0, 7), (0, width - vectors.size)))
    attention = jnp.concatenate([attention.reshape(-1, width), line], axis=0)
    pieces = [expand[:, n * width : (n + 1) * width] for n in range(expand.shape[1] // width)]
    feed_pack = jnp.concatenate(pieces + [contract], axis=0)
    pack_a = lax.all_gather(attention, ALL, axis=0, tiled=False)
    pack_f = lax.all_gather(feed_pack, ALL, axis=0, tiled=False)
    vec = pack_a[:, 256, : vectors.size].reshape((32,) + vectors.shape).swapaxes(0, 1)
    return pack_a, pack_f, vec.reshape(vectors.shape[0], width).astype(F32)


def gather_plain(attention, expand, contract, vectors):
    attention = lax.all_gather(attention, ALL, axis=1, tiled=True)
    expand = lax.all_gather(expand, ALL, axis=0, tiled=True)
    contract = lax.all_gather(contract, ALL, axis=0, tiled=True)
    vectors = lax.all_gather(vectors, ALL, axis=1, tiled=True)
    width = attention.shape[2]
    pack_a = attention.reshape(8, 32, 32, width).swapaxes(0, 1).reshape(32, 256, width)
    first = expand.reshape(32, 32, 4, width).swapaxes(1, 2).reshape(32, 128, width)
    pack_f = jnp.concatenate([first, contract.reshape(32, 128, width)], axis=1)
    return pack_a, pack_f, vectors.astype(F32)


def adam_update(master, gradient, first, second, step_value, clip_scale):
    first_new = beta_first * first.astype(F32) + (1.0 - beta_first) * gradient
    second_new = beta_second * second + (1.0 - beta_second) * gradient * gradient
    direction = (
        first_new
        / (1.0 - beta_first**step_value)
        / (jnp.sqrt(second_new / (1.0 - beta_second**step_value)) + eps_adam)
    )
    master_new = (master - learn_rate * (direction + weight_decay * master)) * clip_scale
    return (first_new, second_new, master_new)


def head_maxima(top, rows):
    return jnp.max(top.reshape(-1, rows), axis=1)


def one_sequence(sel, x, enc, frames, cot, vec, pack_a, pack_f):
    rows = x.shape[0]
    a1, q1, k1, v1 = self_in(x, vec, pack_a)
    o1, lse1, top1 = attend(q1, k1, v1, True, rows)
    x1, a2, q2 = self_out(o1, x, vec, pack_a)
    k2, v2 = cross_in(enc, vec, pack_a)
    o2, lse2, top2 = attend(q2, k2, v2, False, frames)
    maxima = jnp.stack([head_maxima(top1, rows), head_maxima(top2, rows)])
    x2, a3 = cross_out(o2, x1, vec, pack_a)
    result, da3, gb1, gb2, keep1, send1, keep2, send2 = feed(sel, a3, x2, cot, vec, pack_f)
    dx2, do2, sums3, keep_co, send_co = cross_out_grad(sel, da3, x2, cot, o2, vec, pack_a)
    dq2, dk2, dv2 = attend_grad(q2, k2, v2, o2, do2, lse2, False, frames)
    sums_v, keep_kv, send_kv = cross_key_grad(sel, enc, dk2, dv2)
    dx1, do1, sums2, keep_oq, send_oq = cross_query_grad(sel, a2, dq2, x1, dx2, o1, vec, pack_a)
    dq1, dk1, dv1 = attend_grad(q1, k1, v1, o1, do1, lse1, True, rows)
    grad_input, sums1, keep_s, send_s = self_in_grad(sel, a1, dq1, dk1, dv1, x, dx1, vec, pack_a)
    grad_encoder = encoder_grad(dk2, dv2, pack_a)[:frames]
    g_vectors = jnp.concatenate(
        [
            sums1[2:4], sums2[1:3], sums3[0:2],
            sums1[0:2], sums2[3:4], sums2[0:1], sums_v, sums3[2:3], gb2,
            gb1.reshape(-1, x.shape[1]),
        ],
        axis=0,
    )
    packs = [(keep1, send1), (keep2, send2), (keep_co, send_co), (keep_kv, send_kv), (keep_oq, send_oq), (keep_s, send_s)]
    return result, grad_input, grad_encoder, g_vectors, maxima, packs


def local(
    fast,
    inputs,
    encoder,
    cotangent,
    attention_master,
    expand_master,
    contract_master,
    vectors_master,
    attention_first,
    expand_first,
    contract_first,
    vectors_first,
    attention_second,
    expand_second,
    contract_second,
    vectors_second,
):
    sequences, rows, width = inputs.shape
    frames = encoder.shape[1]
    padded = -(-frames // 16) * 16
    owned = [m.astype(BF) for m in (attention_master, expand_master, contract_master, vectors_master)]
    pack_a, pack_f, vec = (gather_fast if fast else gather_plain)(*owned)
    place = lax.axis_index(("y", "x", "c")) if fast else 0
    sel = jnp.full((1,), place, jnp.int32)
    done = []
    for n in range(sequences):
        enc = jnp.pad(encoder[n], ((0, padded - frames), (0, 0)))
        done.append(one_sequence(sel, inputs[n], enc, frames, cotangent[n], vec, pack_a, pack_f))
    result, grad_input, grad_encoder = (jnp.stack([d[k] for d in done]) for k in range(3))
    g_vectors = sum(d[3] for d in done[1:]) + done[0][3] if sequences > 1 else done[0][3]
    maxima = functools.reduce(jnp.maximum, [d[4] for d in done])
    packs = done[0][5]
    for d in done[1:]:
        packs = [tuple(add_rounded(a, b) for a, b in zip(p, q)) for p, q in zip(packs, d[5])]

    if fast:
        maxima = exchange(jnp.pad(maxima, ((0, 6), (0, 112))), jnp.maximum, ("c", "x", "y", "z"))[:2, :16]
        reduce = reduce_fast
    else:
        maxima = lax.pmax(maxima, ALL)
        reduce = reduce_plain
    g_expand, g_contract, g_co, g_kv, g_oq, g_s = [reduce(*p) for p in packs]

    def apart(value):
        return value.reshape(-1, attention_master.shape[1], width)

    g_oq, g_kv = apart(g_oq), apart(g_kv)
    g_attention = jnp.concatenate([apart(g_s), g_oq, g_kv, apart(g_co)], axis=0)
    shard_cols = vectors_master.shape[1]
    first_col = lax.axis_index(ALL) * shard_cols
    if fast:
        g_vectors = exchange(jnp.pad(g_vectors, ((0, 7), (0, 0))), jnp.add, ("c", "x", "y", "z"))[:VEC_ROWS]
        g_vectors = lax.dynamic_slice_in_dim(g_vectors, first_col, shard_cols, 1)
    else:
        g_vectors = lax.psum_scatter(g_vectors, ALL, scatter_dimension=1, tiled=True)

    clip_cols = jnp.repeat(jnp.sqrt(clip_limit / jnp.maximum(maxima, clip_limit)), HD, axis=1)
    unit_row = jnp.ones_like(clip_cols[0])
    clip_attention = jnp.stack(
        [clip_cols[0], clip_cols[0], unit_row, unit_row, clip_cols[1], clip_cols[1], unit_row, unit_row]
    )[:, None, :]
    local_cols = lax.dynamic_slice_in_dim(clip_cols, first_col, shard_cols, 1)
    clip_vectors = jnp.ones_like(vectors_master).at[6].set(local_cols[0]).at[9].set(local_cols[1])
    step_value = float(ADAM_STEP)
    new_attention = adam_update(
        attention_master, g_attention, attention_first, attention_second, step_value, clip_attention
    )
    new_expand = adam_update(expand_master, g_expand, expand_first, expand_second, step_value, 1.0)
    new_contract = adam_update(contract_master, g_contract, contract_first, contract_second, step_value, 1.0)
    new_vectors = adam_update(vectors_master, g_vectors, vectors_first, vectors_second, step_value, clip_vectors)
    return (
        result,
        grad_input,
        grad_encoder,
        g_attention,
        g_expand,
        g_contract,
        g_vectors,
        new_attention[0],
        new_expand[0],
        new_contract[0],
        new_vectors[0],
        new_attention[1],
        new_expand[1],
        new_contract[1],
        new_vectors[1],
        new_attention[2],
        new_expand[2],
        new_contract[2],
        new_vectors[2],
    )


def solution(mesh):
    planes = mesh.shape["dp"] // 2
    side = math.isqrt(planes)
    if side * side * 2 != mesh.shape["dp"]:
        side = 1
    sizes = (mesh.shape["dp"] // (2 * side), side, 2, mesh.shape["fsdp"])
    fast = sizes == (2, 2, 2, 4)
    mesh = Mesh(mesh.devices.reshape(sizes), ALL)
    shards = (
        P(ALL, None, None),
        P(ALL, None, None),
        P(ALL, None, None),
    )
    weights = (P(None, ALL, None), P(ALL, None), P(ALL, None), P(None, ALL))
    return jax.shard_map(
        functools.partial(local, fast),
        mesh=mesh,
        in_specs=shards + weights * 3,
        out_specs=shards + weights * 4,
        check_vma=False,
    )
```

time: 2160 us -> 673 us (0.31)
  waiting for transfers between devices: 1570 us -> 294 us
  matrix products: 326 us -> 0 us
  Pallas kernels: 0 us -> 202 us
  blocking collectives: 113 us -> 0 us
  starting transfers between devices: 0.46 us -> 80.1 us
  other arithmetic: 69.7 us -> 31.3 us
  local copies, waits for them, and re-layouts: 67.8 us -> 40 us
    reduce_scatter x3 -> x0, waiting for transfers between devices: 1440 us -> none  [the longest x1 710 us: local(): lax.psum_scatter(g_attention, ('dp', 'fsdp'), scatter_dimension=1, tiled=...]
    dot_general x86 -> x0, matrix products: 326 us -> none  [the longest x10 64.3 us: matmul(): return jnp.dot(left, right, preferred_element_type=jnp.float32)]
    pallas_call x0 -> x14, Pallas kernels: none -> 202 us  [the longest x2 45.9 us: attend_grad(): pl.pallas_call(functools.partial(attend_grad_kernel, causal, valid), grid...]
    ppermute x0 -> x60, waiting for transfers between devices: none -> 129 us  [the longest x12 51.9 us: reduce_chain(): other = lax.ppermute(out, first, SWAP)]
    ppermute x0 -> x60, starting transfers between devices: none -> 80.1 us  [the longest x18 39.5 us: reduce_fast(): lax.ppermute(piece, 'z', [(n, (n + step) % 4) for n in range(4)])]
    all_gather x1 -> x0, blocking collectives: 73 us -> none  [local(): lax.all_gather(owned_weights[3], ('dp', 'fsdp'), axis=1, tiled=True)]
    all_gather x3 -> x2, waiting for transfers between devices: 117 us -> 166 us  [the longest x1 113 us: gather_fast(): pack_a = lax.all_gather(attention, ALL, axis=0, tiled=False)]
    pmax x1 -> x0, blocking collectives: 39.8 us -> none  [local(): maxima = lax.pmax(jnp.stack([max_self, max_cross]), ('dp', 'fsdp'))]
  transfers between devices with their start and end apart: 7 -> 62, of which waited for: 6 -> 37; matrix products, arithmetic and copies ran while one was open for 10% -> 8% of each run, Pallas kernels for 0% -> 15%
where the time goes in v1:
time: 673 us; the launch traced here: 663 us
  waiting for transfers between devices  294 us (44%)
  Pallas kernels  202 us (30%)
  starting transfers between devices  80.1 us (12%)
  local copies, waits for them, and re-layouts  40 us (6%)
  other arithmetic  31.3 us (5%)
  between operations  15.6 us (2%)
    all_gather x1, waiting for transfers between devices, gather_fast(): pack_a = lax.all_gather(attention, ALL, axis=0, tiled=False)  113 us
    all_gather x1, waiting for transfers between devices, gather_fast(): pack_f = lax.all_gather(feed_pack, ALL, axis=0, tiled=False)  52.2 us
    ppermute x12, waiting for transfers between devices, reduce_chain(): other = lax.ppermute(out, first, SWAP)  51.9 us
    pallas_call x2, Pallas kernels, attend_grad(): pl.pallas_call(functools.partial(attend_grad_kernel, causal, valid), grid...  45.9 us
    ppermute x18, starting transfers between devices, reduce_fast(): lax.ppermute(piece, 'z', [(n, (n + step) % 4) for n in range(4)])  39.5 us
    pallas_call x1, Pallas kernels, feed(): pl.pallas_call(feed_kernel, grid=(8,), out_shape=[shape((rows, width), BF...  32.7 us
    ppermute x18, waiting for transfers between devices, reduce_fast(): lax.ppermute(piece, 'z', [(n, (n + step) % 4) for n in range(4)])  31.7 us
    ppermute x12, waiting for transfers between devices, reduce_chain(): other = lax.ppermute(out, second, SWAP)  31.1 us
  transfers between devices with their start and end apart: 62, of which 37 were waited for; matrix products, arithmetic and copies ran while one was open for 8% of the time, Pallas kernels for 15%

profile of v1, /device:TPU:0, one launch (start us, length us, event | category | flops | bytes accessed | tf_op | source)
XLA Modules:
  0.0 663.3 jit_solution(7177086222341633590)
XLA Ops:
  17.9 113.5 %all-gather.5.cloned.1.call-done = bf16[8448,1024]{1,0:T(8,128)(2,1)} async-done(((bf16[264,1024]{1,0:T(8,128)(2,1)}), bf16[8448,1024]{1,0:T(8,128)(2,1)}) %all-gather.5.cloned.1.call-update) | async-done | bytes 17301520 | tf_op jit(solution)/shard_map/all_gather | solution.py:792
  133.0 6.7 %self_in.1 = (bf16[448,1024]{1,0:T(8,128)(2,1)S(1)}, bf16[448,1024]{1,0:T(8,128)(2,1)S(1)}, bf16[448,1024]{1,0:T(8,128)(2,1)S(1)}, bf16[448,1024]{1,0:T(8,128)(2,1)S(1)}) custom-call(bf16[448,1024]{1,0:T(8,128)(2,1)S(1)} %bitcast.131, f32[17,1024]{1,0:T(8,128)S(1)} %convert_element_type.676.vec_ref, bf16[32,264,1024]{2,1,0:T(8,128)(2,1)} %bitcast.141), custom_call_target="tpu_custom_call" | custom-call | flops 2818572288 | bytes 10485760 | tf_op jit(solution)/shard_map/self_in/pallas_call | solution.py:175
  139.8 8.2 %attend_causal.1 = (bf16[448,1024]{1,0:T(8,128)(2,1)S(1)}, f32[8,1,896]{2,1,0:T(1,128)S(1)}, f32[8,1,896]{2,1,0:T(1,128)S(1)}) custom-call(bf16[448,1024]{1,0:T(8,128)(2,1)S(1)} %get-tuple-element.91.q_ref, bf16[448,1024]{1,0:T(8,128)(2,1)S(1)} %get-tuple-element.92.k_ref, bf16[448,1024]{1,0:T(8,128)(2,1)S(1)} %get-tuple-element.93.v_ref), custom_call_target="tpu_custom_call" | custom-call | flops 3288334336 | bytes 1835008 | tf_op jit(solution)/shard_map/attend_causal/pallas_call | solution.py:241
  154.5 14.2 %cross_in.1 = (bf16[1504,1024]{1,0:T(8,128)(2,1)S(1)}, bf16[1504,1024]{1,0:T(8,128)(2,1)}) custom-call(bf16[1504,1024]{1,0:T(8,128)(2,1)} %pad.22.e_ref, f32[17,1024]{1,0:T(8,128)S(1)} %convert_element_type.676.vec_ref, bf16[32,264,1024]{2,1,0:T(8,128)(2,1)} %bitcast.143), custom_call_target="tpu_custom_call" | custom-call | flops 6308233216 | bytes 14680064 | tf_op jit(solution)/shard_map/cross_in/pallas_call | solution.py:304
  168.8 21.0 %attend.1 = (bf16[448,1024]{1,0:T(8,128)(2,1)S(1)}, f32[8,1,896]{2,1,0:T(1,128)S(1)}, f32[8,1,896]{2,1,0:T(1,128)S(1)}) custom-call(bf16[448,1024]{1,0:T(8,128)(2,1)S(1)} %get-tuple-element.95.q_ref, bf16[1504,1024]{1,0:T(8,128)(2,1)S(1)} %get-tuple-element.96.k_ref, bf16[1504,1024]{1,0:T(8,128)(2,1)} %get-tuple-element.97.v_ref), custom_call_target="tpu_custom_call" | custom-call | flops 11039408128 | bytes 6160384 | tf_op jit(solution)/shard_map/attend/pallas_call | solution.py:241
  195.9 52.2 %all-gather.7.cloned.1.call-done = bf16[8192,1024]{1,0:T(8,128)(2,1)} async-done(((bf16[256,1024]{1,0:T(8,128)(2,1)}), bf16[8192,1024]{1,0:T(8,128)(2,1)}) %all-gather.7.cloned.1.call-update) | async-done | bytes 16777232 | tf_op jit(solution)/shard_map/all_gather | solution.py:793
  250.8 32.7 %feed.1 = (bf16[448,1024]{1,0:T(8,128)(2,1)}, f32[448,1024]{1,0:T(8,128)S(1)}, f32[8,1,512]{2,1,0:T(1,128)S(1)}, f32[1,1024]{1,0:T(1,128)S(1)}, bf16[4,4,32,4096...) custom-call(s32[1]{0:T(128)} %bitcast.sel_ref, ...), custom_call_target="tpu_custom_call" | custom-call | flops 22548578304 | bytes 41943040 | tf_op jit(solution)/shard_map/feed/pallas_call | solution.py:418
  284.7 8.8 %cross_out_grad.1 = (f32[448,1024]{1,0:T(8,128)}, bf16[448,1024]{1,0:T(8,128)(2,1)S(1)}, f32[3,1024]{1,0:T(4,128)S(1)}, bf16[4,4,32,1024]{3,2,1,0:T(8,128)(2,1)S(1)}, bf16[4,4,32,1024]{3,2,1,0:T(8,128)(2,1)S(1)}) custom-call(s32[1]{0:T(128)} %bitcast.sel_ref, f32[448,1024]{1,0:T(8,128)} %copy-done.13, f32[448,1024]{1,0:T(8,128)} %copy-done.11, ...), custom_call_target="tpu_custom_call" | custom-call | flops 1879048192 | bytes 14680064 | tf_op jit(solution)/shard_map/cross_out_grad/pallas_call | solution.py:491
  294.5 32.4 %attend_grad.1 = (bf16[448,1024]{1,0:T(8,128)(2,1)S(1)}, bf16[1504,1024]{1,0:T(8,128)(2,1)}, bf16[1504,1024]{1,0:T(8,128)(2,1)}) custom-call(bf16[448,1024]{1,0:T(8,128)(2,1)S(1)} %copy-done.30, bf16[1504,1024]{1,0:T(8,128)(2,1)} %copy-done.32, bf16[1504,1024]{1,0:T(8,128)(2,1)} %get-tuple-element.97.v_ref, bf16[448,1024]{1,0:T(8,128)(2,1)S(1)} %copy-done.5, ...), custom_call_target="tpu_custom_call" | custom-call | flops 27598520320 | bytes 12320768 | tf_op jit(solution)/shard_map/attend_grad/pallas_call | solution.py:541
  327.8 13.1 %cross_key_grad.1 = (f32[1,1024]{1,0:T(1,128)S(1)}, bf16[4,4,64,1024]{3,2,1,0:T(8,128)(2,1)S(1)}, bf16[4,4,64,1024]{3,2,1,0:T(8,128)(2,1)S(1)}) custom-call(s32[1]{0:T(128)} %bitcast.sel_ref, bf16[1504,1024]{1,0:T(8,128)(2,1)} %pad.22.e_ref, bf16[1504,1024]{1,0:T(8,128)(2,1)} %get-tuple-element.117.dk_ref, bf16[1504,1024]{1,0:T(8,128)(2,1)} %get-tuple-element.118.dv_ref), custom_call_target="tpu_custom_call" | custom-call | flops 6308233216 | bytes 14680064 | tf_op jit(solution)/shard_map/cross_key_grad/pallas_call | solution.py:627
  341.0 14.5 %encoder_grad.1 = f32[1504,1024]{1,0:T(8,128)} custom-call(bf16[1504,1024]{1,0:T(8,128)(2,1)S(1)} %copy-done.6, bf16[1504,1024]{1,0:T(8,128)(2,1)S(1)} %copy-done.7, bf16[32,264,1024]{2,1,0:T(8,128)(2,1)} %bitcast.146), custom_call_target="tpu_custom_call" | custom-call | flops 6308233216 | bytes 16777216 | tf_op jit(solution)/shard_map/encoder_grad/pallas_call | solution.py:657
  356.6 6.6 slice_bitcast_fusion
  363.2 11.6 %cross_query_grad.1 = (f32[448,1024]{1,0:T(8,128)S(1)}, bf16[448,1024]{1,0:T(8,128)(2,1)S(1)}, f32[4,1024]{1,0:T(4,128)S(1)}, bf16[4,4,64,1024]{3,2,1,0:T(8,128)(2,1)}, bf16[4,4,64,1024]{3,2,1,0:T(8,128)(2,1)}) custom-call(s32[1]{0:T(128)} %bitcast.sel_ref, bf16[448,1024]{1,0:T(8,128)(2,1)S(1)} %copy-done.21, bf16[448,1024]{1,0:T(8,128)(2,1)S(1)} %copy-done.23, ...), custom_call_target="tpu_custom_call" | custom-call | flops 3758096384 | bytes 20971520 | tf_op jit(solution)/shard_map/cross_query_grad/pallas_call | solution.py:595
  376.9 13.5 %attend_causal_grad.1 = (bf16[448,1024]{1,0:T(8,128)(2,1)S(1)}, bf16[448,1024]{1,0:T(8,128)(2,1)S(1)}, bf16[448,1024]{1,0:T(8,128)(2,1)S(1)}) custom-call(bf16[448,1024]{1,0:T(8,128)(2,1)S(1)} %get-tuple-element.91.q_ref, bf16[448,1024]{1,0:T(8,128)(2,1)S(1)} %copy-done.26, bf16[448,1024]{1,0:T(8,128)(2,1)S(1)} %copy-done.28, bf16[448,1024]{1,0:T(8,128)(2,1)} %copy-done.2, ...), custom_call_target="tpu_custom_call" | custom-call | flops 8220835840 | bytes 3670016 | tf_op jit(solution)/shard_map/attend_causal_grad/pallas_call | solution.py:541
  391.7 15.8 %self_in_grad.1 = (f32[448,1024]{1,0:T(8,128)}, f32[4,1024]{1,0:T(4,128)S(1)}, bf16[4,4,96,1024]{3,2,1,0:T(8,128)(2,1)}, bf16[4,4,96,1024]{3,2,1,0:T(8,128)(2,1)}) custom-call(s32[1]{0:T(128)} %bitcast.sel_ref, bf16[448,1024]{1,0:T(8,128)(2,1)S(1)} %copy-done.19, bf16[448,1024]{1,0:T(8,128)(2,1)S(1)} %get-tuple-element.112.dq_ref, ...), custom_call_target="tpu_custom_call" | custom-call | flops 5637144576 | bytes 25165824 | tf_op jit(solution)/shard_map/self_in_grad/pallas_call | solution.py:707
  414.8 16.2 %copy.39 = f32[1,1500,1024]{2,0,1:T(1,128)} copy(f32[1,1500,1024]{2,1,0:T(8,128)} %slice_bitcast_fusion) | data formatting | bytes 12288000
  454.9 6.3 collective-permute-done.25
  480.8 7.0 %collective-permute-done.11 = bf16[1,2,4,32,1024]{4,3,2,1,0:T(8,128)(2,1)S(1)} collective-permute-done((bf16[1,2,4,32,1024]{4,3,2,1,0:T(8,128)(2,1)S(1)}, bf16[1,2,4,32,1024]{4,3,2,1,0:T(8,128)(2,1)S(1)}, u32[]{:S(2)}, u32[]{:S(2)}) %collective-permute-start.11) | collective-permute-done | bytes 524320 | tf_op jit(solution)/shard_map/ppermute | solution.py:738
  541.5 6.4 collective-permute-done.23
  549.2 7.9 %collective-permute-done.1 = bf16[2,1,4,48,1024]{4,3,2,1,0:T(8,128)(2,1)S(1)} collective-permute-done((bf16[2,1,4,48,1024]{4,3,2,1,0:T(8,128)(2,1)S(1)}, bf16[2,1,4,48,1024]{4,3,2,1,0:T(8,128)(2,1)S(1)}, u32[]{:S(2)}, u32[]{:S(2)}) %collective-permute-start.1) | collective-permute-done | bytes 786464 | tf_op jit(solution)/shard_map/ppermute | solution.py:738
  596.0 14.0 %collective-permute-done.43 = bf16[1,2,4,64,1024]{4,3,2,1,0:T(8,128)(2,1)S(1)} collective-permute-done((bf16[1,2,4,64,1024]{4,3,2,1,0:T(8,128)(2,1)S(1)}, bf16[1,2,4,64,1024]{4,3,2,1,0:T(8,128)(2,1)S(1)}, u32[]{:S(2)}, u32[]{:S(2)}) %collective-permute-start.43) | collective-permute-done | bytes 1048608 | tf_op jit(solution)/shard_map/ppermute | solution.py:738
  612.7 7.2 %collective-permute-done.36 = bf16[1,1,4,16,4096]{4,3,2,1,0:T(8,128)(2,1)S(1)} collective-permute-done((bf16[1,1,4,16,4096]{4,3,2,1,0:T(8,128)(2,1)S(1)}, bf16[1,1,4,16,4096]{4,3,2,1,0:T(8,128)(2,1)S(1)}, u32[]{:S(2)}, u32[]{:S(2)}) %collective-permute-start.36) | collective-permute-done | bytes 524320 | tf_op jit(solution)/shard_map/ppermute | solution.py:741
  631.5 10.0 %collective-permute-start.47 = (bf16[128,1024]{1,0:T(8,128)(2,1)S(1)}, bf16[128,1024]{1,0:T(8,128)(2,1)S(1)}, u32[]{:S(2)}, u32[]{:S(2)}) collective-permute-start(bf16[128,1024]{1,0:T(8,128)(2,1)S(1)} %get-tuple-element.219), channel_id=1, source_target_pairs={{0,2},{1,3},{2,0},{3,1},{4,6},{5,7},{6,4},{7,5},{8,10},{9,11},{10,... | collective-permute-start | bytes 786440 | tf_op jit(solution)/shard_map/ppermute | solution.py:760
  641.5 7.4 %collective-permute-done.39 = bf16[32,4096]{1,0:T(8,128)(2,1)S(1)} collective-permute-done((bf16[32,4096]{1,0:T(8,128)(2,1)S(1)}, bf16[32,4096]{1,0:T(8,128)(2,1)S(1)}, u32[]{:S(2)}, u32[]{:S(2)}) %collective-permute-start.39) | collective-permute-done | bytes 262176 | tf_op jit(solution)/shard_map/ppermute | solution.py:760
  (327 shorter events, 200.7 us)
Async XLA Ops:
  7.2 124.2 %all-gather.5.cloned.1.call-start = ((), (), s32[]{:S(2)}) async-start(), calls=%async_computation | async-start | bytes 17842176 | tf_op jit(solution)/shard_map/all_gather | solution.py:792
  10.2 237.8 %all-gather.7.cloned.1.call-start = ((), (), s32[]{:S(2)}) async-start(), calls=%async_computation.1 | async-start | bytes 17301504 | tf_op jit(solution)/shard_map/all_gather | solution.py:793
  356.0 34.4 %collective-permute-start.54 = (f32[8,128]{1,0:T(8,128)S(1)}, f32[8,128]{1,0:T(8,128)S(1)}, u32[]{:S(2)}, u32[]{:S(2)}) collective-permute-start(f32[8,128]{1,0:T(8,128)S(1)} %select_maximum_fusion), channel_id=1, source_target_pairs={{0,4},{4,0},{1,5},{5,1},{2,6},{6,2},{3,7},{7,3},{8,12},{12,8},{9,1... | collective-permute-start | bytes 12296 | tf_op jit(solution)/shard_map/ppermute | solution.py:780
  356.3 88.8 %collective-permute-start.24 = (bf16[4,4,32,1024]{3,2,1,0:T(8,128)(2,1)S(1)}, bf16[4,4,32,1024]{3,2,1,0:T(8,128)(2,1)}, u32[]{:S(2)}, u32[]{:S(2)}) collective-permute-start(bf16[4,4,32,1024]{3,2,1,0:T(8,128)(2,1)S(1)} %get-tuple-element.126), channel_id=1, source_target_pairs={{0,4},{4,0},{1,5},{5,1},{2,6},{6,2},{3,7},{7,3},{8,12},{12,8},{9,1... | collective-permute-start | bytes 3145736 | tf_op jit(solution)/shard_map/ppermute | solution.py:747
  411.2 20.0 %collective-permute-start.59 = (f32[8,128]{1,0:T(8,128)S(1)}, f32[8,128]{1,0:T(8,128)S(1)}, u32[]{:S(2)}, u32[]{:S(2)}) collective-permute-start(f32[8,128]{1,0:T(8,128)S(1)} %max.23), channel_id=1, source_target_pairs={{0,3},{1,0},{2,1},{3,2},{4,7},{5,4},{6,5},{7,6},{8,11},{9,8},{10,9... | collective-permute-start | bytes 12296 | tf_op jit(solution)/shard_map/ppermute | solution.py:780
  412.7 19.1 %collective-permute-start.58 = (f32[8,128]{1,0:T(8,128)S(1)}, f32[8,128]{1,0:T(8,128)S(1)}, u32[]{:S(2)}, u32[]{:S(2)}) collective-permute-start(f32[8,128]{1,0:T(8,128)S(1)} %max.23), channel_id=1, source_target_pairs={{0,2},{1,3},{2,0},{3,1},{4,6},{5,7},{6,4},{7,5},{8,10},{9,11},{10,... | collective-permute-start | bytes 12296 | tf_op jit(solution)/shard_map/ppermute | solution.py:780
  413.1 18.7 %collective-permute-start.57 = (f32[8,128]{1,0:T(8,128)S(1)}, f32[8,128]{1,0:T(8,128)S(1)}, u32[]{:S(2)}, u32[]{:S(2)}) collective-permute-start(f32[8,128]{1,0:T(8,128)S(1)} %max.23), channel_id=1, source_target_pairs={{0,1},{1,2},{2,3},{3,0},{4,5},{5,6},{6,7},{7,4},{8,9},{9,10},{10,1... | collective-permute-start | bytes 12296 | tf_op jit(solution)/shard_map/ppermute | solution.py:780
  431.2 40.0 %collective-permute-start.8 = (bf16[4,4,64,1024]{3,2,1,0:T(8,128)(2,1)}, bf16[4,4,64,1024]{3,2,1,0:T(8,128)(2,1)}, u32[]{:S(2)}, u32[]{:S(2)}) collective-permute-start(bf16[4,4,64,1024]{3,2,1,0:T(8,128)(2,1)} %get-tuple-element.122), channel_id=1, source_target_pairs={{0,4},{4,0},{1,5},{5,1},{2,6},{6,2},{3,7},{7,3},{8,12},{12,8},{9,1... | collective-permute-start | bytes 6291464 | tf_op jit(solution)/shard_map/ppermute | solution.py:747
  431.7 45.1 %collective-permute-start.16 = (bf16[4,4,64,1024]{3,2,1,0:T(8,128)(2,1)}, bf16[4,4,64,1024]{3,2,1,0:T(8,128)(2,1)}, u32[]{:S(2)}, u32[]{:S(2)}) collective-permute-start(bf16[4,4,64,1024]{3,2,1,0:T(8,128)(2,1)} %copy-done.24), channel_id=1, source_target_pairs={{0,4},{4,0},{1,5},{5,1},{2,6},{6,2},{3,7},{7,3},{8,12},{12,8},{9,1... | collective-permute-start | bytes 6291464 | tf_op jit(solution)/shard_map/ppermute | solution.py:747
  452.4 72.8 %collective-permute-start = (bf16[4,4,96,1024]{3,2,1,0:T(8,128)(2,1)S(1)}, bf16[4,4,96,1024]{3,2,1,0:T(8,128)(2,1)S(1)}, u32[]{:S(2)}, u32[]{:S(2)}) collective-permute-start(bf16[4,4,96,1024]{3,2,1,0:T(8,128)(2,1)S(1)} %copy-done.51), channel_id=1, source_target_pairs={{0,4},{4,0},{1,5},{5,1},{2,6},{6,2},{3,7},{7,3},{8,12},{12,8},{9,1... | collective-permute-start | bytes 9437192 | tf_op jit(solution)/shard_map/ppermute | solution.py:747
  454.9 103.8 %collective-permute-start.32 = (bf16[4,4,32,4096]{3,2,1,0:T(8,128)(2,1)}, bf16[4,4,32,4096]{3,2,1,0:T(8,128)(2,1)S(1)}, u32[]{:S(2)}, u32[]{:S(2)}) collective-permute-start(bf16[4,4,32,4096]{3,2,1,0:T(8,128)(2,1)} %get-tuple-element.128), channel_id=1, source_target_pairs={{0,4},{4,0},{1,5},{5,1},{2,6},{6,2},{3,7},{7,3},{8,12},{12,8},{9,1... | collective-permute-start | bytes 12582920 | tf_op jit(solution)/shard_map/ppermute | solution.py:747
  489.5 73.4 %collective-permute-start.40 = (bf16[4,4,128,1024]{3,2,1,0:T(8,128)(2,1)S(1)}, bf16[4,4,128,1024]{3,2,1,0:T(8,128)(2,1)S(1)}, u32[]{:S(2)}, u32[]{:S(2)}) collective-permute-start(bf16[4,4,128,1024]{3,2,1,0:T(8,128)(2,1)S(1)} %copy-done.50), channel_id=1, source_target_pairs={{0,4},{4,0},{1,5},{5,1},{2,6},{6,2},{3,7},{7,3},{8,12},{12,8},{9,1... | collective-permute-start | bytes 12582920 | tf_op jit(solution)/shard_map/ppermute | solution.py:747
  537.7 19.4 %collective-permute-start.1 = (bf16[2,1,4,48,1024]{4,3,2,1,0:T(8,128)(2,1)S(1)}, bf16[2,1,4,48,1024]{4,3,2,1,0:T(8,128)(2,1)S(1)}, u32[]{:S(2)}, u32[]{:S(2)}) collective-permute-start(bf16[2,1,4,48,1024]{4,3,2,1,0:T(8,128)(2,1)S(1)} %get-tuple-element.204), channel_id=1, source_target_pairs={{0,8},{8,0},{1,9},{9,1},{2,10},{10,2},{3,11},{11,3},{4,12},{12,4},... | collective-permute-start | bytes 2359304 | tf_op jit(solution)/shard_map/ppermute | solution.py:738
  560.2 30.9 %collective-permute-start.35 = (bf16[1,2,4,16,4096]{4,3,2,1,0:T(8,128)(2,1)S(1)}, bf16[1,2,4,16,4096]{4,3,2,1,0:T(8,128)(2,1)S(1)}, u32[]{:S(2)}, u32[]{:S(2)}) collective-permute-start(bf16[1,2,4,16,4096]{4,3,2,1,0:T(8,128)(2,1)S(1)} %get-tuple-element.198), channel_id=1, source_target_pairs={{0,16},{16,0},{1,17},{17,1},{2,18},{18,2},{3,19},{19,3},{4,20},{20... | collective-permute-start | bytes 3145736 | tf_op jit(solution)/shard_map/ppermute | solution.py:738
  561.0 32.7 %collective-permute-start.33 = (bf16[2,1,4,16,4096]{4,3,2,1,0:T(8,128)(2,1)S(1)}, bf16[2,1,4,16,4096]{4,3,2,1,0:T(8,128)(2,1)S(1)}, u32[]{:S(2)}, u32[]{:S(2)}) collective-permute-start(bf16[2,1,4,16,4096]{4,3,2,1,0:T(8,128)(2,1)S(1)} %get-tuple-element.200), channel_id=1, source_target_pairs={{0,8},{8,0},{1,9},{9,1},{2,10},{10,2},{3,11},{11,3},{4,12},{12,4},... | collective-permute-start | bytes 3145736 | tf_op jit(solution)/shard_map/ppermute | solution.py:738
  577.0 32.9 %collective-permute-start.43 = (bf16[1,2,4,64,1024]{4,3,2,1,0:T(8,128)(2,1)S(1)}, bf16[1,2,4,64,1024]{4,3,2,1,0:T(8,128)(2,1)S(1)}, u32[]{:S(2)}, u32[]{:S(2)}) collective-permute-start(bf16[1,2,4,64,1024]{4,3,2,1,0:T(8,128)(2,1)S(1)} %get-tuple-element.194), channel_id=1, source_target_pairs={{0,16},{16,0},{1,17},{17,1},{2,18},{18,2},{3,19},{19,3},{4,20},{20... | collective-permute-start | bytes 3145736 | tf_op jit(solution)/shard_map/ppermute | solution.py:738
  578.6 32.7 %collective-permute-start.41 = (bf16[2,1,4,64,1024]{4,3,2,1,0:T(8,128)(2,1)S(1)}, bf16[2,1,4,64,1024]{4,3,2,1,0:T(8,128)(2,1)S(1)}, u32[]{:S(2)}, u32[]{:S(2)}) collective-permute-start(bf16[2,1,4,64,1024]{4,3,2,1,0:T(8,128)(2,1)S(1)} %get-tuple-element.196), channel_id=1, source_target_pairs={{0,8},{8,0},{1,9},{9,1},{2,10},{10,2},{3,11},{11,3},{4,12},{12,4},... | collective-permute-start | bytes 3145736 | tf_op jit(solution)/shard_map/ppermute | solution.py:738
  591.3 28.6 %collective-permute-start.36 = (bf16[1,1,4,16,4096]{4,3,2,1,0:T(8,128)(2,1)S(1)}, bf16[1,1,4,16,4096]{4,3,2,1,0:T(8,128)(2,1)S(1)}, u32[]{:S(2)}, u32[]{:S(2)}) collective-permute-start(bf16[1,1,4,16,4096]{4,3,2,1,0:T(8,128)(2,1)S(1)} %add_convert_fusion.19), channel_id=1, source_target_pairs={{0,8},{8,0},{1,9},{9,1},{2,10},{10,2},{3,11},{11,3},{4,12},{12,4},... | collective-permute-start | bytes 1572872 | tf_op jit(solution)/shard_map/ppermute | solution.py:741
  593.8 26.3 %collective-permute-start.34 = (bf16[1,1,4,16,4096]{4,3,2,1,0:T(8,128)(2,1)S(1)}, bf16[1,1,4,16,4096]{4,3,2,1,0:T(8,128)(2,1)S(1)}, u32[]{:S(2)}, u32[]{:S(2)}) collective-permute-start(bf16[1,1,4,16,4096]{4,3,2,1,0:T(8,128)(2,1)S(1)} %add_convert_fusion.22), channel_id=1, source_target_pairs={{0,16},{16,0},{1,17},{17,1},{2,18},{18,2},{3,19},{19,3},{4,20},{20... | collective-permute-start | bytes 1572872 | tf_op jit(solution)/shard_map/ppermute | solution.py:741
  621.2 20.3 %collective-permute-start.38 = (bf16[32,4096]{1,0:T(8,128)(2,1)S(1)}, bf16[32,4096]{1,0:T(8,128)(2,1)S(1)}, u32[]{:S(2)}, u32[]{:S(2)}) collective-permute-start(bf16[32,4096]{1,0:T(8,128)(2,1)S(1)} %get-tuple-element.221), channel_id=1, source_target_pairs={{0,3},{1,0},{2,1},{3,2},{4,7},{5,4},{6,5},{7,6},{8,11},{9,8},{10,9... | collective-permute-start | bytes 786440 | tf_op jit(solution)/shard_map/ppermute | solution.py:760
  624.3 24.6 %collective-permute-start.39 = (bf16[32,4096]{1,0:T(8,128)(2,1)S(1)}, bf16[32,4096]{1,0:T(8,128)(2,1)S(1)}, u32[]{:S(2)}, u32[]{:S(2)}) collective-permute-start(bf16[32,4096]{1,0:T(8,128)(2,1)S(1)} %get-tuple-element.222), channel_id=1, source_target_pairs={{0,2},{1,3},{2,0},{3,1},{4,6},{5,7},{6,4},{7,5},{8,10},{9,11},{10,... | collective-permute-start | bytes 786440 | tf_op jit(solution)/shard_map/ppermute | solution.py:760
  626.2 24.2 %collective-permute-start.45 = (bf16[128,1024]{1,0:T(8,128)(2,1)S(1)}, bf16[128,1024]{1,0:T(8,128)(2,1)S(1)}, u32[]{:S(2)}, u32[]{:S(2)}) collective-permute-start(bf16[128,1024]{1,0:T(8,128)(2,1)S(1)} %get-tuple-element.217), channel_id=1, source_target_pairs={{0,1},{1,2},{2,3},{3,0},{4,5},{5,6},{6,7},{7,4},{8,9},{9,10},{10,1... | collective-permute-start | bytes 786440 | tf_op jit(solution)/shard_map/ppermute | solution.py:760
  627.0 23.4 %collective-permute-start.46 = (bf16[128,1024]{1,0:T(8,128)(2,1)S(1)}, bf16[128,1024]{1,0:T(8,128)(2,1)S(1)}, u32[]{:S(2)}, u32[]{:S(2)}) collective-permute-start(bf16[128,1024]{1,0:T(8,128)(2,1)S(1)} %get-tuple-element.218), channel_id=1, source_target_pairs={{0,3},{1,0},{2,1},{3,2},{4,7},{5,4},{6,5},{7,6},{8,11},{9,8},{10,9... | collective-permute-start | bytes 786440 | tf_op jit(solution)/shard_map/ppermute | solution.py:760
  631.5 23.0 %collective-permute-start.47 = (bf16[128,1024]{1,0:T(8,128)(2,1)S(1)}, bf16[128,1024]{1,0:T(8,128)(2,1)S(1)}, u32[]{:S(2)}, u32[]{:S(2)}) collective-permute-start(bf16[128,1024]{1,0:T(8,128)(2,1)S(1)} %get-tuple-element.219), channel_id=1, source_target_pairs={{0,2},{1,3},{2,0},{3,1},{4,6},{5,7},{6,4},{7,5},{8,10},{9,11},{10,... | collective-permute-start | bytes 786440 | tf_op jit(solution)/shard_map/ppermute | solution.py:760
  (90 other events, 1128.0 us)
Sparse Core Ops, SparseCore 0:
  11.4 119.9 all-gather.4
  134.9 113.0 all-gather.6

commit v2 on v1

v2 whole, which is shorter than its diff:
```python
import functools
import math

import jax
import jax.numpy as jnp
from jax import lax
from jax.experimental import pallas as pl
from jax.experimental.pallas import tpu as pltpu
from jax.sharding import Mesh
from jax.sharding import PartitionSpec as P

HD = 64
ADAM_STEP = 4

eps_norm = 1e-05
clip_limit = 1.0
learn_rate = 0.05
beta_first = 0.9
beta_second = 0.999
eps_adam = 1e-08
weight_decay = 0.1

BF = jnp.bfloat16
F32 = jnp.float32
ALL = ("y", "x", "c", "z")
TILE = 256
KEY_CHUNK = 256
VEC_ROWS = 17
MIB = 1024 * 1024


def dot(left, right):
    return jnp.dot(left, right, preferred_element_type=F32)


def dot_tn(left, right):
    return lax.dot_general(left, right, (((0,), (0,)), ((), ())), preferred_element_type=F32)


def dot_nt(left, right):
    return lax.dot_general(left, right, (((1,), (1,)), ((), ())), preferred_element_type=F32)


def params(limit=60):
    return pltpu.CompilerParams(vmem_limit_bytes=limit * MIB)


def vmem():
    return pl.BlockSpec(memory_space=pltpu.VMEM)


def hbm():
    return pl.BlockSpec(memory_space=pltpu.HBM)


def smem():
    return pl.BlockSpec(memory_space=pltpu.SMEM)


def shape(dims, dtype):
    return jax.ShapeDtypeStruct(tuple(dims), dtype)


def cost(flops, nbytes):
    return pl.CostEstimate(flops=int(flops), bytes_accessed=int(nbytes), transcendentals=0)


class Pack:
    def __init__(self, array, base=0):
        self.array, self.base = array, base


def weight_start(place_ref, pack, row, buf, sem):
    lines = pl.ds(pack.base + row, buf.shape[1])
    pltpu.make_async_copy(pack.array.at[:, lines, :], buf, sem).start()


def call(kernel, packs, args, **settings):
    first, last = len(args), len(args) + len(packs)

    def body(*refs):
        held = [Pack(ref, p.base) for ref, p in zip(refs[first:last], packs)]
        kernel(*refs[:first], *held, *refs[last:])

    specs = settings.pop("in_specs") + [hbm()] * len(packs)
    return pl.pallas_call(body, in_specs=specs, **settings)(*args, *[p.array for p in packs])


def weight_wait(buf, sem):
    pltpu.make_async_copy(buf, buf, sem).wait()


def times(act_ref, buf, put):
    depth = buf.shape[0] * buf.shape[1]

    @pl.loop(0, buf.shape[2] // TILE)
    def _(n):
        start = pl.multiple_of(n * TILE, TILE)
        put(start, dot(act_ref[...], buf[:, :, pl.ds(start, TILE)].reshape(depth, TILE)))


def times_t(act_ref, buf, put):
    per = TILE // buf.shape[1]

    @pl.loop(0, buf.shape[0] // per)
    def _(n):
        start = pl.multiple_of(n * TILE, TILE)
        rows = buf[pl.ds(n * per, per)].reshape(TILE, buf.shape[2])
        put(start, dot_nt(act_ref[...], rows))


def grad_weight(act_ref, grad_ref, out):
    @pl.loop(0, 4)
    def _(n):
        start = pl.multiple_of(n * TILE, TILE)
        tile = dot_tn(act_ref[:, pl.ds(start, TILE)], grad_ref[...])
        out[pl.ds(2 * n, 2)] = tile.astype(BF).reshape((2,) + out.shape[1:])


def block_copies(sel, grad, keep, send, row, sems):
    out = []
    for j in range(8):
        across, plane = j // 4, j % 4
        block = jnp.bitwise_xor(sel, plane * 2 + across)
        target = (send if across else keep).at[plane, :, pl.ds(row, grad.shape[2]), :]
        out.append(pltpu.make_async_copy(grad.at[block], target, sems.at[j]))
    return out


def start_all(copies):
    for one in copies:
        one.start()


def wait_all(copies):
    for one in copies:
        one.wait()


def row_chunks(count, size=64):
    return [slice(a, min(a + size, count)) for a in range(0, count, size)]


def normalise(values):
    centered = values - jnp.mean(values, axis=-1, keepdims=True)
    inv = lax.rsqrt(jnp.mean(centered * centered, axis=-1, keepdims=True) + eps_norm)
    return centered * inv, inv


def norm_into(src, gain, shift, out_ref):
    for rows in row_chunks(src.shape[0]):
        normed, _ = normalise(src[rows, :].astype(F32))
        out_ref[rows, :] = (normed * gain + shift).astype(BF)


def norm_grad(src, grad_ref, gain, put):
    gain_sum = jnp.zeros((1, src.shape[1]), F32)
    shift_sum = jnp.zeros((1, src.shape[1]), F32)
    for rows in row_chunks(src.shape[0]):
        normed, inv = normalise(src[rows, :].astype(F32))
        grad = grad_ref[rows, :]
        gain_sum += jnp.sum(grad * normed, axis=0, keepdims=True)
        shift_sum += jnp.sum(grad, axis=0, keepdims=True)
        scaled = grad * gain
        mean_one = jnp.mean(scaled, axis=-1, keepdims=True)
        mean_two = jnp.mean(scaled * normed, axis=-1, keepdims=True)
        put(rows, inv * (scaled - mean_one - normed * mean_two))
    return gain_sum, shift_sum


def column_sum(ref):
    total = jnp.zeros((1, ref.shape[1]), F32)
    for rows in row_chunks(ref.shape[0], 128):
        total += jnp.sum(ref[rows, :].astype(F32), axis=0, keepdims=True)
    return total


def self_in_kernel(place_ref, x_ref, vec_ref, one, two, a_ref, q_ref, k_ref, v_ref, bufs, sems):
    weight_start(place_ref, one, 0, bufs.at[0], sems.at[0])
    weight_start(place_ref, one, 32, bufs.at[1], sems.at[1])
    weight_start(place_ref, two, 0, bufs.at[2], sems.at[2])
    norm_into(x_ref, vec_ref[0:1, :], vec_ref[1:2, :], a_ref)
    for n, (out, bias) in enumerate(((q_ref, 6), (k_ref, None), (v_ref, 7))):
        weight_wait(bufs.at[n], sems.at[n])

        def put(start, value, out=out, bias=bias):
            if bias is not None:
                value = value + vec_ref[bias : bias + 1, pl.ds(start, TILE)]
            out[:, pl.ds(start, TILE)] = value.astype(BF)

        times(a_ref, bufs.at[n], put)


def self_in(place, x, vec, packs):
    rows, width = x.shape
    full = shape((rows, width), BF)
    return call(
        self_in_kernel,
        packs,
        [place, x, vec],
        out_shape=[full] * 4,
        in_specs=[smem(), vmem(), vmem()],
        out_specs=[vmem()] * 4,
        scratch_shapes=[pltpu.VMEM((3, 32, 32, width), BF), pltpu.SemaphoreType.DMA((3,))],
        compiler_params=params(48),
        cost_estimate=cost(6 * rows * width * width, 10 * MIB),
        name="self_in",
    )


def masked_pair(value):
    lane = lax.broadcasted_iota(jnp.int32, value.shape, 1)
    zero = jnp.zeros_like(value)
    return jnp.concatenate([jnp.where(lane < HD, value, zero), jnp.where(lane < HD, zero, value)], axis=0)


def pair_back(both, rows):
    line = lax.broadcasted_iota(jnp.int32, (2 * HD, rows), 0)
    return jnp.where(line < HD, both[:, :rows], both[:, rows:]).T


def key_chunks(count):
    return [(a, min(a + KEY_CHUNK, count)) for a in range(0, count, KEY_CHUNK)]


def exclude(scores, start, rows, causal, valid):
    key = lax.broadcasted_iota(jnp.int32, scores.shape, 0) + start
    if causal:
        query = lax.broadcasted_iota(jnp.int32, scores.shape, 1)
        query = jnp.where(query >= rows, query - rows, query)
        return jnp.where(key <= query, scores, -1e30)
    if start + scores.shape[0] > valid:
        return jnp.where(key < valid, scores, -1e30)
    return scores


def attend_kernel(causal, valid, q_ref, k_ref, v_ref, o_ref, lse_ref, top_ref, held):
    rows = q_ref.shape[0]
    query = masked_pair(q_ref[...] * jnp.asarray(HD**-0.5, BF))
    top = jnp.full((1, 2 * rows), -1e30, F32)
    for a, b in key_chunks(k_ref.shape[0]):
        scores = exclude(dot_nt(k_ref[a:b, :], query), a, rows, causal, valid)
        held[a:b, :] = scores
        top = jnp.maximum(top, jnp.max(scores, axis=0, keepdims=True))
    total = jnp.zeros((1, 2 * rows), F32)
    mixed = jnp.zeros((2 * HD, 2 * rows), F32)
    for a, b in key_chunks(k_ref.shape[0]):
        probs = jnp.exp(held[a:b, :] - top)
        total += jnp.sum(probs, axis=0, keepdims=True)
        mixed += dot_tn(v_ref[a:b, :], probs.astype(BF))
    o_ref[...] = pair_back(mixed * (1.0 / total), rows).astype(BF)
    lane = lax.broadcasted_iota(jnp.int32, (1, 2 * HD), 1)
    first, second = (jnp.max(part, axis=1, keepdims=True) for part in (top[:, :rows], top[:, rows:]))
    top_ref[0] = jnp.where(lane == 0, first, second)
    lse_ref[0] = top + jnp.log(total)


def attend(query, key, value, causal, valid):
    rows, width = query.shape
    keys = key.shape[0]
    pairs = width // (2 * HD)

    def column(count):
        return pl.BlockSpec((count, 2 * HD), lambda h: (0, h))

    line = pl.BlockSpec((1, 1, 2 * rows), lambda h: (h, 0, 0))
    return pl.pallas_call(
        functools.partial(attend_kernel, causal, valid),
        grid=(pairs,),
        out_shape=[shape((rows, width), BF), shape((pairs, 1, 2 * rows), F32), shape((pairs, 1, 2 * HD), F32)],
        in_specs=[column(rows), column(keys), column(keys)],
        out_specs=[column(rows), line, pl.BlockSpec((1, 1, 2 * HD), lambda h: (h, 0, 0))],
        scratch_shapes=[pltpu.VMEM((keys, 2 * rows), F32)],
        compiler_params=params(48),
        cost_estimate=cost(16 * rows * keys * width, 4 * keys * width),
        name="attend_causal" if causal else "attend",
    )(query, key, value)


def self_out_kernel(place_ref, o_ref, x_ref, vec_ref, one, two, x1_ref, a_ref, q_ref, bufs, sems):
    weight_start(place_ref, two, 32, bufs.at[0], sems.at[0])
    weight_start(place_ref, one, 32, bufs.at[1], sems.at[1])
    weight_wait(bufs.at[0], sems.at[0])

    def put_residual(start, value):
        cols = pl.ds(start, TILE)
        x1_ref[:, cols] = x_ref[:, cols].astype(F32) + (value + vec_ref[8:9, cols])

    times(o_ref, bufs.at[0], put_residual)
    norm_into(x1_ref, vec_ref[2:3, :], vec_ref[3:4, :], a_ref)
    weight_wait(bufs.at[1], sems.at[1])

    def put_query(start, value):
        cols = pl.ds(start, TILE)
        q_ref[:, cols] = (value + vec_ref[9:10, cols]).astype(BF)

    times(a_ref, bufs.at[1], put_query)


def self_out(place, mixed, x, vec, packs):
    rows, width = x.shape
    return call(
        self_out_kernel,
        packs,
        [place, mixed, x, vec],
        out_shape=[shape((rows, width), F32), shape((rows, width), BF), shape((rows, width), BF)],
        in_specs=[smem()] + [vmem()] * 3,
        out_specs=[vmem()] * 3,
        scratch_shapes=[pltpu.VMEM((2, 32, 32, width), BF), pltpu.SemaphoreType.DMA((2,))],
        compiler_params=params(48),
        cost_estimate=cost(4 * rows * width * width, 10 * MIB),
        name="self_out",
    )


def cross_in_kernel(place_ref, e_ref, vec_ref, one, two, k_ref, v_ref, bufs, sems):
    for n, part in enumerate((one, two)):
        weight_start(place_ref, part, 0, bufs.at[n], sems.at[n])
    for n, (out, bias) in enumerate(((k_ref, None), (v_ref, 10))):
        weight_wait(bufs.at[n], sems.at[n])

        def put(start, value, out=out, bias=bias):
            if bias is not None:
                value = value + vec_ref[bias : bias + 1, pl.ds(start, TILE)]
            out[:, pl.ds(start, TILE)] = value.astype(BF)

        times(e_ref, bufs.at[n], put)


def cross_in(place, enc, vec, packs):
    frames, width = enc.shape
    return call(
        cross_in_kernel,
        packs,
        [place, enc, vec],
        out_shape=[shape((frames, width), BF)] * 2,
        in_specs=[smem()] + [vmem()] * 2,
        out_specs=[vmem()] * 2,
        scratch_shapes=[pltpu.VMEM((2, 32, 32, width), BF), pltpu.SemaphoreType.DMA((2,))],
        compiler_params=params(48),
        cost_estimate=cost(4 * frames * width * width, 14 * MIB),
        name="cross_in",
    )


def cross_out_kernel(place_ref, o_ref, x1_ref, vec_ref, two, x2_ref, a_ref, buf, sem):
    weight_start(place_ref, two, 32, buf, sem)
    weight_wait(buf, sem)

    def put(start, value):
        cols = pl.ds(start, TILE)
        x2_ref[:, cols] = x1_ref[:, cols] + (value + vec_ref[11:12, cols])

    times(o_ref, buf, put)
    norm_into(x2_ref, vec_ref[4:5, :], vec_ref[5:6, :], a_ref)


def cross_out(place, mixed, x1, vec, packs):
    rows, width = x1.shape
    return call(
        cross_out_kernel,
        packs,
        [place, mixed, x1, vec],
        out_shape=[shape((rows, width), F32), shape((rows, width), BF)],
        in_specs=[smem()] + [vmem()] * 3,
        out_specs=[vmem()] * 2,
        scratch_shapes=[pltpu.VMEM((32, 32, width), BF), pltpu.SemaphoreType.DMA],
        compiler_params=params(48),
        cost_estimate=cost(2 * rows * width * width, 8 * MIB),
        name="cross_out",
    )


def whole(dims):
    return pl.BlockSpec(dims, lambda n: (0,) * len(dims))


def feed_kernel(
    a_ref, x2_ref, e_ref, vec_ref, bias_ref, w1_ref, w2_ref, out_ref, df_ref, gb1_ref, gb2_ref, grad_ref, total
):
    step = pl.program_id(0)
    wide = w1_ref.shape[2]
    depth = a_ref.shape[1]

    @pl.when(step == 0)
    def _():
        total[...] = x2_ref[...] + vec_ref[12:13, :]
        gb2_ref[...] = column_sum(e_ref)

    w2 = w2_ref[...].reshape(wide, depth)
    pre = dot(a_ref[...], w1_ref[...].reshape(depth, wide)) + bias_ref[0]
    cdf = 0.5 * (1.0 + lax.erf(pre * math.sqrt(0.5)))
    act = (pre * cdf).astype(BF)
    slope = cdf + pre * (jnp.exp(-0.5 * (pre * pre)) * (1.0 / math.sqrt(2.0 * math.pi)))
    grad_ref[0] = dot_tn(act, e_ref[...]).astype(BF).reshape(grad_ref.shape[1:])
    grad_pre = (dot_nt(e_ref[...], w2) * slope).astype(BF)
    df_ref[...] = grad_pre
    gb1_ref[0] = jnp.sum(grad_pre.astype(F32), axis=0, keepdims=True)
    total[...] += dot(act, w2)

    @pl.when(step == pl.num_programs(0) - 1)
    def _():
        out_ref[...] = total[...].astype(BF)


def feed(a3, x2, cot, vec, pack):
    rows, width = a3.shape
    hidden = 4 * width
    wide = hidden // 8
    bias = vec[13:].reshape(8, 1, wide)
    return pl.pallas_call(
        feed_kernel,
        grid=(8,),
        out_shape=[
            shape((rows, width), BF), shape((rows, hidden), BF), shape((8, 1, wide), F32), shape((1, width), F32),
            shape((8, 4, 256, width), BF),
        ],
        in_specs=[
            whole((rows, width)),
            whole((rows, width)),
            whole((rows, width)),
            whole(vec.shape),
            pl.BlockSpec((1, 1, wide), lambda n: (n, 0, 0)),
            pl.BlockSpec((32, 32, wide), lambda n: (0, n // 2, n % 2)),
            pl.BlockSpec((4, 128, width), lambda n: (n, 1, 0)),
        ],
        out_specs=[
            whole((rows, width)),
            pl.BlockSpec((rows, wide), lambda n: (0, n)),
            pl.BlockSpec((1, 1, wide), lambda n: (n, 0, 0)),
            whole((1, width)),
            pl.BlockSpec((1, 4, 128, width), lambda n: (n, 0, 1, 0)),
        ],
        scratch_shapes=[pltpu.VMEM((rows, width), F32)],
        compiler_params=params(48),
        cost_estimate=cost(8 * rows * width * hidden, 30 * MIB),
        name="feed",
    )(a3, x2, cot, vec, bias, pack, pack)


def feed_grad_kernel(a_ref, df_ref, w1_ref, grad_in, da_ref, grad_ref):
    wide = w1_ref.shape[2]
    grad_pre = df_ref[...]
    grad_ref[...] = dot_tn(a_ref[...], grad_pre).astype(BF).reshape(grad_ref.shape)

    @pl.when(pl.program_id(0) == 0)
    def _():
        da_ref[...] = jnp.zeros_like(da_ref)

    da_ref[...] += dot_nt(grad_pre, w1_ref[...].reshape(a_ref.shape[1], wide))


def feed_grad(a3, df, grad, pack):
    rows, width = a3.shape
    hidden = df.shape[1]
    wide = hidden // 8
    return pl.pallas_call(
        feed_grad_kernel,
        grid=(8,),
        out_shape=[shape((rows, width), F32), shape(grad.shape, BF)],
        in_specs=[
            whole((rows, width)),
            pl.BlockSpec((rows, wide), lambda n: (0, n)),
            pl.BlockSpec((32, 32, wide), lambda n: (0, n // 2, n % 2)),
            hbm(),
        ],
        out_specs=[
            whole((rows, width)),
            pl.BlockSpec((8, 4, 32, wide), lambda n: (0, 0, n // 2, n % 2)),
        ],
        input_output_aliases={3: 1},
        compiler_params=params(48),
        cost_estimate=cost(4 * rows * width * hidden, 22 * MIB),
        name="feed_grad",
    )(a3, df, pack, grad)


def cross_out_grad_kernel(
    place_ref, da_ref, x2_ref, cot_ref, o_ref, vec_ref, two,
    dx_ref, do_ref, sums_ref, keep, send, buf, e_ref, grad, sem, sems,
):
    weight_start(place_ref, two, 32, buf, sem)

    def put(rows, value):
        total = cot_ref[rows, :].astype(F32) + value
        dx_ref[rows, :] = total
        e_ref[rows, :] = total.astype(BF)

    gain, shift = norm_grad(x2_ref, da_ref, vec_ref[4:5, :], put)
    sums_ref[0:1, :] = gain
    sums_ref[1:2, :] = shift
    sums_ref[2:3, :] = column_sum(e_ref)
    grad_weight(o_ref, e_ref, grad)
    out = block_copies(place_ref[0], grad, keep, send, 64, sems)
    start_all(out)
    weight_wait(buf, sem)

    def put_mixed(start, value):
        do_ref[:, pl.ds(start, TILE)] = value.astype(BF)

    times_t(e_ref, buf, put_mixed)
    wait_all(out)


def cross_out_grad(place, da3, x2, cot, mixed, vec, packs):
    rows, width = x2.shape
    blocks = shape((4, 4, 96, width), BF)
    return call(
        cross_out_grad_kernel,
        packs,
        [place, da3, x2, cot, mixed, vec],
        out_shape=[
            shape((rows, width), F32), shape((rows, width), BF), shape((3, width), F32), blocks, blocks,
        ],
        in_specs=[smem()] + [vmem()] * 5,
        out_specs=[vmem()] * 3 + [hbm()] * 2,
        scratch_shapes=[
            pltpu.VMEM((32, 32, width), BF), pltpu.VMEM((rows, width), BF), pltpu.VMEM((8, 4, 32, width), BF),
            pltpu.SemaphoreType.DMA, pltpu.SemaphoreType.DMA((8,)),
        ],
        compiler_params=params(48),
        cost_estimate=cost(4 * rows * width * width, 14 * MIB),
        name="cross_out_grad",
    )


def attend_grad_kernel(causal, valid, q_ref, k_ref, v_ref, o_ref, do_ref, lse_ref, *refs):
    dq_ref, dk_ref, dv_ref = refs[-3:]
    rows = q_ref.shape[0]
    scale = jnp.asarray(HD**-0.5, BF)
    query = masked_pair(q_ref[...] * scale)
    grad_out = masked_pair(do_ref[...])
    product = (do_ref[...].astype(F32) * o_ref[...].astype(F32)).T
    delta = jnp.concatenate(
        [jnp.sum(product[:HD], axis=0, keepdims=True), jnp.sum(product[HD:], axis=0, keepdims=True)], axis=1
    )
    lse = lse_ref[0]
    grad_query = jnp.zeros((2 * HD, 2 * rows), F32)
    for a, b in key_chunks(k_ref.shape[0]):
        key = k_ref[a:b, :]
        scores = exclude(dot_nt(key, query), a, rows, causal, valid)
        probs = jnp.exp(scores - lse)
        grad_probs = dot_nt(v_ref[a:b, :], grad_out)
        grad_scores = (probs * (grad_probs - delta)).astype(BF)
        dv_ref[a:b, :] = dot(probs.astype(BF), grad_out).astype(BF)
        dk_ref[a:b, :] = dot(grad_scores, query).astype(BF)
        grad_query += dot_tn(key, grad_scores)
    dq_ref[...] = (pair_back(grad_query, rows) * HD**-0.5).astype(BF)


def attend_grad(query, key, value, mixed, grad_mixed, lse, causal, valid, part=(0, 1), before=()):
    rows, width = query.shape
    keys = key.shape[0]
    pairs = width // (2 * HD) // part[1]
    skip = part[0] * pairs

    def column(count):
        return pl.BlockSpec((count, 2 * HD), lambda h: (0, h + skip))

    line = pl.BlockSpec((1, 1, 2 * rows), lambda h: (h + skip, 0, 0))
    return pl.pallas_call(
        functools.partial(attend_grad_kernel, causal, valid),
        grid=(pairs,),
        out_shape=[shape((rows, width), BF)] + [shape((keys, width), BF)] * 2,
        in_specs=[column(rows), column(keys), column(keys), column(rows), column(rows), line] + [hbm()] * len(before),
        out_specs=[column(rows), column(keys), column(keys)],
        input_output_aliases={6 + n: n for n in range(len(before))},
        compiler_params=params(),
        cost_estimate=cost(40 * rows * keys * width // part[1], 8 * keys * width),
        name="attend_causal_grad" if causal else "attend_grad",
    )(query, key, value, mixed, grad_mixed, lse, *before)


def cross_query_grad_kernel(
    place_ref, a_ref, dq_ref, x1_ref, dx2_ref, o_ref, vec_ref, keep_in, send_in, one, two,
    dx_ref, do_ref, sums_ref, keep, send, bufs, da_ref, e_ref, grads, sem, sems,
):
    for n, part in enumerate((one, two)):
        weight_start(place_ref, part, 32, bufs.at[n], sem.at[n])
    place = place_ref[0]
    grad_weight(a_ref, dq_ref, grads.at[0])
    out = block_copies(place, grads.at[0], keep, send, 32, sems.at[0])
    start_all(out)
    sums_ref[0:1, :] = column_sum(dq_ref)
    weight_wait(bufs.at[0], sem.at[0])

    def put_act(start, value):
        da_ref[:, pl.ds(start, TILE)] = value

    times_t(dq_ref, bufs.at[0], put_act)

    def put(rows, value):
        total = dx2_ref[rows, :] + value
        dx_ref[rows, :] = total
        e_ref[rows, :] = total.astype(BF)

    gain, shift = norm_grad(x1_ref, da_ref, vec_ref[2:3, :], put)
    sums_ref[1:2, :] = gain
    sums_ref[2:3, :] = shift
    sums_ref[3:4, :] = column_sum(e_ref)
    grad_weight(o_ref, e_ref, grads.at[1])
    more = block_copies(place, grads.at[1], keep, send, 0, sems.at[1])
    start_all(more)
    weight_wait(bufs.at[1], sem.at[1])

    def put_mixed(start, value):
        do_ref[:, pl.ds(start, TILE)] = value.astype(BF)

    times_t(e_ref, bufs.at[1], put_mixed)
    wait_all(out)
    wait_all(more)


def cross_query_grad(place, a2, dq2, x1, dx2, mixed, vec, keep, send, packs):
    rows, width = x1.shape
    return call(
        cross_query_grad_kernel,
        packs,
        [place, a2, dq2, x1, dx2, mixed, vec, keep, send],
        out_shape=[
            shape((rows, width), F32), shape((rows, width), BF), shape((4, width), F32),
            shape(keep.shape, BF), shape(send.shape, BF),
        ],
        in_specs=[smem()] + [vmem()] * 6 + [hbm()] * 2,
        out_specs=[vmem()] * 3 + [hbm()] * 2,
        scratch_shapes=[
            pltpu.VMEM((2, 32, 32, width), BF), pltpu.VMEM((rows, width), F32), pltpu.VMEM((rows, width), BF),
            pltpu.VMEM((2, 8, 4, 32, width), BF), pltpu.SemaphoreType.DMA((2,)), pltpu.SemaphoreType.DMA((2, 8)),
        ],
        input_output_aliases={7: 3, 8: 4},
        compiler_params=params(),
        cost_estimate=cost(8 * rows * width * width, 20 * MIB),
        name="cross_query_grad",
    )


def cross_key_grad_kernel(place_ref, e_ref, dk_ref, dv_ref, keep_in, send_in, sums_ref, keep, send, grads, sems):
    copies = []
    for n, ref in enumerate((dk_ref, dv_ref)):
        grad_weight(e_ref, ref, grads.at[n])
        out = block_copies(place_ref[0], grads.at[n], keep, send, 96 + 32 * n, sems.at[n])
        start_all(out)
        copies += out
    sums_ref[...] = column_sum(dv_ref)
    wait_all(copies)


def cross_key_grad(place, enc, dk2, dv2, keep, send):
    frames, width = enc.shape
    return pl.pallas_call(
        cross_key_grad_kernel,
        out_shape=[shape((1, width), F32), shape(keep.shape, BF), shape(send.shape, BF)],
        in_specs=[smem()] + [vmem()] * 3 + [hbm()] * 2,
        input_output_aliases={4: 1, 5: 2},
        out_specs=[vmem()] + [hbm()] * 2,
        scratch_shapes=[pltpu.VMEM((2, 8, 4, 32, width), BF), pltpu.SemaphoreType.DMA((2, 8))],
        compiler_params=params(),
        cost_estimate=cost(4 * frames * width * width, 14 * MIB),
        name="cross_key_grad",
    )(place, enc, dk2, dv2, keep, send)


def encoder_grad_kernel(frames, place_ref, dk_ref, dv_ref, one, two, out_ref, bufs, sems):
    for n, part in enumerate((one, two)):
        weight_start(place_ref, part, 0, bufs.at[n], sems.at[n])
    for n in range(2):
        weight_wait(bufs.at[n], sems.at[n])
    width = dk_ref.shape[1]
    per = TILE // 32
    lines = width // 128

    @pl.loop(0, width // TILE)
    def _(n):
        total = dot_nt(dk_ref[...], bufs[0, pl.ds(n * per, per)].reshape(TILE, width))
        total += dot_nt(dv_ref[...], bufs[1, pl.ds(n * per, per)].reshape(TILE, width))
        for side in range(TILE // 128):
            start = n * (TILE // 128) + side
            out_ref[pl.ds(start, frames, stride=lines), :] = total[:frames, side * 128 : (side + 1) * 128]


def encoder_grad(place, dk2, dv2, packs, frames):
    width = dk2.shape[1]
    return call(
        functools.partial(encoder_grad_kernel, frames),
        packs,
        [place, dk2, dv2],
        out_shape=shape((frames * (width // 128), 128), F32),
        in_specs=[smem()] + [vmem()] * 2,
        out_specs=vmem(),
        scratch_shapes=[pltpu.VMEM((2, 32, 32, width), BF), pltpu.SemaphoreType.DMA((2,))],
        compiler_params=params(),
        cost_estimate=cost(4 * frames * width * width, 16 * MIB),
        name="encoder_grad",
    )


def self_weight_grad_kernel(place_ref, a_ref, dq_ref, dk_ref, dv_ref, sums_ref, keep, send, grads, sems):
    out = []
    for n, ref in enumerate((dq_ref, dk_ref, dv_ref)):
        grad_weight(a_ref, ref, grads.at[n])
        more = block_copies(place_ref[0], grads.at[n], keep, send, 32 * n, sems.at[n])
        start_all(more)
        out += more
    sums_ref[0:1, :] = column_sum(dq_ref)
    sums_ref[1:2, :] = column_sum(dv_ref)
    wait_all(out)


def self_weight_grad(place, a1, dq1, dk1, dv1):
    rows, width = a1.shape
    blocks = shape((4, 4, 160, width), BF)
    return pl.pallas_call(
        self_weight_grad_kernel,
        out_shape=[shape((2, width), F32), blocks, blocks],
        in_specs=[smem()] + [vmem()] * 4,
        out_specs=[vmem()] + [hbm()] * 2,
        scratch_shapes=[pltpu.VMEM((3, 8, 4, 32, width), BF), pltpu.SemaphoreType.DMA((3, 8))],
        compiler_params=params(),
        cost_estimate=cost(6 * rows * width * width, 10 * MIB),
        name="self_weight_grad",
    )(place, a1, dq1, dk1, dv1)


def self_in_grad_kernel(
    place_ref, dq_ref, dk_ref, dv_ref, x_ref, dx1_ref, vec_ref, one, two, dx_ref, sums_ref, bufs, da_ref, sems
):
    weight_start(place_ref, one, 0, bufs.at[0], sems.at[0])
    weight_start(place_ref, one, 32, bufs.at[1], sems.at[1])
    weight_start(place_ref, two, 0, bufs.at[2], sems.at[2])
    for n, ref in enumerate((dq_ref, dk_ref, dv_ref)):
        weight_wait(bufs.at[n], sems.at[n])

        def put_act(start, value, n=n):
            if n:
                da_ref[:, pl.ds(start, TILE)] += value
            else:
                da_ref[:, pl.ds(start, TILE)] = value

        times_t(ref, bufs.at[n], put_act)

    def put(rows, value):
        dx_ref[rows, :] = dx1_ref[rows, :] + value

    gain, shift = norm_grad(x_ref, da_ref, vec_ref[0:1, :], put)
    sums_ref[0:1, :] = gain
    sums_ref[1:2, :] = shift


def self_in_grad(place, dq1, dk1, dv1, x, dx1, vec, packs):
    rows, width = x.shape
    return call(
        self_in_grad_kernel,
        packs,
        [place, dq1, dk1, dv1, x, dx1, vec],
        out_shape=[shape((rows, width), F32), shape((2, width), F32)],
        in_specs=[smem()] + [vmem()] * 6,
        out_specs=[vmem()] * 2,
        scratch_shapes=[
            pltpu.VMEM((3, 32, 32, width), BF), pltpu.VMEM((rows, width), F32), pltpu.SemaphoreType.DMA((3,)),
        ],
        compiler_params=params(),
        cost_estimate=cost(6 * rows * width * width, 14 * MIB),
        name="self_in_grad",
    )


SWAP = [(0, 1), (1, 0)]
MATRICES = ((0, 1), (2, 3), (5, 4), (6, 7))


class Unit:
    def __init__(self, chain):
        self.chain, self.result, self.moved = chain, None, None
        self.wanted = next(chain)

    def advance(self, arrived):
        try:
            self.wanted = self.chain.send(arrived)
        except StopIteration as stop:
            self.wanted, self.result = None, stop.value


def step(run=None, inputs=(), start=(), finish=()):
    start, finish = ([u for u in units if u is not None] for units in (start, finish))
    operands = [[value for value, _, _ in u.wanted] for u in start]
    inputs, operands = lax.optimization_barrier((tuple(inputs), operands))
    for u, values in zip(start, operands):
        u.moved = [lax.ppermute(v, axis, pairs) for v, (_, axis, pairs) in zip(values, u.wanted)]
    out = run(*inputs) if run else ()
    if finish:
        out, moved = lax.optimization_barrier((out, [u.moved for u in finish]))
        for u, values in zip(finish, moved):
            u.advance(values)
    return out


def turns():
    return [[(n, (n + k) % 4) for n in range(4)] for k in range(4)]


def add_rounded(left, right):
    return (left.astype(F32) + right.astype(F32)).astype(BF)


def add_kernel(plan, sources, place_ref, *refs):
    left, right = refs[:sources], refs[sources : 2 * sources]
    *outs, one, two, total, sems, out_sems = refs[2 * sources :]
    pieces = plan(place_ref)
    copies = [
        [
            pltpu.make_async_copy(side[source].at[index], held.at[n], sems.at[k, n])
            for k, (side, held) in enumerate(((left, one), (right, two)))
        ]
        for n, (source, index, _, _) in enumerate(pieces)
    ]
    for pair in copies:
        start_all(pair)
    away = []
    for n, (_, _, out, index) in enumerate(pieces):
        wait_all(copies[n])
        total[n] = add_rounded(one[n], two[n])
        away.append(pltpu.make_async_copy(total.at[n], outs[out].at[index], out_sems.at[n]))
        away[-1].start()
    wait_all(away)


def add_pieces(place, left, right, outs, piece, plan, count):
    held = pltpu.VMEM((count,) + piece, BF)
    return pl.pallas_call(
        functools.partial(add_kernel, plan, len(left)),
        out_shape=[shape(o, BF) for o in outs],
        in_specs=[smem()] + [hbm()] * (2 * len(left)),
        out_specs=[hbm()] * len(outs),
        scratch_shapes=[
            held, held, held, pltpu.SemaphoreType.DMA((2, count)), pltpu.SemaphoreType.DMA((count,)),
        ],
        compiler_params=params(),
        cost_estimate=cost(0, 6 * count * math.prod(piece)),
        name="add_pieces",
    )(place, *left, *right)


def turn_z(place_ref, k):
    return jnp.bitwise_and(place_ref[1] + k, 3)


def reduce_chain(place, keep, send):
    rows, columns = keep.shape[2:]
    half = rows // 2
    parts = [pl.ds(0, half), pl.ds(half, half)]
    (moved,) = yield [(send, "c", SWAP)]

    def plan_one(_):
        out = []
        for plane in (3, 1, 2, 0):
            y, x = plane // 2, plane % 2
            out.append((0, (plane, slice(None), parts[0]), 0 if x else 2, y))
            out.append((0, (plane, slice(None), parts[1]), 1 if y else 3, x))
        return out

    outs = [(2, 4, half, columns)] * 4
    one, two, *mine = add_pieces(place, [keep], [moved], outs, (4, half, columns), plan_one, 8)
    moved = yield [(one, "x", SWAP), (two, "y", SWAP)]

    def plan_two(_):
        return [(n, side, n if side else 2 + n, slice(None)) for side in (1, 0) for n in range(2)]

    outs = [(4, half, columns)] * 4
    one, two, *mine = add_pieces(place, mine, list(moved), outs, (4, half, columns), plan_two, 4)
    moved = yield [(one, "y", SWAP), (two, "x", SWAP)]

    def plan_three(place_ref):
        return [(n, turn_z(place_ref, k), k, parts[n]) for k in (2, 1, 3, 0) for n in range(2)]

    pieces = add_pieces(place, mine, list(moved), [(rows, columns)] * 4, (half, columns), plan_three, 8)
    moved = yield [(pieces[k], "z", turns()[k]) for k in (1, 3, 2)]
    return functools.reduce(jnp.add, [value.astype(F32) for value in moved], pieces[0].astype(F32))


def z_chain(both):
    here = lax.axis_index("z")

    def piece(k):
        return lax.dynamic_index_in_dim(both, lax.rem(here + k, 4), 0, keepdims=False)

    moved = yield [(piece(k), "z", turns()[k]) for k in (1, 3, 2)]
    return functools.reduce(jnp.add, [value.astype(F32) for value in moved], piece(0).astype(F32))


def reduce_plain(keep, send):
    count = lax.axis_size(ALL)
    rows, columns = keep.shape[2:]
    total = jnp.stack([keep, send], axis=1).reshape(32, rows, columns)
    many = rows // 32
    total = total.reshape(32, many, 32, columns).swapaxes(0, 1).reshape(many, 1024, columns)
    mine = lax.psum_scatter(total.astype(F32), ALL, scatter_dimension=1, tiled=True)
    return mine.reshape(many * (1024 // count), columns)


def reduce_feed_plain(grad):
    columns = grad.shape[3]
    grad1 = grad[:, :, :128].reshape(32, 4, 32, columns).swapaxes(1, 2).reshape(1024, 4 * columns)
    grad2 = grad[:, :, 128:].reshape(4096, columns)
    return [lax.psum_scatter(g.astype(F32), ALL, scatter_dimension=0, tiled=True) for g in (grad1, grad2)]


def table_chain(table):
    row = lax.broadcasted_iota(jnp.int32, table.shape, 0)

    def combine(left, right):
        return jnp.where(row < VEC_ROWS, left + right, jnp.maximum(left, right))

    for axis in ("c", "x", "y"):
        moved = yield [(table, axis, SWAP)]
        table = combine(table, moved[0])
    for pairs in ([(0, 1), (1, 0), (2, 3), (3, 2)], [(0, 2), (2, 0), (1, 3), (3, 1)]):
        moved = yield [(table, "z", pairs)]
        table = combine(table, moved[0])
    return table


def vector_table(pack, row, rows, shard_cols):
    table = pack[:, row, : rows * shard_cols].reshape(32, rows, shard_cols).swapaxes(0, 1)
    return table.reshape(rows, 32 * shard_cols).astype(F32)


def feed_shard(expand, contract):
    width = contract.shape[1]
    pieces = [expand[:, n * width : (n + 1) * width] for n in range(expand.shape[1] // width)]
    return jnp.concatenate(pieces + [contract], axis=0)


def gather_fast(attention, expand, contract, vectors):
    width = attention.shape[2]
    line = jnp.pad(vectors.reshape(1, -1), ((0, 15), (0, width - vectors.size)))
    shard = jnp.concatenate([attention[m] for group in MATRICES for m in group] + [line], axis=0)
    pack = lax.all_gather(shard, ALL, axis=0, tiled=False)
    pack_f = lax.all_gather(feed_shard(expand, contract), ALL, axis=0, tiled=False)
    return parts_of(pack), pack_f, vector_table(pack, 256, *vectors.shape)


def parts_of(pack):
    return [Pack(pack, 64 * n) for n in range(4)]


def gather_plain(attention, expand, contract, vectors):
    attention = lax.all_gather(attention, ALL, axis=1, tiled=True)
    expand = lax.all_gather(expand, ALL, axis=0, tiled=True)
    contract = lax.all_gather(contract, ALL, axis=0, tiled=True)
    vectors = lax.all_gather(vectors, ALL, axis=1, tiled=True)
    width = attention.shape[2]
    pack = jnp.concatenate([attention[m].reshape(32, 32, width) for group in MATRICES for m in group], axis=1)
    first = expand.reshape(32, 32, 4, width).swapaxes(1, 2).reshape(32, 128, width)
    pack_f = jnp.concatenate([first, contract.reshape(32, 128, width)], axis=1)
    return parts_of(pack), pack_f, vectors.astype(F32)


def adam_update(master, gradient, first, second, step_value, clip_scale):
    first_new = beta_first * first.astype(F32) + (1.0 - beta_first) * gradient
    second_new = beta_second * second + (1.0 - beta_second) * gradient * gradient
    direction = (
        first_new
        / (1.0 - beta_first**step_value)
        / (jnp.sqrt(second_new / (1.0 - beta_second**step_value)) + eps_adam)
    )
    master_new = (master - learn_rate * (direction + weight_decay * master)) * clip_scale
    return (first_new, second_new, master_new)


def table_kernel(sums1, bias1, sums2, sums3, sums_v, gb1, gb2, top1, top2, out):
    out[...] = jnp.zeros_like(out)
    rows = [
        sums1[0:1, :], sums1[1:2, :], sums2[1:2, :], sums2[2:3, :], sums3[0:1, :], sums3[1:2, :],
        bias1[0:1, :], bias1[1:2, :], sums2[3:4, :], sums2[0:1, :], sums_v[...], sums3[2:3, :], gb2[...],
    ]
    for n, row in enumerate(rows):
        out[n : n + 1, :] = row
    half = gb1.shape[2]
    for n in range(gb1.shape[0]):
        out[len(rows) + n // 2 : len(rows) + n // 2 + 1, n % 2 * half : (n % 2 + 1) * half] = gb1[n]
    for n, top in enumerate((top1, top2)):
        for pair in range(top.shape[0]):
            lanes = slice(pair * 2 * HD, (pair + 1) * 2 * HD)
            out[VEC_ROWS + n : VEC_ROWS + n + 1, lanes] = top[pair]


def vector_table_of(*pieces):
    width = pieces[0].shape[1]
    return pl.pallas_call(
        table_kernel,
        out_shape=shape((24, width), F32),
        in_specs=[vmem()] * len(pieces),
        out_specs=vmem(),
        compiler_params=params(),
        cost_estimate=cost(0, 200000),
        name="vector_table",
    )(*pieces)


def maxima_of(table):
    return table[VEC_ROWS : VEC_ROWS + 2].reshape(2, -1, 2 * HD)[:, :, :2].reshape(2, -1)


def sequence_plain(place, x, enc, frames, cot, vec, packs, pack_f):
    rows, width = x.shape
    one_a, one_b, two_a, two_b = packs
    a1, q1, k1, v1 = self_in(place, x, vec, [one_a, one_b])
    o1, lse1, top1 = attend(q1, k1, v1, True, rows)
    x1, a2, q2 = self_out(place, o1, x, vec, [two_a, one_b])
    k2, v2 = cross_in(place, enc, vec, [two_a, two_b])
    o2, lse2, top2 = attend(q2, k2, v2, False, frames)
    x2, a3 = cross_out(place, o2, x1, vec, [two_b])
    result, df, gb1, gb2, grad = feed(a3, x2, cot, vec, pack_f)
    da3, grad = feed_grad(a3, df, grad, pack_f)
    dx2, do2, sums3, keep1, send1 = cross_out_grad(place, da3, x2, cot, o2, vec, [two_b])
    dq2, dk2, dv2 = attend_grad(q2, k2, v2, o2, do2, lse2, False, frames)
    dx1, do1, sums2, keep1, send1 = cross_query_grad(place, a2, dq2, x1, dx2, o1, vec, keep1, send1, [two_a, one_b])
    dq1, dk1, dv1 = attend_grad(q1, k1, v1, o1, do1, lse1, True, rows)
    bias1, keep2, send2 = self_weight_grad(place, a1, dq1, dk1, dv1)
    sums_v, keep2, send2 = cross_key_grad(place, enc, dk2, dv2, keep2, send2)
    grad_input, sums1 = self_in_grad(place, dq1, dk1, dv1, x, dx1, vec, [one_a, one_b])
    grad_encoder = encoder_grad(place, dk2, dv2, [two_a, two_b], frames).reshape(frames, width)
    table = vector_table_of(sums1, bias1, sums2, sums3, sums_v, gb1, gb2, top1, top2)
    g_vectors, maxima = table[:VEC_ROWS], maxima_of(table)
    return result, grad_input, grad_encoder, g_vectors, maxima, [(grad,), (keep1, send1), (keep2, send2)]


def gradients_plain(inputs, encoder, cotangent, owned):
    packs, pack_f, vec = gather_plain(*owned)
    place = jnp.zeros((2,), jnp.int32)
    frames = encoder.shape[1]
    done = []
    for n in range(inputs.shape[0]):
        enc = pad_frames(encoder[n])
        done.append(sequence_plain(place, inputs[n], enc, frames, cotangent[n], vec, packs, pack_f))
    result, grad_input, grad_encoder = (jnp.stack([d[k] for d in done]) for k in range(3))
    g_vectors = functools.reduce(jnp.add, [d[3] for d in done])
    maxima = functools.reduce(jnp.maximum, [d[4] for d in done])
    both = done[0][5]
    for d in done[1:]:
        both = [tuple(add_rounded(a, b) for a, b in zip(p, q)) for p, q in zip(both, d[5])]
    sums = reduce_feed_plain(*both[0]) + [reduce_plain(*p) for p in both[1:]]
    g_vectors = lax.psum_scatter(g_vectors, ALL, scatter_dimension=1, tiled=True)
    return result, grad_input, grad_encoder, sums, g_vectors, lax.pmax(maxima, ALL)


def pad_frames(enc):
    return jnp.pad(enc, ((0, -enc.shape[0] % 16), (0, 0)))


def gradients_fast(inputs, encoder, cotangent, owned):
    attention, expand, contract, vectors = owned
    x, cot = inputs[0], cotangent[0]
    rows, width = x.shape
    frames = encoder.shape[1]
    place = jnp.stack([lax.axis_index(("y", "x", "c")), lax.axis_index("z")]).astype(jnp.int32)
    (one_a, one_b, two_a, two_b), pack_f, vec = gather_fast(*owned)
    enc = pad_frames(encoder[0])
    a1, q1, k1, v1 = self_in(place, x, vec, [one_a, one_b])
    o1, lse1, top1 = attend(q1, k1, v1, True, rows)
    x1, a2, q2 = self_out(place, o1, x, vec, [two_a, one_b])
    k2, v2 = cross_in(place, enc, vec, [two_a, two_b])
    o2, lse2, top2 = attend(q2, k2, v2, False, frames)
    x2, a3 = cross_out(place, o2, x1, vec, [two_b])

    result, df, gb1, gb2, grad = feed(a3, x2, cot, vec, pack_f)
    da3, grad = feed_grad(a3, df, grad, pack_f)
    rf = lax.psum_scatter(grad, ("y", "x", "c"), scatter_dimension=0, tiled=True)[0]
    rf = lax.psum_scatter(rf, "z", scatter_dimension=0, tiled=True)[0].astype(F32)
    dx2, do2, sums3, keep, send = cross_out_grad(place, da3, x2, cot, o2, vec, [two_b])
    dq2, dk2, dv2 = attend_grad(q2, k2, v2, o2, do2, lse2, False, frames)
    dx1, do1, sums2, keep, send = cross_query_grad(place, a2, dq2, x1, dx2, o1, vec, keep, send, [two_a, one_b])
    r1 = Unit(reduce_chain(place, keep, send))
    dq1, dk1, dv1 = step(
        lambda do1: attend_grad(q1, k1, v1, o1, do1, lse1, True, rows), [do1], start=[r1], finish=[r1]
    )
    bias1, keep, send = step(
        lambda dq1, dk1, dv1: self_weight_grad(place, a1, dq1, dk1, dv1), [dq1, dk1, dv1], start=[r1]
    )
    sums_v, keep, send = step(
        lambda dk2: cross_key_grad(place, enc, dk2, dv2, keep, send), [dk2], finish=[r1]
    )
    r2 = Unit(reduce_chain(place, keep, send))
    grad_input, sums1 = step(
        lambda dq1, dk1, dv1: self_in_grad(place, dq1, dk1, dv1, x, dx1, vec, [one_a, one_b]),
        [dq1, dk1, dv1],
        start=[r1, r2],
        finish=[r1, r2],
    )
    table = Unit(table_chain(vector_table_of(sums1, bias1, sums2, sums3, sums_v, gb1, gb2, top1, top2)))
    step(start=[table], finish=[table])
    grad_encoder = step(
        lambda dk2: encoder_grad(place, dk2, dv2, [two_a, two_b], frames),
        [dk2],
        start=[r1, r2],
        finish=[r1, r2],
    )
    step(start=[r2, table], finish=[r2, table])
    step(start=[r2, table], finish=[r2, table])
    step(start=[table], finish=[table])
    step(start=[table], finish=[table])
    total = table.result
    shard_cols = vectors.shape[1]
    g_vectors = lax.dynamic_slice_in_dim(total[:VEC_ROWS], lax.axis_index(ALL) * shard_cols, shard_cols, 1)
    maxima = maxima_of(total)
    grad_encoder = grad_encoder.reshape(1, frames, width)
    g_expand = rf[:128].reshape(4, 32, width).swapaxes(0, 1).reshape(32, 4 * width)
    sums = [g_expand, rf[128:], r1.result, r2.result]
    return result[None], grad_input[None], grad_encoder, sums, g_vectors, maxima


def local(
    fast,
    inputs,
    encoder,
    cotangent,
    attention_master,
    expand_master,
    contract_master,
    vectors_master,
    attention_first,
    expand_first,
    contract_first,
    vectors_first,
    attention_second,
    expand_second,
    contract_second,
    vectors_second,
):
    width = inputs.shape[2]
    owned = [m.astype(BF) for m in (attention_master, expand_master, contract_master, vectors_master)]
    compute = gradients_fast if fast and inputs.shape[0] == 1 else gradients_plain
    result, grad_input, grad_encoder, sums, g_vectors, maxima = compute(inputs, encoder, cotangent, owned)
    g_expand, g_contract = sums[:2]
    out_query, rest = (value.reshape(-1, attention_master.shape[1], width) for value in sums[2:])
    g_attention = jnp.concatenate([rest[:3], out_query[:2], rest[3:], out_query[2:]], axis=0)
    shard_cols = vectors_master.shape[1]
    first_col = lax.axis_index(ALL) * shard_cols

    clip_cols = jnp.repeat(jnp.sqrt(clip_limit / jnp.maximum(maxima, clip_limit)), HD, axis=1)
    unit_row = jnp.ones_like(clip_cols[0])
    clip_attention = jnp.stack(
        [clip_cols[0], clip_cols[0], unit_row, unit_row, clip_cols[1], clip_cols[1], unit_row, unit_row]
    )[:, None, :]
    local_cols = lax.dynamic_slice_in_dim(clip_cols, first_col, shard_cols, 1)
    row = lax.broadcasted_iota(jnp.int32, vectors_master.shape, 0)
    clip_vectors = jnp.where(row == 6, local_cols[0:1], jnp.where(row == 9, local_cols[1:2], 1.0))
    step_value = float(ADAM_STEP)
    new_attention = adam_update(
        attention_master, g_attention, attention_first, attention_second, step_value, clip_attention
    )
    new_expand = adam_update(expand_master, g_expand, expand_first, expand_second, step_value, 1.0)
    new_contract = adam_update(contract_master, g_contract, contract_first, contract_second, step_value, 1.0)
    new_vectors = adam_update(vectors_master, g_vectors, vectors_first, vectors_second, step_value, clip_vectors)
    return (
        result,
        grad_input,
        grad_encoder,
        g_attention,
        g_expand,
        g_contract,
        g_vectors,
        new_attention[0],
        new_expand[0],
        new_contract[0],
        new_vectors[0],
        new_attention[1],
        new_expand[1],
        new_contract[1],
        new_vectors[1],
        new_attention[2],
        new_expand[2],
        new_contract[2],
        new_vectors[2],
    )


def solution(mesh):
    planes = mesh.shape["dp"] // 2
    side = math.isqrt(planes)
    if side * side * 2 != mesh.shape["dp"]:
        side = 1
    sizes = (mesh.shape["dp"] // (2 * side), side, 2, mesh.shape["fsdp"])
    fast = sizes == (2, 2, 2, 4)
    mesh = Mesh(mesh.devices.reshape(sizes), ALL)
    shards = (
        P(ALL, None, None),
        P(ALL, None, None),
        P(ALL, None, None),
    )
    weights = (P(None, ALL, None), P(ALL, None), P(ALL, None), P(None, ALL))
    return jax.shard_map(
        functools.partial(local, fast),
        mesh=mesh,
        in_specs=shards + weights * 3,
        out_specs=shards + weights * 4,
        check_vma=False,
    )
```

time: 673 us -> 574 us (0.85)
  starting transfers between devices: 80.1 us -> 19.7 us
  Pallas kernels: 202 us -> 247 us
  waiting for transfers between devices: 294 us -> 249 us
  other arithmetic: 31.3 us -> 12.4 us
  local copies, waits for them, and re-layouts: 40 us -> 28.2 us
    ppermute x60 -> x21, starting transfers between devices: 80.1 us -> 19.4 us  [step(): lax.ppermute(v, axis, pairs)]
    pallas_call x8 -> x17, Pallas kernels: 81 us -> 135 us  [the longest x8 82 us: call(): pl.pallas_call(body, in_specs=specs, **settings)]
    ppermute x60 -> x21, waiting for transfers between devices: 129 us -> 83.5 us  [step(): lax.ppermute(v, axis, pairs)]
    convert_element_type x25 -> x2, other arithmetic: 16.3 us -> 2.56 us  [the longest x1 1.38 us: gradients_fast(): lax.psum_scatter(rf, 'z', scatter_dimension=0, tiled=True)[0].astype(F32)]
    pallas_call x1, Pallas kernels: 32.7 us -> 23.2 us  [feed(): pl.pallas_call(feed_kernel, grid=(8,), out_shape=[shape((rows, width), BF...]
    unnamed x109 -> x128, local copies, waits for them, and re-layouts: 29.9 us -> 21.7 us
  transfers between devices with their start and end apart: 62 -> 25, of which waited for: 37 -> 15; matrix products, arithmetic and copies ran while one was open for 8% -> 2% of each run, Pallas kernels for 15% -> 37%
where the time goes in v2:
time: 574 us; the launch traced here: 571 us
  waiting for transfers between devices  249 us (43%)
  Pallas kernels  247 us (43%)
  local copies, waits for them, and re-layouts  28.2 us (5%)
  starting transfers between devices  19.7 us (3%)
  between operations  14.9 us (3%)
  other arithmetic  12.4 us (2%)
    all_gather x1, waiting for transfers between devices, gather_fast(): pack = lax.all_gather(shard, ALL, axis=0, tiled=False)  119 us
    ppermute x21, waiting for transfers between devices, step(): lax.ppermute(v, axis, pairs)  83.5 us
    pallas_call x8, Pallas kernels, call(): pl.pallas_call(body, in_specs=specs, **settings)  82 us
    all_gather x1, waiting for transfers between devices, gather_fast(): lax.all_gather(feed_shard(expand, contract), ALL, axis=0, tiled=False)  46.4 us
    pallas_call x2, Pallas kernels, attend_grad(): pl.pallas_call(functools.partial(attend_grad_kernel, causal, valid), grid...  44.9 us
    pallas_call x2, Pallas kernels, attend(): pl.pallas_call(functools.partial(attend_kernel, causal, valid), grid=(pai...  29.1 us
    pallas_call x6, Pallas kernels, add_pieces(): pl.pallas_call(functools.partial(add_kernel, plan, len(left)), out_shape=...  26.7 us
    pallas_call x1, Pallas kernels, feed(): pl.pallas_call(feed_kernel, grid=(8,), out_shape=[shape((rows, width), BF...  23.2 us
  transfers between devices with their start and end apart: 25, of which 15 were waited for; matrix products, arithmetic and copies ran while one was open for 2% of the time, Pallas kernels for 37%

profile of v2, /device:TPU:0, one launch (start us, length us, event | category | flops | bytes accessed | tf_op | source)
XLA Modules:
  0.0 570.7 jit_solution(4223681911968896815)
XLA Ops:
  15.5 118.6 %all-gather.5.cloned.1.call-done = bf16[8704,1024]{1,0:T(8,128)(2,1)} async-done(((bf16[272,1024]{1,0:T(8,128)(2,1)}), bf16[8704,1024]{1,0:T(8,128)(2,1)}) %all-gather.5.cloned.1.call-update) | async-done | bytes 17825808 | tf_op jit(solution)/shard_map/all_gather | solution.py:937
  135.7 7.4 %self_in.1 = (bf16[448,1024]{1,0:T(8,128)(2,1)S(1)}, bf16[448,1024]{1,0:T(8,128)(2,1)S(1)}, bf16[448,1024]{1,0:T(8,128)(2,1)S(1)}, bf16[448,1024]{1,0:T(8,128)(2,1)S(1)}) custom-call(s32[2]{0:T(128)S(1)} %pad_add_fusion.refs_0_.place_ref, bf16[448,1024]{1,0:T(8,128)(2,1)S(1)} %bitcast.68, ...), custom_call_target="tpu_custom_call" | custom-call | flops 2818572288 | bytes 10485760 | tf_op jit(solution)/shard_map/self_in/pallas_call | solution.py:86
  144.0 8.3 %attend_causal.1 = (bf16[448,1024]{1,0:T(8,128)(2,1)S(1)}, f32[8,1,896]{2,1,0:T(1,128)S(1)}, f32[8,1,128]{2,1,0:T(1,128)S(1)}) custom-call(bf16[448,1024]{1,0:T(8,128)(2,1)S(1)} %get-tuple-element.144.q_ref, bf16[448,1024]{1,0:T(8,128)(2,1)S(1)} %get-tuple-element.145.k_ref, bf16[448,1024]{1,0:T(8,128)(2,1)S(1)} %get-tuple-element.146.v_ref), custom_call_target="tpu_custom_call" | custom-call | flops 3288334336 | bytes 1835008 | tf_op jit(solution)/shard_map/attend_causal/pallas_call | solution.py:267
  153.6 6.1 %self_out.1 = (f32[448,1024]{1,0:T(8,128)S(1)}, bf16[448,1024]{1,0:T(8,128)(2,1)S(1)}, bf16[448,1024]{1,0:T(8,128)(2,1)S(1)}) custom-call(s32[2]{0:T(128)S(1)} %pad_add_fusion.refs_0_.place_ref, bf16[448,1024]{1,0:T(8,128)(2,1)S(1)} %get-tuple-element.147.refs_1_.refs_5_.o_ref, bf16[448,1024]{1,0:T(8,128)(2,1)S(1)} %bitcast.69, ...), custom_call_target="tpu_custom_call" | custom-call | flops 1879048192 | bytes 10485760 | tf_op jit(solution)/shard_map/self_out/pallas_call | solution.py:86
  160.6 14.5 %cross_in.1 = (bf16[1504,1024]{1,0:T(8,128)(2,1)S(1)}, bf16[1504,1024]{1,0:T(8,128)(2,1)}) custom-call(s32[2]{0:T(128)S(1)} %pad_add_fusion.refs_0_.place_ref, bf16[1504,1024]{1,0:T(8,128)(2,1)} %pad.9.refs_1_.e_ref, f32[17,1024]{1,0:T(8,128)S(1)} %convert_element_type.70.refs_2_.refs_3_.vec_ref.refs_5_.refs_6_, bf16[32,272,1024]{2,1,0:T(8,128)(2,1)} %bitcast.77, ...), custom_call_target="tpu_custom_call" | custom-call | flops 6308233216 | bytes 14680064 | tf_op jit(solution)/shard_map/cross_in/pallas_call | solution.py:86
  175.1 20.8 %attend.1 = (bf16[448,1024]{1,0:T(8,128)(2,1)S(1)}, f32[8,1,896]{2,1,0:T(1,128)S(1)}, f32[8,1,128]{2,1,0:T(1,128)S(1)}) custom-call(bf16[448,1024]{1,0:T(8,128)(2,1)S(1)} %get-tuple-element.148.q_ref, bf16[1504,1024]{1,0:T(8,128)(2,1)S(1)} %get-tuple-element.149.k_ref, bf16[1504,1024]{1,0:T(8,128)(2,1)} %get-tuple-element.150.v_ref), custom_call_target="tpu_custom_call" | custom-call | flops 11039408128 | bytes 6160384 | tf_op jit(solution)/shard_map/attend/pallas_call | solution.py:267
  204.3 46.4 %all-gather.7.cloned.1.call-done = bf16[8192,1024]{1,0:T(8,128)(2,1)} async-done(((bf16[256,1024]{1,0:T(8,128)(2,1)}), bf16[8192,1024]{1,0:T(8,128)(2,1)}) %all-gather.7.cloned.1.call-update) | async-done | bytes 16777232 | tf_op jit(solution)/shard_map/all_gather | solution.py:938
  254.5 23.2 %feed.1 = (bf16[448,1024]{1,0:T(8,128)(2,1)}, bf16[448,4096]{1,0:T(8,128)(2,1)}, f32[8,1,512]{2,1,0:T(1,128)S(1)}, f32[1,1024]{1,0:T(1,128)S(1)}, bf16[8,4,256,1024]{3,2,1,0:T(8,128)(2,1)}) custom-call(bf16[448,1024]{1,0:T(8,128)(2,1)S(1)} %copy-done.13, f32[448,1024]{1,0:T(8,128)S(1)} %copy-done.6, bf16[448,1024]{1,0:T(8,128)(2,1)S(1)} %bitcast.70, ...), custom_call_target="tpu_custom_call" | custom-call | flops 15032385536 | bytes 31457280 | tf_op jit(solution)/shard_map/feed/pallas_call | solution.py:411
  277.7 15.3 %feed_grad.1 = (f32[448,1024]{1,0:T(8,128)S(1)}, bf16[8,4,256,1024]{3,2,1,0:T(8,128)(2,1)}) custom-call(bf16[448,1024]{1,0:T(8,128)(2,1)S(1)} %copy-done.13, bf16[448,4096]{1,0:T(8,128)(2,1)} %get-tuple-element.157.df_ref, bf16[32,256,1024]{2,1,0:T(8,128)(2,1)} %bitcast.89, ...), custom_call_target="tpu_custom_call", output_to_operand_aliasing={{1}: (3, {})} | custom-call | flops 7516192768 | bytes 23068672 | tf_op jit(solution)/shard_map/feed_grad/pallas_call | solution.py:457
  295.8 8.1 %cross_out_grad.1 = (f32[448,1024]{1,0:T(8,128)S(1)}, bf16[448,1024]{1,0:T(8,128)(2,1)S(1)}, f32[3,1024]{1,0:T(4,128)S(1)}, bf16[4,4,96,1024]{3,2,1,0:T(8,128)(2,1)}, bf16[4,4,96,1024]{3,2,1,0:T(8,128)(2,1)}) custom-call(s32[2]{0:T(128)S(1)} %pad_add_fusion.refs_0_.place_ref, f32[448,1024]{1,0:T(8,128)} %copy-done.7, f32[448,1024]{1,0:T(8,128)} %copy-done.5, ...), custom_call_target="tpu_custom_call" | custom-call | flops 1879048192 | bytes 14680064 | tf_op jit(solution)/shard_map/cross_out_grad/pallas_call | solution.py:86
  306.0 31.9 %attend_grad.1 = (bf16[448,1024]{1,0:T(8,128)(2,1)}, bf16[1504,1024]{1,0:T(8,128)(2,1)}, bf16[1504,1024]{1,0:T(8,128)(2,1)}) custom-call(bf16[448,1024]{1,0:T(8,128)(2,1)} %copy-done.25, bf16[1504,1024]{1,0:T(8,128)(2,1)} %copy-done.20, bf16[1504,1024]{1,0:T(8,128)(2,1)} %get-tuple-element.150.v_ref, bf16[448,1024]{1,0:T(8,128)(2,1)} %copy-done.4, ...), custom_call_target="tpu_custom_call" | custom-call | flops 27598520320 | bytes 12320768 | tf_op jit(solution)/shard_map/attend_grad/pallas_call | solution.py:561
  337.9 13.8 %cross_query_grad.1 = (f32[448,1024]{1,0:T(8,128)}, bf16[448,1024]{1,0:T(8,128)(2,1)}, f32[4,1024]{1,0:T(4,128)}, bf16[4,4,96,1024]{3,2,1,0:T(8,128)(2,1)}, bf16[4,4,96,1024]{3,2,1,0:T(8,128)(2,1)}) custom-call(s32[2]{0:T(128)} %copy-done.14, bf16[448,1024]{1,0:T(8,128)(2,1)} %copy-done.11, ...), custom_call_target="tpu_custom_call", output_to_operand_aliasing={{3}: (7, {}), {4}: (8, {})} | custom-call | flops 3758096384 | bytes 20971520 | tf_op jit(solution)/shard_map/cross_query_grad/pallas_call | solution.py:86
  352.1 13.0 %attend_causal_grad.1 = (bf16[448,1024]{1,0:T(8,128)(2,1)}, bf16[448,1024]{1,0:T(8,128)(2,1)}, bf16[448,1024]{1,0:T(8,128)(2,1)}) custom-call(bf16[448,1024]{1,0:T(8,128)(2,1)} %copy-done.22, bf16[448,1024]{1,0:T(8,128)(2,1)} %copy-done.23, bf16[448,1024]{1,0:T(8,128)(2,1)} %copy-done.24, bf16[448,1024]{1,0:T(8,128)(2,1)} %copy-done.3, ...), custom_call_target="tpu_custom_call" | custom-call | flops 8220835840 | bytes 3670016 | tf_op jit(solution)/shard_map/attend_causal_grad/pallas_call | solution.py:561
  366.8 5.2 add_pieces.6
  373.7 9.9 %self_weight_grad.1 = (f32[2,1024]{1,0:T(2,128)}, bf16[4,4,160,1024]{3,2,1,0:T(8,128)(2,1)}, bf16[4,4,160,1024]{3,2,1,0:T(8,128)(2,1)}) custom-call(s32[2]{0:T(128)} %copy-done.14, bf16[448,1024]{1,0:T(8,128)(2,1)} %copy-done.21, bf16[448,1024]{1,0:T(8,128)(2,1)} %get-tuple-element.201.dq_ref.refs_1_, bf16[448,1024]{1,0:T(8,128)(2,1)} %get-tuple-element.202.dk_ref.refs_2_, ...), custom_call_target="tpu_custom_call" | custom-call | flops 2818572288 | bytes 10485760 | tf_op jit(solution)/shard_map/self_weight_grad/pallas_call | solution.py:712
  383.6 14.4 %cross_key_grad.1 = (f32[1,1024]{1,0:T(1,128)}, bf16[4,4,160,1024]{3,2,1,0:T(8,128)(2,1)}, bf16[4,4,160,1024]{3,2,1,0:T(8,128)(2,1)}) custom-call(s32[2]{0:T(128)} %copy-done.14, bf16[1504,1024]{1,0:T(8,128)(2,1)} %pad.9.refs_1_.e_ref, bf16[1504,1024]{1,0:T(8,128)(2,1)} %get-tuple-element.222.dk_ref.refs_1_, ...), custom_call_target="tpu_custom_call", output_to_operand_aliasing={{1}: (4, {}), {2}: (5, {})} | custom-call | flops 6308233216 | bytes 14680064 | tf_op jit(solution)/shard_map/cross_key_grad/pallas_call | solution.py:650
  408.9 12.1 %self_in_grad.1 = (f32[448,1024]{1,0:T(8,128)}, f32[2,1024]{1,0:T(2,128)}) custom-call(s32[2]{0:T(128)} %copy-done.14, bf16[448,1024]{1,0:T(8,128)(2,1)} %get-tuple-element.201.dq_ref.refs_1_, bf16[448,1024]{1,0:T(8,128)(2,1)} %get-tuple-element.202.dk_ref.refs_2_, bf16[448,1024]{1,0:T(8,128)(2,1)} %get-tuple-element.203.dv_ref.refs_3_, ...), custom_call_target="tpu_custom_call" | custom-call | flops 2818572288 | bytes 14680064 | tf_op jit(solution)/shard_map/self_in_grad/pallas_call | solution.py:86
  423.6 7.0 %add_pieces.9 = (bf16[2,4,80,1024]{3,2,1,0:T(8,128)(2,1)}, bf16[2,4,80,1024]{3,2,1,0:T(8,128)(2,1)}, bf16[2,4,80,1024]{3,2,1,0:T(8,128)(2,1)}, bf16[2,4,80,1024]{3,2,1,0:T(8,128)(2,1)}) custom-call(s32[2]{0:T(128)} %copy-done.14, bf16[4,4,160,1024]{3,2,1,0:T(8,128)(2,1)} %get-tuple-element.218.refs_0_, bf16[4,4,160,1024]{3,2,1,0:T(8,128)(2,1)} %collective-permute-done.5.refs_1_), custom_call_target="tpu_custom_call" | custom-call | bytes 15728640 | tf_op jit(solution)/shard_map/add_pieces/pallas_call | solution.py:829
  437.8 15.0 %encoder_grad.1 = f32[12000,128]{1,0:T(8,128)} custom-call(s32[2]{0:T(128)} %copy-done.14, bf16[1504,1024]{1,0:T(8,128)(2,1)} %get-tuple-element.222.dk_ref.refs_1_, bf16[1504,1024]{1,0:T(8,128)(2,1)} %get-tuple-element.182.dv_ref.refs_2_, bf16[32,272,1024]{2,1,0:T(8,128)(2,1)} %bitcast.85, bf16[32,272,1024]{2,1,0:T(8,128)(2,1)} %bitcast.86), custom_call_target="tpu_custom_call" | custom-call | flops 6291456000 | bytes 16777216 | tf_op jit(solution)/shard_map/encoder_grad/pallas_call | solution.py:86
  456.8 5.8 %collective-permute-done.6 = bf16[96,1024]{1,0:T(8,128)(2,1)S(1)} collective-permute-done((bf16[96,1024]{1,0:T(8,128)(2,1)}, bf16[96,1024]{1,0:T(8,128)(2,1)S(1)}, u32[]{:S(2)}, u32[]{:S(2)}) %collective-permute-start.6) | collective-permute-done | bytes 196640 | tf_op jit(solution)/shard_map/ppermute | solution.py:788
  466.9 20.0 %collective-permute-done.8 = bf16[96,1024]{1,0:T(8,128)(2,1)S(1)} collective-permute-done((bf16[96,1024]{1,0:T(8,128)(2,1)}, bf16[96,1024]{1,0:T(8,128)(2,1)S(1)}, u32[]{:S(2)}, u32[]{:S(2)}) %collective-permute-start.8) | collective-permute-done | bytes 196640 | tf_op jit(solution)/shard_map/ppermute | solution.py:788
  496.1 13.2 %collective-permute-done.14 = f32[24,1024]{1,0:T(8,128)S(1)} collective-permute-done((f32[24,1024]{1,0:T(8,128)S(1)}, f32[24,1024]{1,0:T(8,128)S(1)}, u32[]{:S(2)}, u32[]{:S(2)}) %collective-permute-start.14) | collective-permute-done | bytes 98336 | tf_op jit(solution)/shard_map/ppermute | solution.py:788
  527.8 14.4 %collective-permute-done.17 = bf16[160,1024]{1,0:T(8,128)(2,1)S(1)} collective-permute-done((bf16[160,1024]{1,0:T(8,128)(2,1)}, bf16[160,1024]{1,0:T(8,128)(2,1)S(1)}, u32[]{:S(2)}, u32[]{:S(2)}) %collective-permute-start.17) | collective-permute-done | bytes 327712 | tf_op jit(solution)/shard_map/ppermute | solution.py:788
  547.3 6.1 %collective-permute-done.20 = f32[24,1024]{1,0:T(8,128)S(1)} collective-permute-done((f32[24,1024]{1,0:T(8,128)S(1)}, f32[24,1024]{1,0:T(8,128)S(1)}, u32[]{:S(2)}, u32[]{:S(2)}) %collective-permute-start.20) | collective-permute-done | bytes 98336 | tf_op jit(solution)/shard_map/ppermute | solution.py:788
  (231 shorter events, 105.5 us)
Async XLA Ops:
  7.2 126.8 %all-gather.5.cloned.1.call-start = ((), (), s32[]{:S(2)}) async-start(), calls=%async_computation.4 | async-start | bytes 18382848 | tf_op jit(solution)/shard_map/all_gather | solution.py:937
  10.4 240.3 %all-gather.7.cloned.1.call-start = ((), (), s32[]{:S(2)}) async-start(), calls=%async_computation.5 | async-start | bytes 17301504 | tf_op jit(solution)/shard_map/all_gather | solution.py:938
  11.4 445.3 %reduce-scatter.3.cloned.1.call-start = ((), (), s32[]{:S(2)}) async-start(), calls=%async_computation.2 | async-start | bytes 18874368 | tf_op jit(solution)/shard_map/reduce_scatter | solution.py:1068
  294.3 264.2 %reduce-scatter.5.cloned.1.call-start = ((), (), s32[]{:S(2)}) async-start(), calls=%async_computation.3 | async-start | bytes 2621440 | tf_op jit(solution)/shard_map/reduce_scatter | solution.py:1069
  351.8 13.4 %collective-permute-start = (bf16[4,4,96,1024]{3,2,1,0:T(8,128)(2,1)}, bf16[4,4,96,1024]{3,2,1,0:T(8,128)(2,1)S(1)}, u32[]{:S(2)}, u32[]{:S(2)}) collective-permute-start(bf16[4,4,96,1024]{3,2,1,0:T(8,128)(2,1)} %get-tuple-element.173), channel_id=1, source_target_pairs={{0,4},{4,0},{1,5},{5,1},{2,6},{6,2},{3,7},{7,3},{8,12},{12,8},{9,1... | collective-permute-start | bytes 9437192 | tf_op jit(solution)/shard_map/ppermute | solution.py:788
  372.1 27.5 %collective-permute-start.1 = (bf16[2,4,48,1024]{3,2,1,0:T(8,128)(2,1)}, bf16[2,4,48,1024]{3,2,1,0:T(8,128)(2,1)S(1)}, u32[]{:S(2)}, u32[]{:S(2)}) collective-permute-start(bf16[2,4,48,1024]{3,2,1,0:T(8,128)(2,1)} %get-tuple-element.194), channel_id=1, source_target_pairs={{0,8},{8,0},{1,9},{9,1},{2,10},{10,2},{3,11},{11,3},{4,12},{12,4},... | collective-permute-start | bytes 2359304 | tf_op jit(solution)/shard_map/ppermute | solution.py:788
  373.2 28.2 %collective-permute-start.2 = (bf16[2,4,48,1024]{3,2,1,0:T(8,128)(2,1)}, bf16[2,4,48,1024]{3,2,1,0:T(8,128)(2,1)S(1)}, u32[]{:S(2)}, u32[]{:S(2)}) collective-permute-start(bf16[2,4,48,1024]{3,2,1,0:T(8,128)(2,1)} %get-tuple-element.195), channel_id=1, source_target_pairs={{0,16},{16,0},{1,17},{17,1},{2,18},{18,2},{3,19},{19,3},{4,20},{20... | collective-permute-start | bytes 2359304 | tf_op jit(solution)/shard_map/ppermute | solution.py:788
  405.6 18.0 %collective-permute-start.5 = (bf16[4,4,160,1024]{3,2,1,0:T(8,128)(2,1)}, bf16[4,4,160,1024]{3,2,1,0:T(8,128)(2,1)}, u32[]{:S(2)}, u32[]{:S(2)}) collective-permute-start(bf16[4,4,160,1024]{3,2,1,0:T(8,128)(2,1)} %get-tuple-element.209), channel_id=1, source_target_pairs={{0,4},{4,0},{1,5},{5,1},{2,6},{6,2},{3,7},{7,3},{8,12},{12,8},{9,1... | collective-permute-start | bytes 15728648 | tf_op jit(solution)/shard_map/ppermute | solution.py:788
  405.7 17.9 %collective-permute-start.3 = (bf16[4,48,1024]{2,1,0:T(8,128)(2,1)}, bf16[4,48,1024]{2,1,0:T(8,128)(2,1)S(1)}, u32[]{:S(2)}, u32[]{:S(2)}) collective-permute-start(bf16[4,48,1024]{2,1,0:T(8,128)(2,1)} %get-tuple-element.207), channel_id=1, source_target_pairs={{0,16},{16,0},{1,17},{17,1},{2,18},{18,2},{3,19},{19,3},{4,20},{20... | collective-permute-start | bytes 1179656 | tf_op jit(solution)/shard_map/ppermute | solution.py:788
  406.9 16.7 %collective-permute-start.4 = (bf16[4,48,1024]{2,1,0:T(8,128)(2,1)}, bf16[4,48,1024]{2,1,0:T(8,128)(2,1)S(1)}, u32[]{:S(2)}, u32[]{:S(2)}) collective-permute-start(bf16[4,48,1024]{2,1,0:T(8,128)(2,1)} %get-tuple-element.208), channel_id=1, source_target_pairs={{0,8},{8,0},{1,9},{9,1},{2,10},{10,2},{3,11},{11,3},{4,12},{12,4},... | collective-permute-start | bytes 1179656 | tf_op jit(solution)/shard_map/ppermute | solution.py:788
  433.7 53.2 %collective-permute-start.9 = (bf16[2,4,80,1024]{3,2,1,0:T(8,128)(2,1)}, bf16[2,4,80,1024]{3,2,1,0:T(8,128)(2,1)S(1)}, u32[]{:S(2)}, u32[]{:S(2)}) collective-permute-start(bf16[2,4,80,1024]{3,2,1,0:T(8,128)(2,1)} %get-tuple-element.226), channel_id=1, source_target_pairs={{0,8},{8,0},{1,9},{9,1},{2,10},{10,2},{3,11},{11,3},{4,12},{12,4},... | collective-permute-start | bytes 3932168 | tf_op jit(solution)/shard_map/ppermute | solution.py:788
  434.8 52.0 %collective-permute-start.10 = (bf16[2,4,80,1024]{3,2,1,0:T(8,128)(2,1)}, bf16[2,4,80,1024]{3,2,1,0:T(8,128)(2,1)S(1)}, u32[]{:S(2)}, u32[]{:S(2)}) collective-permute-start(bf16[2,4,80,1024]{3,2,1,0:T(8,128)(2,1)} %get-tuple-element.227), channel_id=1, source_target_pairs={{0,16},{16,0},{1,17},{17,1},{2,18},{18,2},{3,19},{19,3},{4,20},{20... | collective-permute-start | bytes 3932168 | tf_op jit(solution)/shard_map/ppermute | solution.py:788
  437.8 18.9 %collective-permute-start.11 = (f32[24,1024]{1,0:T(8,128)}, f32[24,1024]{1,0:T(8,128)S(1)}, u32[]{:S(2)}, u32[]{:S(2)}) collective-permute-start(f32[24,1024]{1,0:T(8,128)} %vector_table.1), channel_id=1, source_target_pairs={{0,4},{4,0},{1,5},{5,1},{2,6},{6,2},{3,7},{7,3},{8,12},{12,8},{9,1... | collective-permute-start | bytes 294920 | tf_op jit(solution)/shard_map/ppermute | solution.py:788
  452.8 9.8 %collective-permute-start.6 = (bf16[96,1024]{1,0:T(8,128)(2,1)}, bf16[96,1024]{1,0:T(8,128)(2,1)S(1)}, u32[]{:S(2)}, u32[]{:S(2)}) collective-permute-start(bf16[96,1024]{1,0:T(8,128)(2,1)} %get-tuple-element.223), channel_id=1, source_target_pairs={{0,1},{1,2},{2,3},{3,0},{4,5},{5,6},{6,7},{7,4},{8,9},{9,10},{10,1... | collective-permute-start | bytes 589832 | tf_op jit(solution)/shard_map/ppermute | solution.py:788
  452.9 14.0 %collective-permute-start.7 = (bf16[96,1024]{1,0:T(8,128)(2,1)}, bf16[96,1024]{1,0:T(8,128)(2,1)S(1)}, u32[]{:S(2)}, u32[]{:S(2)}) collective-permute-start(bf16[96,1024]{1,0:T(8,128)(2,1)} %get-tuple-element.224), channel_id=1, source_target_pairs={{0,3},{1,0},{2,1},{3,2},{4,7},{5,4},{6,5},{7,6},{8,11},{9,8},{10,9... | collective-permute-start | bytes 589832 | tf_op jit(solution)/shard_map/ppermute | solution.py:788
  456.7 30.2 %collective-permute-start.8 = (bf16[96,1024]{1,0:T(8,128)(2,1)}, bf16[96,1024]{1,0:T(8,128)(2,1)S(1)}, u32[]{:S(2)}, u32[]{:S(2)}) collective-permute-start(bf16[96,1024]{1,0:T(8,128)(2,1)} %get-tuple-element.225), channel_id=1, source_target_pairs={{0,2},{1,3},{2,0},{3,1},{4,6},{5,7},{6,4},{7,5},{8,10},{9,11},{10,... | collective-permute-start | bytes 589832 | tf_op jit(solution)/shard_map/ppermute | solution.py:788
  493.0 16.3 %collective-permute-start.12 = (bf16[4,80,1024]{2,1,0:T(8,128)(2,1)}, bf16[4,80,1024]{2,1,0:T(8,128)(2,1)S(1)}, u32[]{:S(2)}, u32[]{:S(2)}) collective-permute-start(bf16[4,80,1024]{2,1,0:T(8,128)(2,1)} %get-tuple-element.246), channel_id=1, source_target_pairs={{0,16},{16,0},{1,17},{17,1},{2,18},{18,2},{3,19},{19,3},{4,20},{20... | collective-permute-start | bytes 1966088 | tf_op jit(solution)/shard_map/ppermute | solution.py:788
  494.0 15.2 %collective-permute-start.13 = (bf16[4,80,1024]{2,1,0:T(8,128)(2,1)}, bf16[4,80,1024]{2,1,0:T(8,128)(2,1)S(1)}, u32[]{:S(2)}, u32[]{:S(2)}) collective-permute-start(bf16[4,80,1024]{2,1,0:T(8,128)(2,1)} %get-tuple-element.247), channel_id=1, source_target_pairs={{0,8},{8,0},{1,9},{9,1},{2,10},{10,2},{3,11},{11,3},{4,12},{12,4},... | collective-permute-start | bytes 1966088 | tf_op jit(solution)/shard_map/ppermute | solution.py:788
  494.0 15.2 %collective-permute-start.14 = (f32[24,1024]{1,0:T(8,128)S(1)}, f32[24,1024]{1,0:T(8,128)S(1)}, u32[]{:S(2)}, u32[]{:S(2)}) collective-permute-start(f32[24,1024]{1,0:T(8,128)S(1)} %maximum_select_fusion.4), channel_id=1, source_target_pairs={{0,8},{8,0},{1,9},{9,1},{2,10},{10,2},{3,11},{11,3},{4,12},{12,4},... | collective-permute-start | bytes 294920 | tf_op jit(solution)/shard_map/ppermute | solution.py:788
  513.8 12.8 %collective-permute-start.15 = (bf16[160,1024]{1,0:T(8,128)(2,1)}, bf16[160,1024]{1,0:T(8,128)(2,1)S(1)}, u32[]{:S(2)}, u32[]{:S(2)}) collective-permute-start(bf16[160,1024]{1,0:T(8,128)(2,1)} %get-tuple-element.256), channel_id=1, source_target_pairs={{0,1},{1,2},{2,3},{3,0},{4,5},{5,6},{6,7},{7,4},{8,9},{9,10},{10,1... | collective-permute-start | bytes 983048 | tf_op jit(solution)/shard_map/ppermute | solution.py:788
  513.8 14.0 %collective-permute-start.16 = (bf16[160,1024]{1,0:T(8,128)(2,1)}, bf16[160,1024]{1,0:T(8,128)(2,1)S(1)}, u32[]{:S(2)}, u32[]{:S(2)}) collective-permute-start(bf16[160,1024]{1,0:T(8,128)(2,1)} %get-tuple-element.257), channel_id=1, source_target_pairs={{0,3},{1,0},{2,1},{3,2},{4,7},{5,4},{6,5},{7,6},{8,11},{9,8},{10,9... | collective-permute-start | bytes 983048 | tf_op jit(solution)/shard_map/ppermute | solution.py:788
  517.8 24.5 %collective-permute-start.17 = (bf16[160,1024]{1,0:T(8,128)(2,1)}, bf16[160,1024]{1,0:T(8,128)(2,1)S(1)}, u32[]{:S(2)}, u32[]{:S(2)}) collective-permute-start(bf16[160,1024]{1,0:T(8,128)(2,1)} %get-tuple-element.258), channel_id=1, source_target_pairs={{0,2},{1,3},{2,0},{3,1},{4,6},{5,7},{6,4},{7,5},{8,10},{9,11},{10,... | collective-permute-start | bytes 983048 | tf_op jit(solution)/shard_map/ppermute | solution.py:788
  542.3 4.6 collective-permute-start.19
  547.0 6.4 %collective-permute-start.20 = (f32[24,1024]{1,0:T(8,128)S(1)}, f32[24,1024]{1,0:T(8,128)S(1)}, u32[]{:S(2)}, u32[]{:S(2)}) collective-permute-start(f32[24,1024]{1,0:T(8,128)S(1)} %maximum_select_fusion.1), channel_id=1, source_target_pairs={{0,2},{2,0},{1,3},{3,1},{4,6},{6,4},{5,7},{7,5},{8,10},{10,8},{9,1... | collective-permute-start | bytes 294920 | tf_op jit(solution)/shard_map/ppermute | solution.py:788
  (58 other events, 1169.4 us)
Sparse Core Ops, SparseCore 0:
  11.5 122.5 all-gather.4
  137.6 113.0 all-gather.6
  293.2 129.3 reduce-scatter.2
  456.8 47.5 reduce-scatter.4

commit v3 on v2

--- a/solution.py
+++ b/solution.py
@@ -23,7 +23,7 @@
 BF = jnp.bfloat16
 F32 = jnp.float32
 ALL = ("y", "x", "c", "z")
-TILE = 256
+TILE = 512
 KEY_CHUNK = 256
 VEC_ROWS = 17
 MIB = 1024 * 1024
@@ -107,24 +107,6 @@
         start = pl.multiple_of(n * TILE, TILE)
         rows = buf[pl.ds(n * per, per)].reshape(TILE, buf.shape[2])
         put(start, dot_nt(act_ref[...], rows))
-
-
-def grad_weight(act_ref, grad_ref, out):
-    @pl.loop(0, 4)
-    def _(n):
-        start = pl.multiple_of(n * TILE, TILE)
-        tile = dot_tn(act_ref[:, pl.ds(start, TILE)], grad_ref[...])
-        out[pl.ds(2 * n, 2)] = tile.astype(BF).reshape((2,) + out.shape[1:])
-
-
-def block_copies(sel, grad, keep, send, row, sems):
-    out = []
-    for j in range(8):
-        across, plane = j // 4, j % 4
-        block = jnp.bitwise_xor(sel, plane * 2 + across)
-        target = (send if across else keep).at[plane, :, pl.ds(row, grad.shape[2]), :]
-        out.append(pltpu.make_async_copy(grad.at[block], target, sems.at[j]))
-    return out
 
 
 def start_all(copies):
@@ -413,7 +395,7 @@
         grid=(8,),
         out_shape=[
             shape((rows, width), BF), shape((rows, hidden), BF), shape((8, 1, wide), F32), shape((1, width), F32),
-            shape((8, 4, 256, width), BF),
+            shape((8, 4, 128, width), BF),
         ],
         in_specs=[
             whole((rows, width)),
@@ -429,56 +411,42 @@
             pl.BlockSpec((rows, wide), lambda n: (0, n)),
             pl.BlockSpec((1, 1, wide), lambda n: (n, 0, 0)),
             whole((1, width)),
-            pl.BlockSpec((1, 4, 128, width), lambda n: (n, 0, 1, 0)),
+            pl.BlockSpec((1, 4, 128, width), lambda n: (n, 0, 0, 0)),
         ],
         scratch_shapes=[pltpu.VMEM((rows, width), F32)],
-        compiler_params=params(48),
+        compiler_params=params(),
         cost_estimate=cost(8 * rows * width * hidden, 30 * MIB),
         name="feed",
     )(a3, x2, cot, vec, bias, pack, pack)
 
 
-def feed_grad_kernel(a_ref, df_ref, w1_ref, grad_in, da_ref, grad_ref):
-    wide = w1_ref.shape[2]
-    grad_pre = df_ref[...]
-    grad_ref[...] = dot_tn(a_ref[...], grad_pre).astype(BF).reshape(grad_ref.shape)
-
+def feed_grad_kernel(df_ref, w1_ref, da_ref):
     @pl.when(pl.program_id(0) == 0)
     def _():
         da_ref[...] = jnp.zeros_like(da_ref)
 
-    da_ref[...] += dot_nt(grad_pre, w1_ref[...].reshape(a_ref.shape[1], wide))
-
-
-def feed_grad(a3, df, grad, pack):
-    rows, width = a3.shape
-    hidden = df.shape[1]
-    wide = hidden // 8
+    da_ref[...] += dot_nt(df_ref[...], w1_ref[...].reshape(da_ref.shape[1], w1_ref.shape[2]))
+
+
+def feed_grad(df, pack):
+    rows, hidden = df.shape
+    width = pack.shape[2]
     return pl.pallas_call(
         feed_grad_kernel,
-        grid=(8,),
-        out_shape=[shape((rows, width), F32), shape(grad.shape, BF)],
+        grid=(hidden // width,),
+        out_shape=shape((rows, width), F32),
         in_specs=[
-            whole((rows, width)),
-            pl.BlockSpec((rows, wide), lambda n: (0, n)),
-            pl.BlockSpec((32, 32, wide), lambda n: (0, n // 2, n % 2)),
-            hbm(),
+            pl.BlockSpec((rows, width), lambda n: (0, n)),
+            pl.BlockSpec((32, 32, width), lambda n: (0, n, 0)),
         ],
-        out_specs=[
-            whole((rows, width)),
-            pl.BlockSpec((8, 4, 32, wide), lambda n: (0, 0, n // 2, n % 2)),
-        ],
-        input_output_aliases={3: 1},
-        compiler_params=params(48),
-        cost_estimate=cost(4 * rows * width * hidden, 22 * MIB),
+        out_specs=whole((rows, width)),
+        compiler_params=params(),
+        cost_estimate=cost(2 * rows * width * hidden, 12 * MIB),
         name="feed_grad",
-    )(a3, df, pack, grad)
-
-
-def cross_out_grad_kernel(
-    place_ref, da_ref, x2_ref, cot_ref, o_ref, vec_ref, two,
-    dx_ref, do_ref, sums_ref, keep, send, buf, e_ref, grad, sem, sems,
-):
+    )(df, pack)
+
+
+def cross_out_grad_kernel(place_ref, da_ref, x2_ref, cot_ref, vec_ref, two, dx_ref, do_ref, e_ref, sums_ref, buf, sem):
     weight_start(place_ref, two, 32, buf, sem)
 
     def put(rows, value):
@@ -490,42 +458,34 @@
     sums_ref[0:1, :] = gain
     sums_ref[1:2, :] = shift
     sums_ref[2:3, :] = column_sum(e_ref)
-    grad_weight(o_ref, e_ref, grad)
-    out = block_copies(place_ref[0], grad, keep, send, 64, sems)
-    start_all(out)
     weight_wait(buf, sem)
 
     def put_mixed(start, value):
         do_ref[:, pl.ds(start, TILE)] = value.astype(BF)
 
     times_t(e_ref, buf, put_mixed)
-    wait_all(out)
-
-
-def cross_out_grad(place, da3, x2, cot, mixed, vec, packs):
+
+
+def cross_out_grad(place, da3, x2, cot, vec, packs):
     rows, width = x2.shape
-    blocks = shape((4, 4, 96, width), BF)
+    low = shape((rows, width), BF)
     return call(
         cross_out_grad_kernel,
         packs,
-        [place, da3, x2, cot, mixed, vec],
-        out_shape=[
-            shape((rows, width), F32), shape((rows, width), BF), shape((3, width), F32), blocks, blocks,
-        ],
-        in_specs=[smem()] + [vmem()] * 5,
-        out_specs=[vmem()] * 3 + [hbm()] * 2,
-        scratch_shapes=[
-            pltpu.VMEM((32, 32, width), BF), pltpu.VMEM((rows, width), BF), pltpu.VMEM((8, 4, 32, width), BF),
-            pltpu.SemaphoreType.DMA, pltpu.SemaphoreType.DMA((8,)),
-        ],
-        compiler_params=params(48),
-        cost_estimate=cost(4 * rows * width * width, 14 * MIB),
+        [place, da3, x2, cot, vec],
+        out_shape=[shape((rows, width), F32), low, low, shape((3, width), F32)],
+        in_specs=[smem()] + [vmem()] * 4,
+        out_specs=[vmem()] * 4,
+        scratch_shapes=[pltpu.VMEM((32, 32, width), BF), pltpu.SemaphoreType.DMA],
+        compiler_params=params(),
+        cost_estimate=cost(2 * rows * width * width, 10 * MIB),
         name="cross_out_grad",
     )
 
 
-def attend_grad_kernel(causal, valid, q_ref, k_ref, v_ref, o_ref, do_ref, lse_ref, *refs):
-    dq_ref, dk_ref, dv_ref = refs[-3:]
+def attend_grad_kernel(
+    causal, valid, q_ref, k_ref, v_ref, o_ref, do_ref, lse_ref, dq_ref, dk_ref, dv_ref, sums_ref
+):
     rows = q_ref.shape[0]
     scale = jnp.asarray(HD**-0.5, BF)
     query = masked_pair(q_ref[...] * scale)
@@ -536,52 +496,50 @@
     )
     lse = lse_ref[0]
     grad_query = jnp.zeros((2 * HD, 2 * rows), F32)
+    value_sum = jnp.zeros((1, 2 * HD), F32)
     for a, b in key_chunks(k_ref.shape[0]):
         key = k_ref[a:b, :]
         scores = exclude(dot_nt(key, query), a, rows, causal, valid)
         probs = jnp.exp(scores - lse)
         grad_probs = dot_nt(v_ref[a:b, :], grad_out)
         grad_scores = (probs * (grad_probs - delta)).astype(BF)
-        dv_ref[a:b, :] = dot(probs.astype(BF), grad_out).astype(BF)
+        grad_value = dot(probs.astype(BF), grad_out).astype(BF)
+        dv_ref[a:b, :] = grad_value
+        value_sum += jnp.sum(grad_value.astype(F32), axis=0, keepdims=True)
         dk_ref[a:b, :] = dot(grad_scores, query).astype(BF)
         grad_query += dot_tn(key, grad_scores)
-    dq_ref[...] = (pair_back(grad_query, rows) * HD**-0.5).astype(BF)
-
-
-def attend_grad(query, key, value, mixed, grad_mixed, lse, causal, valid, part=(0, 1), before=()):
+    grad_query = (pair_back(grad_query, rows) * HD**-0.5).astype(BF)
+    dq_ref[...] = grad_query
+    sums_ref[0:1, :] = jnp.sum(grad_query.astype(F32), axis=0, keepdims=True)
+    sums_ref[1:2, :] = value_sum
+
+
+def attend_grad(query, key, value, mixed, grad_mixed, lse, causal, valid):
     rows, width = query.shape
     keys = key.shape[0]
-    pairs = width // (2 * HD) // part[1]
-    skip = part[0] * pairs
+    pairs = width // (2 * HD)
 
     def column(count):
-        return pl.BlockSpec((count, 2 * HD), lambda h: (0, h + skip))
-
-    line = pl.BlockSpec((1, 1, 2 * rows), lambda h: (h + skip, 0, 0))
+        return pl.BlockSpec((count, 2 * HD), lambda h: (0, h))
+
+    line = pl.BlockSpec((1, 1, 2 * rows), lambda h: (h, 0, 0))
     return pl.pallas_call(
         functools.partial(attend_grad_kernel, causal, valid),
         grid=(pairs,),
-        out_shape=[shape((rows, width), BF)] + [shape((keys, width), BF)] * 2,
-        in_specs=[column(rows), column(keys), column(keys), column(rows), column(rows), line] + [hbm()] * len(before),
-        out_specs=[column(rows), column(keys), column(keys)],
-        input_output_aliases={6 + n: n for n in range(len(before))},
+        out_shape=[shape((rows, width), BF)] + [shape((keys, width), BF)] * 2 + [shape((2, width), F32)],
+        in_specs=[column(rows), column(keys), column(keys), column(rows), column(rows), line],
+        out_specs=[column(rows), column(keys), column(keys), column(2)],
         compiler_params=params(),
-        cost_estimate=cost(40 * rows * keys * width // part[1], 8 * keys * width),
+        cost_estimate=cost(40 * rows * keys * width, 8 * keys * width),
         name="attend_causal_grad" if causal else "attend_grad",
-    )(query, key, value, mixed, grad_mixed, lse, *before)
+    )(query, key, value, mixed, grad_mixed, lse)
 
 
 def cross_query_grad_kernel(
-    place_ref, a_ref, dq_ref, x1_ref, dx2_ref, o_ref, vec_ref, keep_in, send_in, one, two,
-    dx_ref, do_ref, sums_ref, keep, send, bufs, da_ref, e_ref, grads, sem, sems,
+    place_ref, dq_ref, x1_ref, dx2_ref, vec_ref, one, two, dx_ref, do_ref, e_ref, sums_ref, bufs, da_ref, sem
 ):
     for n, part in enumerate((one, two)):
         weight_start(place_ref, part, 32, bufs.at[n], sem.at[n])
-    place = place_ref[0]
-    grad_weight(a_ref, dq_ref, grads.at[0])
-    out = block_copies(place, grads.at[0], keep, send, 32, sems.at[0])
-    start_all(out)
-    sums_ref[0:1, :] = column_sum(dq_ref)
     weight_wait(bufs.at[0], sem.at[0])
 
     def put_act(start, value):
@@ -595,69 +553,102 @@
         e_ref[rows, :] = total.astype(BF)
 
     gain, shift = norm_grad(x1_ref, da_ref, vec_ref[2:3, :], put)
-    sums_ref[1:2, :] = gain
-    sums_ref[2:3, :] = shift
-    sums_ref[3:4, :] = column_sum(e_ref)
-    grad_weight(o_ref, e_ref, grads.at[1])
-    more = block_copies(place, grads.at[1], keep, send, 0, sems.at[1])
-    start_all(more)
+    sums_ref[0:1, :] = gain
+    sums_ref[1:2, :] = shift
+    sums_ref[2:3, :] = column_sum(e_ref)
     weight_wait(bufs.at[1], sem.at[1])
 
     def put_mixed(start, value):
         do_ref[:, pl.ds(start, TILE)] = value.astype(BF)
 
     times_t(e_ref, bufs.at[1], put_mixed)
-    wait_all(out)
-    wait_all(more)
-
-
-def cross_query_grad(place, a2, dq2, x1, dx2, mixed, vec, keep, send, packs):
+
+
+def cross_query_grad(place, dq2, x1, dx2, vec, packs):
     rows, width = x1.shape
+    low = shape((rows, width), BF)
     return call(
         cross_query_grad_kernel,
         packs,
-        [place, a2, dq2, x1, dx2, mixed, vec, keep, send],
-        out_shape=[
-            shape((rows, width), F32), shape((rows, width), BF), shape((4, width), F32),
-            shape(keep.shape, BF), shape(send.shape, BF),
+        [place, dq2, x1, dx2, vec],
+        out_shape=[shape((rows, width), F32), low, low, shape((3, width), F32)],
+        in_specs=[smem()] + [vmem()] * 4,
+        out_specs=[vmem()] * 4,
+        scratch_shapes=[
+            pltpu.VMEM((2, 32, 32, width), BF), pltpu.VMEM((rows, width), F32), pltpu.SemaphoreType.DMA((2,)),
         ],
-        in_specs=[smem()] + [vmem()] * 6 + [hbm()] * 2,
-        out_specs=[vmem()] * 3 + [hbm()] * 2,
-        scratch_shapes=[
-            pltpu.VMEM((2, 32, 32, width), BF), pltpu.VMEM((rows, width), F32), pltpu.VMEM((rows, width), BF),
-            pltpu.VMEM((2, 8, 4, 32, width), BF), pltpu.SemaphoreType.DMA((2,)), pltpu.SemaphoreType.DMA((2, 8)),
+        compiler_params=params(),
+        cost_estimate=cost(4 * rows * width * width, 14 * MIB),
+        name="cross_query_grad",
+    )
+
+
+def weight_grads_kernel(jobs, lefts, rights, place_ref, *refs):
+    count = 2 * (lefts + rights)
+    one_away, two_away, one_mine, two_mine = refs[count : count + 4]
+    held, (grads, in_sems, sems) = refs[count + 4 : 2 * count + 4], refs[2 * count + 4 :]
+    order = []
+    for left, right, _ in jobs:
+        order += [n for n in (2 * left, 2 * (lefts + right), 2 * left + 1, 2 * (lefts + right) + 1) if n not in order]
+    pending = {n: pltpu.make_async_copy(refs[n], held[n], in_sems.at[n]) for n in order}
+    start_all(pending.values())
+
+    def ready(n):
+        if n in pending:
+            pending.pop(n).wait()
+        return held[n]
+
+    core = jnp.bitwise_and(place_ref[0], 1)
+    plane = lax.shift_right_logical(place_ref[0], 1)
+    split = len(jobs) // 2
+    width = one_mine.shape[3]
+    copies = []
+    for pair in ((3, 1), (2, 0)):
+        starts = [pl.multiple_of((jnp.bitwise_xor(plane, j) * 2 + core) * 128, 128) for j in pair]
+        turned = {}
+        for k, (left, right, block) in enumerate(jobs):
+            wide = slice(block * width, (block + 1) * width)
+            total = None
+            for side in range(2):
+                act, grad = ready(2 * left + side), ready(2 * (lefts + right) + side)
+                if (left, side) not in turned:
+                    columns = jnp.concatenate([act[:, pl.ds(start, 128)] for start in starts], axis=1)
+                    turned[left, side] = columns.T
+                value = dot(turned[left, side], grad[:, wide])
+                total = value if total is None else total + value
+            rounded = total.astype(BF).reshape((2,) + grads.shape[2:])
+            lines = pl.ds(32 * (k % split), 32)
+            for n, j in enumerate(pair):
+                grads[k, j] = rounded[n]
+                y, x = j // 2, j % 2
+                if k < split:
+                    target = (one_away if x else one_mine).at[y, :, lines, :]
+                else:
+                    target = (two_away if y else two_mine).at[x, :, lines, :]
+                copies.append(pltpu.make_async_copy(grads.at[k, j], target, sems.at[k, j]))
+                copies[-1].start()
+    wait_all(copies)
+
+
+def weight_grads(place, lefts, rights, jobs):
+    width = lefts[0][0].shape[1]
+    count = len(jobs)
+    blocks = shape((2, 4, 16 * count, width), BF)
+    operands = [value for pair in lefts + rights for value in pair]
+    flops = sum(4 * lefts[left][0].shape[0] * width * width // 2 for left, _, _ in jobs)
+    return pl.pallas_call(
+        functools.partial(weight_grads_kernel, jobs, len(lefts), len(rights)),
+        out_shape=[blocks] * 4,
+        in_specs=[smem()] + [hbm()] * len(operands),
+        out_specs=[hbm()] * 4,
+        scratch_shapes=[pltpu.VMEM(value.shape, BF) for value in operands] + [
+            pltpu.VMEM((count, 4, 4, 32, width), BF), pltpu.SemaphoreType.DMA((len(operands),)),
+            pltpu.SemaphoreType.DMA((count, 4)),
         ],
-        input_output_aliases={7: 3, 8: 4},
         compiler_params=params(),
-        cost_estimate=cost(8 * rows * width * width, 20 * MIB),
-        name="cross_query_grad",
-    )
-
-
-def cross_key_grad_kernel(place_ref, e_ref, dk_ref, dv_ref, keep_in, send_in, sums_ref, keep, send, grads, sems):
-    copies = []
-    for n, ref in enumerate((dk_ref, dv_ref)):
-        grad_weight(e_ref, ref, grads.at[n])
-        out = block_copies(place_ref[0], grads.at[n], keep, send, 96 + 32 * n, sems.at[n])
-        start_all(out)
-        copies += out
-    sums_ref[...] = column_sum(dv_ref)
-    wait_all(copies)
-
-
-def cross_key_grad(place, enc, dk2, dv2, keep, send):
-    frames, width = enc.shape
-    return pl.pallas_call(
-        cross_key_grad_kernel,
-        out_shape=[shape((1, width), F32), shape(keep.shape, BF), shape(send.shape, BF)],
-        in_specs=[smem()] + [vmem()] * 3 + [hbm()] * 2,
-        input_output_aliases={4: 1, 5: 2},
-        out_specs=[vmem()] + [hbm()] * 2,
-        scratch_shapes=[pltpu.VMEM((2, 8, 4, 32, width), BF), pltpu.SemaphoreType.DMA((2, 8))],
-        compiler_params=params(),
-        cost_estimate=cost(4 * frames * width * width, 14 * MIB),
-        name="cross_key_grad",
-    )(place, enc, dk2, dv2, keep, send)
+        cost_estimate=cost(flops, 12 * MIB),
+        name="weight_grads",
+    )(place, *operands)
 
 
 def encoder_grad_kernel(frames, place_ref, dk_ref, dv_ref, one, two, out_ref, bufs, sems):
@@ -692,33 +683,6 @@
         cost_estimate=cost(4 * frames * width * width, 16 * MIB),
         name="encoder_grad",
     )
-
-
-def self_weight_grad_kernel(place_ref, a_ref, dq_ref, dk_ref, dv_ref, sums_ref, keep, send, grads, sems):
-    out = []
-    for n, ref in enumerate((dq_ref, dk_ref, dv_ref)):
-        grad_weight(a_ref, ref, grads.at[n])
-        more = block_copies(place_ref[0], grads.at[n], keep, send, 32 * n, sems.at[n])
-        start_all(more)
-        out += more
-    sums_ref[0:1, :] = column_sum(dq_ref)
-    sums_ref[1:2, :] = column_sum(dv_ref)
-    wait_all(out)
-
-
-def self_weight_grad(place, a1, dq1, dk1, dv1):
-    rows, width = a1.shape
-    blocks = shape((4, 4, 160, width), BF)
-    return pl.pallas_call(
-        self_weight_grad_kernel,
-        out_shape=[shape((2, width), F32), blocks, blocks],
-        in_specs=[smem()] + [vmem()] * 4,
-        out_specs=[vmem()] + [hbm()] * 2,
-        scratch_shapes=[pltpu.VMEM((3, 8, 4, 32, width), BF), pltpu.SemaphoreType.DMA((3, 8))],
-        compiler_params=params(),
-        cost_estimate=cost(6 * rows * width * width, 10 * MIB),
-        name="self_weight_grad",
-    )(place, a1, dq1, dk1, dv1)
 
 
 def self_in_grad_kernel(
@@ -844,30 +808,54 @@
     return jnp.bitwise_and(place_ref[1] + k, 3)
 
 
-def reduce_chain(place, keep, send):
-    rows, columns = keep.shape[2:]
-    half = rows // 2
+def swap_chain(values):
+    moved = yield [(value, "c", SWAP) for value in values]
+    return list(zip(values, moved))
+
+
+NEAR = [(0, 1), (1, 0), (2, 3), (3, 2)]
+FAR = [(0, 2), (2, 0), (1, 3), (3, 1)]
+
+
+def pick_z(both, k):
+    return lax.dynamic_index_in_dim(both, jnp.bitwise_xor(lax.axis_index("z"), k), 0, keepdims=False)
+
+
+def z_halves(both):
+    away, mine = (jnp.stack([pick_z(both, k), pick_z(both, k ^ 2)]) for k in (1, 0))
+    return (yield from z_two(away, mine))
+
+
+def z_two(away, mine):
+    (moved,) = yield [(away, "z", NEAR)]
+    near = mine[0].astype(F32) + moved[0].astype(F32)
+    (moved,) = yield [(add_rounded(mine[1], moved[1]), "z", FAR)]
+    return near + moved.astype(F32)
+
+
+def reduce_chain(place, halving, one, two, *mine):
+    half, columns = one.shape[2:]
+    rows = 2 * half
     parts = [pl.ds(0, half), pl.ds(half, half)]
-    (moved,) = yield [(send, "c", SWAP)]
-
-    def plan_one(_):
-        out = []
-        for plane in (3, 1, 2, 0):
-            y, x = plane // 2, plane % 2
-            out.append((0, (plane, slice(None), parts[0]), 0 if x else 2, y))
-            out.append((0, (plane, slice(None), parts[1]), 1 if y else 3, x))
-        return out
-
-    outs = [(2, 4, half, columns)] * 4
-    one, two, *mine = add_pieces(place, [keep], [moved], outs, (4, half, columns), plan_one, 8)
     moved = yield [(one, "x", SWAP), (two, "y", SWAP)]
 
     def plan_two(_):
         return [(n, side, n if side else 2 + n, slice(None)) for side in (1, 0) for n in range(2)]
 
     outs = [(4, half, columns)] * 4
-    one, two, *mine = add_pieces(place, mine, list(moved), outs, (4, half, columns), plan_two, 4)
+    one, two, *mine = add_pieces(place, list(mine), list(moved), outs, (4, half, columns), plan_two, 4)
     moved = yield [(one, "y", SWAP), (two, "x", SWAP)]
+
+    if halving:
+
+        def plan_halves(place_ref):
+            turns = [(1, 0, 0), (3, 0, 1), (2, 1, 1), (0, 1, 0)]
+            return [
+                (n, jnp.bitwise_xor(place_ref[1], turn), out, (at, parts[n])) for turn, out, at in turns for n in range(2)
+            ]
+
+        outs = [(2, rows, columns)] * 2
+        return (yield from z_two(*add_pieces(place, mine, list(moved), outs, (half, columns), plan_halves, 8)))
 
     def plan_three(place_ref):
         return [(n, turn_z(place_ref, k), k, parts[n]) for k in (2, 1, 3, 0) for n in range(2)]
@@ -877,31 +865,9 @@
     return functools.reduce(jnp.add, [value.astype(F32) for value in moved], pieces[0].astype(F32))
 
 
-def z_chain(both):
-    here = lax.axis_index("z")
-
-    def piece(k):
-        return lax.dynamic_index_in_dim(both, lax.rem(here + k, 4), 0, keepdims=False)
-
-    moved = yield [(piece(k), "z", turns()[k]) for k in (1, 3, 2)]
-    return functools.reduce(jnp.add, [value.astype(F32) for value in moved], piece(0).astype(F32))
-
-
-def reduce_plain(keep, send):
-    count = lax.axis_size(ALL)
-    rows, columns = keep.shape[2:]
-    total = jnp.stack([keep, send], axis=1).reshape(32, rows, columns)
-    many = rows // 32
-    total = total.reshape(32, many, 32, columns).swapaxes(0, 1).reshape(many, 1024, columns)
-    mine = lax.psum_scatter(total.astype(F32), ALL, scatter_dimension=1, tiled=True)
-    return mine.reshape(many * (1024 // count), columns)
-
-
-def reduce_feed_plain(grad):
-    columns = grad.shape[3]
-    grad1 = grad[:, :, :128].reshape(32, 4, 32, columns).swapaxes(1, 2).reshape(1024, 4 * columns)
-    grad2 = grad[:, :, 128:].reshape(4096, columns)
-    return [lax.psum_scatter(g.astype(F32), ALL, scatter_dimension=0, tiled=True) for g in (grad1, grad2)]
+def reduce_feed_plain(grad1, grad2):
+    grad2 = grad2.reshape(-1, grad2.shape[3])
+    return [lax.psum_scatter(g, ALL, scatter_dimension=0, tiled=True) for g in (grad1, grad2)]
 
 
 def table_chain(table):
@@ -913,10 +879,8 @@
     for axis in ("c", "x", "y"):
         moved = yield [(table, axis, SWAP)]
         table = combine(table, moved[0])
-    for pairs in ([(0, 1), (1, 0), (2, 3), (3, 2)], [(0, 2), (2, 0), (1, 3), (3, 1)]):
-        moved = yield [(table, "z", pairs)]
-        table = combine(table, moved[0])
-    return table
+    moved = yield [(table, "z", turns()[k]) for k in (1, 3, 2)]
+    return functools.reduce(combine, moved, table)
 
 
 def vector_table(pack, row, rows, shard_cols):
@@ -932,7 +896,7 @@
 
 def gather_fast(attention, expand, contract, vectors):
     width = attention.shape[2]
-    line = jnp.pad(vectors.reshape(1, -1), ((0, 15), (0, width - vectors.size)))
+    line = jnp.pad(vectors.reshape(1, -1), ((0, 7), (0, width - vectors.size)))
     shard = jnp.concatenate([attention[m] for group in MATRICES for m in group] + [line], axis=0)
     pack = lax.all_gather(shard, ALL, axis=0, tiled=False)
     pack_f = lax.all_gather(feed_shard(expand, contract), ALL, axis=0, tiled=False)
@@ -967,11 +931,11 @@
     return (first_new, second_new, master_new)
 
 
-def table_kernel(sums1, bias1, sums2, sums3, sums_v, gb1, gb2, top1, top2, out):
+def table_kernel(sums1, bias1, sums2, bias2, sums3, gb1, gb2, top1, top2, out):
     out[...] = jnp.zeros_like(out)
     rows = [
-        sums1[0:1, :], sums1[1:2, :], sums2[1:2, :], sums2[2:3, :], sums3[0:1, :], sums3[1:2, :],
-        bias1[0:1, :], bias1[1:2, :], sums2[3:4, :], sums2[0:1, :], sums_v[...], sums3[2:3, :], gb2[...],
+        sums1[0:1, :], sums1[1:2, :], sums2[0:1, :], sums2[1:2, :], sums3[0:1, :], sums3[1:2, :],
+        bias1[0:1, :], bias1[1:2, :], sums2[2:3, :], bias2[0:1, :], bias2[1:2, :], sums3[2:3, :], gb2[...],
     ]
     for n, row in enumerate(rows):
         out[n : n + 1, :] = row
@@ -1010,19 +974,19 @@
     k2, v2 = cross_in(place, enc, vec, [two_a, two_b])
     o2, lse2, top2 = attend(q2, k2, v2, False, frames)
     x2, a3 = cross_out(place, o2, x1, vec, [two_b])
-    result, df, gb1, gb2, grad = feed(a3, x2, cot, vec, pack_f)
-    da3, grad = feed_grad(a3, df, grad, pack_f)
-    dx2, do2, sums3, keep1, send1 = cross_out_grad(place, da3, x2, cot, o2, vec, [two_b])
-    dq2, dk2, dv2 = attend_grad(q2, k2, v2, o2, do2, lse2, False, frames)
-    dx1, do1, sums2, keep1, send1 = cross_query_grad(place, a2, dq2, x1, dx2, o1, vec, keep1, send1, [two_a, one_b])
-    dq1, dk1, dv1 = attend_grad(q1, k1, v1, o1, do1, lse1, True, rows)
-    bias1, keep2, send2 = self_weight_grad(place, a1, dq1, dk1, dv1)
-    sums_v, keep2, send2 = cross_key_grad(place, enc, dk2, dv2, keep2, send2)
+    result, df, gb1, gb2, grad2 = feed(a3, x2, cot, vec, pack_f)
+    da3 = feed_grad(df, pack_f)
+    dx2, do2, e2, sums3 = cross_out_grad(place, da3, x2, cot, vec, [two_b])
+    dq2, dk2, dv2, bias2 = attend_grad(q2, k2, v2, o2, do2, lse2, False, frames)
+    dx1, do1, e1, sums2 = cross_query_grad(place, dq2, x1, dx2, vec, [two_a, one_b])
+    dq1, dk1, dv1, bias1 = attend_grad(q1, k1, v1, o1, do1, lse1, True, rows)
     grad_input, sums1 = self_in_grad(place, dq1, dk1, dv1, x, dx1, vec, [one_a, one_b])
     grad_encoder = encoder_grad(place, dk2, dv2, [two_a, two_b], frames).reshape(frames, width)
-    table = vector_table_of(sums1, bias1, sums2, sums3, sums_v, gb1, gb2, top1, top2)
-    g_vectors, maxima = table[:VEC_ROWS], maxima_of(table)
-    return result, grad_input, grad_encoder, g_vectors, maxima, [(grad,), (keep1, send1), (keep2, send2)]
+    table = vector_table_of(sums1, bias1, sums2, bias2, sums3, gb1, gb2, top1, top2)
+    pairs = ((a1, dq1), (a1, dk1), (a1, dv1), (o1, e1), (a2, dq2), (enc, dk2), (enc, dv2), (o2, e2))
+    g_attention = jnp.stack([dot_tn(left, right) for left, right in pairs])
+    sums = [dot_tn(a3, df), grad2.astype(F32), g_attention]
+    return result, grad_input, grad_encoder, table[:VEC_ROWS], maxima_of(table), sums
 
 
 def gradients_plain(inputs, encoder, cotangent, owned):
@@ -1036,10 +1000,8 @@
     result, grad_input, grad_encoder = (jnp.stack([d[k] for d in done]) for k in range(3))
     g_vectors = functools.reduce(jnp.add, [d[3] for d in done])
     maxima = functools.reduce(jnp.maximum, [d[4] for d in done])
-    both = done[0][5]
-    for d in done[1:]:
-        both = [tuple(add_rounded(a, b) for a, b in zip(p, q)) for p, q in zip(both, d[5])]
-    sums = reduce_feed_plain(*both[0]) + [reduce_plain(*p) for p in both[1:]]
+    grad1, grad2, g_attention = (functools.reduce(jnp.add, values) for values in zip(*[d[5] for d in done]))
+    sums = reduce_feed_plain(grad1, grad2) + [lax.psum_scatter(g_attention, ALL, scatter_dimension=1, tiled=True)]
     g_vectors = lax.psum_scatter(g_vectors, ALL, scatter_dimension=1, tiled=True)
     return result, grad_input, grad_encoder, sums, g_vectors, lax.pmax(maxima, ALL)
 
@@ -1063,49 +1025,82 @@
     o2, lse2, top2 = attend(q2, k2, v2, False, frames)
     x2, a3 = cross_out(place, o2, x1, vec, [two_b])
 
-    result, df, gb1, gb2, grad = feed(a3, x2, cot, vec, pack_f)
-    da3, grad = feed_grad(a3, df, grad, pack_f)
-    rf = lax.psum_scatter(grad, ("y", "x", "c"), scatter_dimension=0, tiled=True)[0]
-    rf = lax.psum_scatter(rf, "z", scatter_dimension=0, tiled=True)[0].astype(F32)
-    dx2, do2, sums3, keep, send = cross_out_grad(place, da3, x2, cot, o2, vec, [two_b])
-    dq2, dk2, dv2 = attend_grad(q2, k2, v2, o2, do2, lse2, False, frames)
-    dx1, do1, sums2, keep, send = cross_query_grad(place, a2, dq2, x1, dx2, o1, vec, keep, send, [two_a, one_b])
-    r1 = Unit(reduce_chain(place, keep, send))
-    dq1, dk1, dv1 = step(
-        lambda do1: attend_grad(q1, k1, v1, o1, do1, lse1, True, rows), [do1], start=[r1], finish=[r1]
-    )
-    bias1, keep, send = step(
-        lambda dq1, dk1, dv1: self_weight_grad(place, a1, dq1, dk1, dv1), [dq1, dk1, dv1], start=[r1]
-    )
-    sums_v, keep, send = step(
-        lambda dk2: cross_key_grad(place, enc, dk2, dv2, keep, send), [dk2], finish=[r1]
-    )
-    r2 = Unit(reduce_chain(place, keep, send))
-    grad_input, sums1 = step(
-        lambda dq1, dk1, dv1: self_in_grad(place, dq1, dk1, dv1, x, dx1, vec, [one_a, one_b]),
-        [dq1, dk1, dv1],
-        start=[r1, r2],
-        finish=[r1, r2],
-    )
-    table = Unit(table_chain(vector_table_of(sums1, bias1, sums2, sums3, sums_v, gb1, gb2, top1, top2)))
+    acts = Unit(swap_chain([a3, a1, o1, a2, o2, enc]))
+    (x2,) = step(lambda x2: (x2,), [x2], start=[acts], finish=[acts])
+    a3, a1, o1, a2, o2, enc = acts.result
+
+    result, df, gb1, gb2, grad2 = feed(a3[0], x2, cot, vec, pack_f)
+    plane_2 = lax.psum_scatter(grad2, ("y", "x", "c"), scatter_dimension=0, tiled=True)[0]
+    swap_df = Unit(swap_chain([df]))
+    da3 = step(lambda df: feed_grad(df, pack_f), [df], start=[swap_df], finish=[swap_df])
+    f1 = Unit(reduce_chain(place, True, *weight_grads(place, [a3], swap_df.result, [(0, 0, k) for k in range(4)])))
+
+    def cross_back(da3):
+        dx2, do2, e2, sums3 = cross_out_grad(place, da3, x2, cot, vec, [two_b])
+        swap = Unit(swap_chain([e2]))
+        out = step(
+            lambda do2: attend_grad(q2, k2, v2, o2[0], do2, lse2, False, frames), [do2], start=[swap], finish=[swap]
+        )
+        return dx2, swap.result, sums3, *out
+
+    dx2, swap_e2, sums3, dq2, dk2, dv2, bias2 = step(cross_back, [da3], start=[f1], finish=[f1])
+    swap_2 = Unit(swap_chain([dq2, dk2, dv2]))
+    dx1, do1, e1, sums2 = step(
+        lambda dx2: cross_query_grad(place, dq2, x1, dx2, vec, [two_a, one_b]),
+        [dx2],
+        start=[swap_2],
+        finish=[swap_2],
+    )
+    swap_e1 = Unit(swap_chain([e1]))
+    rights = swap_2.result + swap_e2
+    blocks = step(
+        lambda *rights: weight_grads(
+            place, [enc, a2, o2], [rights[k : k + 2] for k in range(0, 8, 2)], ((0, 1, 0), (1, 0, 0), (0, 2, 0), (2, 3, 0))
+        ),
+        [value for pair in rights for value in pair],
+        start=[swap_e1, f1],
+        finish=[swap_e1, f1],
+    )
+    r1 = Unit(reduce_chain(place, True, *blocks))
+    f2 = Unit(z_halves(plane_2))
+    dq1, dk1, dv1, bias1 = step(
+        lambda do1: attend_grad(q1, k1, v1, o1[0], do1, lse1, True, rows),
+        [do1],
+        start=[r1, f1, f2],
+        finish=[r1, f1, f2],
+    )
+    swap_1 = Unit(swap_chain([dq1, dk1, dv1]))
+    step(start=[swap_1], finish=[swap_1])
+    rights = swap_e1.result + swap_1.result
+    blocks = step(
+        lambda *rights: weight_grads(
+            place, [o1, a1], [rights[k : k + 2] for k in range(0, 8, 2)], ((0, 0, 0), (1, 1, 0), (1, 2, 0), (1, 3, 0))
+        ),
+        [value for pair in rights for value in pair],
+        start=[r1, f1],
+        finish=[r1, f1],
+    )
+    r2 = Unit(reduce_chain(place, False, *blocks))
+
+    def last(dx1, dk2):
+        grad_input, sums1 = self_in_grad(place, dq1, dk1, dv1, x, dx1, vec, [one_a, one_b])
+        return grad_input, sums1, encoder_grad(place, dk2, dv2, [two_a, two_b], frames)
+
+    grad_input, sums1, grad_encoder = step(last, [dx1, dk2], start=[r2, r1, f2], finish=[r2, r1, f2])
+    table = Unit(table_chain(vector_table_of(sums1, bias1, sums2, bias2, sums3, gb1, gb2, top1, top2)))
     step(start=[table], finish=[table])
-    grad_encoder = step(
-        lambda dk2: encoder_grad(place, dk2, dv2, [two_a, two_b], frames),
-        [dk2],
-        start=[r1, r2],
-        finish=[r1, r2],
-    )
+    step(start=[r2, r1, table], finish=[r2, r1, table])
     step(start=[r2, table], finish=[r2, table])
-    step(start=[r2, table], finish=[r2, table])
-    step(start=[table], finish=[table])
     step(start=[table], finish=[table])
     total = table.result
     shard_cols = vectors.shape[1]
     g_vectors = lax.dynamic_slice_in_dim(total[:VEC_ROWS], lax.axis_index(ALL) * shard_cols, shard_cols, 1)
     maxima = maxima_of(total)
     grad_encoder = grad_encoder.reshape(1, frames, width)
-    g_expand = rf[:128].reshape(4, 32, width).swapaxes(0, 1).reshape(32, 4 * width)
-    sums = [g_expand, rf[128:], r1.result, r2.result]
+    g_expand = f1.result.reshape(4, 32, width).swapaxes(0, 1).reshape(32, 4 * width)
+    cross, own = (value.reshape(4, 32, width) for value in (r1.result, r2.result))
+    g_attention = jnp.concatenate([own[1:], own[:1], cross[1:2], cross[:1], cross[2:]], axis=0)
+    sums = [g_expand, f2.result, g_attention]
     return result[None], grad_input[None], grad_encoder, sums, g_vectors, maxima
 
 
@@ -1127,13 +1122,10 @@
     contract_second,
     vectors_second,
 ):
-    width = inputs.shape[2]
     owned = [m.astype(BF) for m in (attention_master, expand_master, contract_master, vectors_master)]
     compute = gradients_fast if fast and inputs.shape[0] == 1 else gradients_plain
     result, grad_input, grad_encoder, sums, g_vectors, maxima = compute(inputs, encoder, cotangent, owned)
-    g_expand, g_contract = sums[:2]
-    out_query, rest = (value.reshape(-1, attention_master.shape[1], width) for value in sums[2:])
-    g_attention = jnp.concatenate([rest[:3], out_query[:2], rest[3:], out_query[2:]], axis=0)
+    g_expand, g_contract, g_attention = sums
     shard_cols = vectors_master.shape[1]
     first_col = lax.axis_index(ALL) * shard_cols
 

time: 574 us -> 558 us (0.972); the launches traced: 571 us -> 549 us
  waiting for transfers between devices: 249 us -> 219 us
  starting transfers between devices: 19.7 us -> 34.2 us
  local copies, waits for them, and re-layouts: 28.2 us -> 21.1 us
  Pallas kernels: 247 us -> 241 us
    ppermute x21 -> x42, waiting for transfers between devices: 83.5 us -> 67.1 us  [step(): lax.ppermute(v, axis, pairs)]
    ppermute x21 -> x42, starting transfers between devices: 19.4 us -> 34.1 us  [step(): lax.ppermute(v, axis, pairs)]
    all_gather x1, waiting for transfers between devices: 46.4 us -> 36.5 us  [gather_fast(): lax.all_gather(feed_shard(expand, contract), ALL, axis=0, tiled=False)]
    pallas_call x8, Pallas kernels: 82 us -> 72.5 us  [call(): pl.pallas_call(body, in_specs=specs, **settings)]
    unnamed x128 -> x142, local copies, waits for them, and re-layouts: 21.7 us -> 13.9 us
    pallas_call x3 -> x4, Pallas kernels: 39.6 us -> 46 us  [the longest x3 37.3 us: weight_grads(): pl.pallas_call(functools.partial(weight_grads_kernel, jobs, len(lefts), l...]
  transfers between devices with their start and end apart: 25 -> 45, of which waited for: 15 -> 16; matrix products, arithmetic and copies ran while one was open for 2% -> 3% of each run, Pallas kernels for 37% -> 38%
where the time goes in v3:
time: 558 us; the launch traced here: 549 us
  Pallas kernels  241 us (43%)
  waiting for transfers between devices  219 us (39%)
  starting transfers between devices  34.2 us (6%)
  local copies, waits for them, and re-layouts  21.1 us (4%)
  other arithmetic  18 us (3%)
  between operations  15.4 us (3%)
    all_gather x1, waiting for transfers between devices, gather_fast(): pack = lax.all_gather(shard, ALL, axis=0, tiled=False)  116 us
    pallas_call x8, Pallas kernels, call(): pl.pallas_call(body, in_specs=specs, **settings)  72.5 us
    ppermute x42, waiting for transfers between devices, step(): lax.ppermute(v, axis, pairs)  67.1 us
    pallas_call x2, Pallas kernels, attend_grad(): pl.pallas_call(functools.partial(attend_grad_kernel, causal, valid), grid...  45.5 us
    pallas_call x3, Pallas kernels, weight_grads(): pl.pallas_call(functools.partial(weight_grads_kernel, jobs, len(lefts), l...  37.3 us
    all_gather x1, waiting for transfers between devices, gather_fast(): lax.all_gather(feed_shard(expand, contract), ALL, axis=0, tiled=False)  36.5 us
    ppermute x42, starting transfers between devices, step(): lax.ppermute(v, axis, pairs)  34.1 us
    pallas_call x2, Pallas kernels, attend(): pl.pallas_call(functools.partial(attend_kernel, causal, valid), grid=(pai...  29.7 us
  transfers between devices with their start and end apart: 45, of which 16 were waited for; matrix products, arithmetic and copies ran while one was open for 3% of the time, Pallas kernels for 38%

profile of v3, /device:TPU:0, one launch (start us, length us, event | category | flops | bytes accessed | tf_op | source)
XLA Modules:
  0.0 548.9 jit_solution(18187132315106362542)
XLA Ops:
  11.5 4.0 pad.9.refs_1_.refs_0_
  15.6 115.8 %all-gather.5.cloned.1.call-done = bf16[8448,1024]{1,0:T(8,128)(2,1)} async-done(((bf16[264,1024]{1,0:T(8,128)(2,1)}), bf16[8448,1024]{1,0:T(8,128)(2,1)}) %all-gather.5.cloned.1.call-update) | async-done | bytes 17301520 | tf_op jit(solution)/shard_map/all_gather | solution.py:901
  133.0 6.4 %self_in.1 = (bf16[448,1024]{1,0:T(8,128)(2,1)}, bf16[448,1024]{1,0:T(8,128)(2,1)S(1)}, bf16[448,1024]{1,0:T(8,128)(2,1)S(1)}, bf16[448,1024]{1,0:T(8,128)(2,1)S(1)}) custom-call(s32[2]{0:T(128)S(1)} %pad_add_fusion.refs_0_.place_ref, bf16[448,1024]{1,0:T(8,128)(2,1)S(1)} %bitcast.99, ...), custom_call_target="tpu_custom_call" | custom-call | flops 2818572288 | bytes 10485760 | tf_op jit(solution)/shard_map/self_in/pallas_call | solution.py:86
  139.4 8.9 %attend_causal.1 = (bf16[448,1024]{1,0:T(8,128)(2,1)}, f32[8,1,896]{2,1,0:T(1,128)S(1)}, f32[8,1,128]{2,1,0:T(1,128)S(1)}) custom-call(bf16[448,1024]{1,0:T(8,128)(2,1)S(1)} %get-tuple-element.230.q_ref, bf16[448,1024]{1,0:T(8,128)(2,1)S(1)} %get-tuple-element.231.k_ref, bf16[448,1024]{1,0:T(8,128)(2,1)S(1)} %get-tuple-element.232.v_ref), custom_call_target="tpu_custom_call" | custom-call | flops 3288334336 | bytes 1835008 | tf_op jit(solution)/shard_map/attend_causal/pallas_call | solution.py:249
  149.5 6.3 %self_out.1 = (f32[448,1024]{1,0:T(8,128)S(1)}, bf16[448,1024]{1,0:T(8,128)(2,1)}, bf16[448,1024]{1,0:T(8,128)(2,1)S(1)}) custom-call(s32[2]{0:T(128)S(1)} %pad_add_fusion.refs_0_.place_ref, bf16[448,1024]{1,0:T(8,128)(2,1)} %get-tuple-element.246.refs_1_.o_ref.refs_0_, bf16[448,1024]{1,0:T(8,128)(2,1)S(1)} %bitcast.100, ...), custom_call_target="tpu_custom_call" | custom-call | flops 1879048192 | bytes 10485760 | tf_op jit(solution)/shard_map/self_out/pallas_call | solution.py:86
  155.8 13.2 %cross_in.1 = (bf16[1504,1024]{1,0:T(8,128)(2,1)S(1)}, bf16[1504,1024]{1,0:T(8,128)(2,1)}) custom-call(s32[2]{0:T(128)S(1)} %pad_add_fusion.refs_0_.place_ref, bf16[1504,1024]{1,0:T(8,128)(2,1)} %pad.9.refs_1_.refs_0_, f32[17,1024]{1,0:T(8,128)S(1)} %convert_element_type.134.refs_2_.refs_3_.vec_ref.refs_4_.refs_6_, bf16[32,264,1024]{2,1,0:T(8,128)(2,1)} %bitcast.106, ...), custom_call_target="tpu_custom_call" | custom-call | flops 6308233216 | bytes 14680064 | tf_op jit(solution)/shard_map/cross_in/pallas_call | solution.py:86
  169.0 20.8 %attend.1 = (bf16[448,1024]{1,0:T(8,128)(2,1)S(1)}, f32[8,1,896]{2,1,0:T(1,128)S(1)}, f32[8,1,128]{2,1,0:T(1,128)S(1)}) custom-call(bf16[448,1024]{1,0:T(8,128)(2,1)S(1)} %get-tuple-element.234.q_ref, bf16[1504,1024]{1,0:T(8,128)(2,1)S(1)} %get-tuple-element.235.k_ref, bf16[1504,1024]{1,0:T(8,128)(2,1)} %get-tuple-element.236.v_ref), custom_call_target="tpu_custom_call" | custom-call | flops 11039408128 | bytes 6160384 | tf_op jit(solution)/shard_map/attend/pallas_call | solution.py:249
  197.5 5.3 collective-permute-done.refs_1_
  211.6 36.5 %all-gather.7.cloned.1.call-done = bf16[8192,1024]{1,0:T(8,128)(2,1)} async-done(((bf16[256,1024]{1,0:T(8,128)(2,1)}), bf16[8192,1024]{1,0:T(8,128)(2,1)}) %all-gather.7.cloned.1.call-update) | async-done | bytes 16777232 | tf_op jit(solution)/shard_map/all_gather | solution.py:902
  248.1 24.5 %feed.1 = (bf16[448,1024]{1,0:T(8,128)(2,1)}, bf16[448,4096]{1,0:T(8,128)(2,1)}, f32[8,1,512]{2,1,0:T(1,128)}, f32[1,1024]{1,0:T(1,128)}, bf16[8,4,128,1024]{3,2,1,0:T(8,128)(2,1)}) custom-call(bf16[448,1024]{1,0:T(8,128)(2,1)} %copy-done.13, f32[448,1024]{1,0:T(8,128)} %copy-done.3, bf16[448,1024]{1,0:T(8,128)(2,1)} %bitcast.128, f32[17,1024]{1,0:T(8,128)} %copy-done.2, ...), custom_call_target="tpu_custom_call" | custom-call | flops 15032385536 | bytes 31457280 | tf_op jit(solution)/shard_map/feed/pallas_call | solution.py:393
  273.0 8.8 %feed_grad.1.refs_1_ = f32[448,1024]{1,0:T(8,128)} custom-call(bf16[448,4096]{1,0:T(8,128)(2,1)} %get-tuple-element.254.df_ref.refs_2_, bf16[32,256,1024]{2,1,0:T(8,128)(2,1)} %bitcast.118), custom_call_target="tpu_custom_call" | custom-call | flops 3758096384 | bytes 12582912 | tf_op jit(solution)/shard_map/feed_grad/pallas_call | solution.py:434
  283.8 11.4 %weight_grads.3 = (bf16[2,4,64,1024]{3,2,1,0:T(8,128)(2,1)}, bf16[2,4,64,1024]{3,2,1,0:T(8,128)(2,1)}, bf16[2,4,64,1024]{3,2,1,0:T(8,128)(2,1)}, bf16[2,4,64,1024]{3,2,1,0:T(8,128)(2,1)}) custom-call(s32[2]{0:T(128)} %copy-done.5, bf16[448,1024]{1,0:T(8,128)(2,1)} %copy-done.13, bf16[448,1024]{1,0:T(8,128)(2,1)} %copy-done.60, ...), custom_call_target="tpu_custom_call" | custom-call | flops 3758096384 | bytes 12582912 | tf_op jit(solution)/shard_map/weight_grads/pallas_call | solution.py:639
  295.2 7.2 %cross_out_grad.1 = (f32[448,1024]{1,0:T(8,128)}, bf16[448,1024]{1,0:T(8,128)(2,1)}, bf16[448,1024]{1,0:T(8,128)(2,1)}, f32[3,1024]{1,0:T(4,128)}) custom-call(s32[2]{0:T(128)} %copy-done.5, f32[448,1024]{1,0:T(8,128)} %feed_grad.1.refs_1_, f32[448,1024]{1,0:T(8,128)} %copy-done.3, bf16[448,1024]{1,0:T(8,128)(2,1)} %bitcast.129, f32[17,1024]{1,0:T(8,128)} %copy-done.2, ...), custom_call_target="tpu_custom_call" | custom-call | flops 939524096 | bytes 10485760 | tf_op jit(solution)/shard_map/cross_out_grad/pallas_call | solution.py:86
  305.0 32.2 %attend_grad.1 = (bf16[448,1024]{1,0:T(8,128)(2,1)}, bf16[1504,1024]{1,0:T(8,128)(2,1)}, bf16[1504,1024]{1,0:T(8,128)(2,1)}, f32[2,1024]{1,0:T(2,128)}) custom-call(bf16[448,1024]{1,0:T(8,128)(2,1)} %copy-done.12, bf16[1504,1024]{1,0:T(8,128)(2,1)} %copy-done.8, bf16[1504,1024]{1,0:T(8,128)(2,1)} %get-tuple-element.236.v_ref, bf16[448,1024]{1,0:T(8,128)(2,1)} %copy-done.4, ...), custom_call_target="tpu_custom_call" | custom-call | flops 27598520320 | bytes 12320768 | tf_op jit(solution)/shard_map/attend_grad/pallas_call | solution.py:526
  337.2 5.9 %collective-permute-done.8.refs_2_ = bf16[2,4,64,1024]{3,2,1,0:T(8,128)(2,1)S(1)} collective-permute-done((bf16[2,4,64,1024]{3,2,1,0:T(8,128)(2,1)}, bf16[2,4,64,1024]{3,2,1,0:T(8,128)(2,1)S(1)}, u32[]{:S(2)}, u32[]{:S(2)}) %collective-permute-start.8) | collective-permute-done | bytes 1048608 | tf_op jit(solution)/shard_map/ppermute | solution.py:752
  348.2 9.6 %cross_query_grad.1 = (f32[448,1024]{1,0:T(8,128)}, bf16[448,1024]{1,0:T(8,128)(2,1)}, bf16[448,1024]{1,0:T(8,128)(2,1)}, f32[3,1024]{1,0:T(4,128)}) custom-call(s32[2]{0:T(128)} %copy-done.5, bf16[448,1024]{1,0:T(8,128)(2,1)} %get-tuple-element.307.refs_1_.refs_6_, f32[448,1024]{1,0:T(8,128)} %copy-done.1, f32[448,1024]{1,0:T(8,128)} %get-tuple-element.283.refs_3_, ...), custom_call_target="tpu_custom_call" | custom-call | flops 1879048192 | bytes 14680064 | tf_op jit(solution)/shard_map/cross_query_grad/pallas_call | solution.py:86
  360.6 16.6 %weight_grads.4 = (bf16[2,4,64,1024]{3,2,1,0:T(8,128)(2,1)}, bf16[2,4,64,1024]{3,2,1,0:T(8,128)(2,1)}, bf16[2,4,64,1024]{3,2,1,0:T(8,128)(2,1)}, bf16[2,4,64,1024]{3,2,1,0:T(8,128)(2,1)}) custom-call(s32[2]{0:T(128)} %copy-done.5, bf16[1504,1024]{1,0:T(8,128)(2,1)} %pad.9.refs_1_.refs_0_, bf16[1504,1024]{1,0:T(8,128)(2,1)} %collective-permute-done.5.refs_1_, ...), custom_call_target="tpu_custom_call" | custom-call | flops 8187281408 | bytes 12582912 | tf_op jit(solution)/shard_map/weight_grads/pallas_call | solution.py:639
  386.7 13.3 %attend_causal_grad.1 = (bf16[448,1024]{1,0:T(8,128)(2,1)}, bf16[448,1024]{1,0:T(8,128)(2,1)}, bf16[448,1024]{1,0:T(8,128)(2,1)}, f32[2,1024]{1,0:T(2,128)}) custom-call(bf16[448,1024]{1,0:T(8,128)(2,1)} %copy-done.9, bf16[448,1024]{1,0:T(8,128)(2,1)} %copy-done.10, bf16[448,1024]{1,0:T(8,128)(2,1)} %copy-done.11, ...), custom_call_target="tpu_custom_call" | custom-call | flops 8220835840 | bytes 3670016 | tf_op jit(solution)/shard_map/attend_causal_grad/pallas_call | solution.py:526
  400.0 9.2 %collective-permute-done.19 = bf16[2,128,1024]{2,1,0:T(8,128)(2,1)S(1)} collective-permute-done((bf16[2,128,1024]{2,1,0:T(8,128)(2,1)}, bf16[2,128,1024]{2,1,0:T(8,128)(2,1)S(1)}, u32[]{:S(2)}, u32[]{:S(2)}) %collective-permute-start.19) | collective-permute-done | bytes 524320 | tf_op jit(solution)/shard_map/ppermute | solution.py:752
  422.1 9.3 %weight_grads.5 = (bf16[2,4,64,1024]{3,2,1,0:T(8,128)(2,1)}, bf16[2,4,64,1024]{3,2,1,0:T(8,128)(2,1)}, bf16[2,4,64,1024]{3,2,1,0:T(8,128)(2,1)}, bf16[2,4,64,1024]{3,2,1,0:T(8,128)(2,1)}) custom-call(s32[2]{0:T(128)} %copy-done.5, bf16[448,1024]{1,0:T(8,128)(2,1)} %get-tuple-element.246.refs_1_.o_ref.refs_0_, bf16[448,1024]{1,0:T(8,128)(2,1)} %copy-done.57, ...), custom_call_target="tpu_custom_call" | custom-call | flops 3758096384 | bytes 12582912 | tf_op jit(solution)/shard_map/weight_grads/pallas_call | solution.py:639
  440.4 14.8 %encoder_grad.1 = f32[12000,128]{1,0:T(8,128)} custom-call(s32[2]{0:T(128)} %copy-done.5, bf16[1504,1024]{1,0:T(8,128)(2,1)} %get-tuple-element.387.refs_8_.refs_1_, bf16[1504,1024]{1,0:T(8,128)(2,1)} %get-tuple-element.311.refs_10_.refs_2_, bf16[32,264,1024]{2,1,0:T(8,128)(2,1)} %bitcast.112, bf16[32,264,1024]{2,1,0:T(8,128)(2,1)} %bitcast.113), custom_call_target="tpu_custom_call" | custom-call | flops 6291456000 | bytes 16777216 | tf_op jit(solution)/shard_map/encoder_grad/pallas_call | solution.py:86
  458.7 11.1 %self_in_grad.1 = (f32[448,1024]{1,0:T(8,128)}, f32[2,1024]{1,0:T(2,128)}) custom-call(s32[2]{0:T(128)} %copy-done.5, bf16[448,1024]{1,0:T(8,128)(2,1)} %get-tuple-element.363.refs_6_.refs_1_, bf16[448,1024]{1,0:T(8,128)(2,1)} %get-tuple-element.365.refs_8_.refs_2_, bf16[448,1024]{1,0:T(8,128)(2,1)} %get-tuple-element.367.refs_10_.refs_3_, ...), custom_call_target="tpu_custom_call" | custom-call | flops 2818572288 | bytes 14680064 | tf_op jit(solution)/shard_map/self_in_grad/pallas_call | solution.py:86
  484.7 11.1 %collective-permute-done.34 = f32[24,1024]{1,0:T(8,128)S(1)} collective-permute-done((f32[24,1024]{1,0:T(8,128)S(1)}, f32[24,1024]{1,0:T(8,128)S(1)}, u32[]{:S(2)}, u32[]{:S(2)}) %collective-permute-start.34) | collective-permute-done | bytes 98336 | tf_op jit(solution)/shard_map/ppermute | solution.py:752
  513.6 12.2 %collective-permute-done.37 = bf16[128,1024]{1,0:T(8,128)(2,1)S(1)} collective-permute-done((bf16[128,1024]{1,0:T(8,128)(2,1)}, bf16[128,1024]{1,0:T(8,128)(2,1)S(1)}, u32[]{:S(2)}, u32[]{:S(2)}) %collective-permute-start.37) | collective-permute-done | bytes 262176 | tf_op jit(solution)/shard_map/ppermute | solution.py:752
  (286 shorter events, 119.4 us)
Async XLA Ops:
  7.2 124.2 %all-gather.5.cloned.1.call-start = ((), (), s32[]{:S(2)}) async-start(), calls=%async_computation.2 | async-start | bytes 17842176 | tf_op jit(solution)/shard_map/all_gather | solution.py:901
  10.4 237.7 %all-gather.7.cloned.1.call-start = ((), (), s32[]{:S(2)}) async-start(), calls=%async_computation.3 | async-start | bytes 17301504 | tf_op jit(solution)/shard_map/all_gather | solution.py:902
  11.4 370.0 %reduce-scatter.2.cloned.1.call-start = ((), (), s32[]{:S(2)}) async-start(), calls=%async_computation.1 | async-start | bytes 9437184 | tf_op jit(solution)/shard_map/reduce_scatter | solution.py:1033
  196.2 15.4 %collective-permute-start.5 = (bf16[1504,1024]{1,0:T(8,128)(2,1)}, bf16[1504,1024]{1,0:T(8,128)(2,1)}, u32[]{:S(2)}, u32[]{:S(2)}) collective-permute-start(bf16[1504,1024]{1,0:T(8,128)(2,1)} %pad.9.refs_1_.refs_0_), channel_id=1, source_target_pairs={{0,4},{4,0},{1,5},{5,1},{2,6},{6,2},{3,7},{7,3},{8,12},{12,8},{9,1... | collective-permute-start | bytes 9240584 | tf_op jit(solution)/shard_map/ppermute | solution.py:752
  302.4 34.7 %collective-permute-start.7 = (bf16[448,1024]{1,0:T(8,128)(2,1)}, bf16[448,1024]{1,0:T(8,128)(2,1)S(1)}, u32[]{:S(2)}, u32[]{:S(2)}) collective-permute-start(bf16[448,1024]{1,0:T(8,128)(2,1)} %get-tuple-element.313.refs_12_), channel_id=1, source_target_pairs={{0,4},{4,0},{1,5},{5,1},{2,6},{6,2},{3,7},{7,3},{8,12},{12,8},{9,1... | collective-permute-start | bytes 2752520 | tf_op jit(solution)/shard_map/ppermute | solution.py:752
  302.8 40.3 %collective-permute-start.8 = (bf16[2,4,64,1024]{3,2,1,0:T(8,128)(2,1)}, bf16[2,4,64,1024]{3,2,1,0:T(8,128)(2,1)S(1)}, u32[]{:S(2)}, u32[]{:S(2)}) collective-permute-start(bf16[2,4,64,1024]{3,2,1,0:T(8,128)(2,1)} %get-tuple-element.277), channel_id=1, source_target_pairs={{0,8},{8,0},{1,9},{9,1},{2,10},{10,2},{3,11},{11,3},{4,12},{12,4},... | collective-permute-start | bytes 3145736 | tf_op jit(solution)/shard_map/ppermute | solution.py:752
  304.3 38.8 %collective-permute-start.9 = (bf16[2,4,64,1024]{3,2,1,0:T(8,128)(2,1)S(1)}, bf16[2,4,64,1024]{3,2,1,0:T(8,128)(2,1)S(1)}, u32[]{:S(2)}, u32[]{:S(2)}) collective-permute-start(bf16[2,4,64,1024]{3,2,1,0:T(8,128)(2,1)S(1)} %copy-done.55), channel_id=1, source_target_pairs={{0,16},{16,0},{1,17},{17,1},{2,18},{18,2},{3,19},{19,3},{4,20},{20... | collective-permute-start | bytes 3145736 | tf_op jit(solution)/shard_map/ppermute | solution.py:752
  357.8 19.5 %collective-permute-start.13 = (bf16[448,1024]{1,0:T(8,128)(2,1)}, bf16[448,1024]{1,0:T(8,128)(2,1)S(1)}, u32[]{:S(2)}, u32[]{:S(2)}) collective-permute-start(bf16[448,1024]{1,0:T(8,128)(2,1)} %get-tuple-element.361.refs_4_), channel_id=1, source_target_pairs={{0,4},{4,0},{1,5},{5,1},{2,6},{6,2},{3,7},{7,3},{8,12},{12,8},{9,1... | collective-permute-start | bytes 2752520 | tf_op jit(solution)/shard_map/ppermute | solution.py:752
  357.9 19.3 %collective-permute-start.14 = (bf16[4,64,1024]{2,1,0:T(8,128)(2,1)}, bf16[4,64,1024]{2,1,0:T(8,128)(2,1)S(1)}, u32[]{:S(2)}, u32[]{:S(2)}) collective-permute-start(bf16[4,64,1024]{2,1,0:T(8,128)(2,1)} %get-tuple-element.320), channel_id=1, source_target_pairs={{0,16},{16,0},{1,17},{17,1},{2,18},{18,2},{3,19},{19,3},{4,20},{20... | collective-permute-start | bytes 1572872 | tf_op jit(solution)/shard_map/ppermute | solution.py:752
  359.4 17.8 %collective-permute-start.15 = (bf16[4,64,1024]{2,1,0:T(8,128)(2,1)}, bf16[4,64,1024]{2,1,0:T(8,128)(2,1)S(1)}, u32[]{:S(2)}, u32[]{:S(2)}) collective-permute-start(bf16[4,64,1024]{2,1,0:T(8,128)(2,1)} %get-tuple-element.321), channel_id=1, source_target_pairs={{0,8},{8,0},{1,9},{9,1},{2,10},{10,2},{3,11},{11,3},{4,12},{12,4},... | collective-permute-start | bytes 1572872 | tf_op jit(solution)/shard_map/ppermute | solution.py:752
  383.3 25.9 %collective-permute-start.16 = (bf16[2,4,64,1024]{3,2,1,0:T(8,128)(2,1)}, bf16[2,4,64,1024]{3,2,1,0:T(8,128)(2,1)S(1)}, u32[]{:S(2)}, u32[]{:S(2)}) collective-permute-start(bf16[2,4,64,1024]{3,2,1,0:T(8,128)(2,1)} %get-tuple-element.336), channel_id=1, source_target_pairs={{0,8},{8,0},{1,9},{9,1},{2,10},{10,2},{3,11},{11,3},{4,12},{12,4},... | collective-permute-start | bytes 3145736 | tf_op jit(solution)/shard_map/ppermute | solution.py:752
  384.1 25.2 %collective-permute-start.17 = (bf16[2,4,64,1024]{3,2,1,0:T(8,128)(2,1)}, bf16[2,4,64,1024]{3,2,1,0:T(8,128)(2,1)S(1)}, u32[]{:S(2)}, u32[]{:S(2)}) collective-permute-start(bf16[2,4,64,1024]{3,2,1,0:T(8,128)(2,1)} %get-tuple-element.337), channel_id=1, source_target_pairs={{0,16},{16,0},{1,17},{17,1},{2,18},{18,2},{3,19},{19,3},{4,20},{20... | collective-permute-start | bytes 3145736 | tf_op jit(solution)/shard_map/ppermute | solution.py:752
  384.6 15.3 %collective-permute-start.18 = (bf16[2,128,1024]{2,1,0:T(8,128)(2,1)}, bf16[2,128,1024]{2,1,0:T(8,128)(2,1)S(1)}, u32[]{:S(2)}, u32[]{:S(2)}) collective-permute-start(bf16[2,128,1024]{2,1,0:T(8,128)(2,1)} %get-tuple-element.338), channel_id=1, source_target_pairs={{0,1},{1,0},{2,3},{3,2},{4,5},{5,4},{6,7},{7,6},{8,9},{9,8},{10,11... | collective-permute-start | bytes 1572872 | tf_op jit(solution)/shard_map/ppermute | solution.py:752
  386.1 23.1 %collective-permute-start.19 = (bf16[2,128,1024]{2,1,0:T(8,128)(2,1)}, bf16[2,128,1024]{2,1,0:T(8,128)(2,1)S(1)}, u32[]{:S(2)}, u32[]{:S(2)}) collective-permute-start(bf16[2,128,1024]{2,1,0:T(8,128)(2,1)} %pad_maximum_fusion), channel_id=1, source_target_pairs={{0,1},{1,0},{2,3},{3,2},{4,5},{5,4},{6,7},{7,6},{8,9},{9,8},{10,11... | collective-permute-start | bytes 1572872 | tf_op jit(solution)/shard_map/ppermute | solution.py:752
  415.5 18.5 %collective-permute-start.23 = (bf16[4,64,1024]{2,1,0:T(8,128)(2,1)}, bf16[4,64,1024]{2,1,0:T(8,128)(2,1)S(1)}, u32[]{:S(2)}, u32[]{:S(2)}) collective-permute-start(bf16[4,64,1024]{2,1,0:T(8,128)(2,1)} %get-tuple-element.373), channel_id=1, source_target_pairs={{0,16},{16,0},{1,17},{17,1},{2,18},{18,2},{3,19},{19,3},{4,20},{20... | collective-permute-start | bytes 1572872 | tf_op jit(solution)/shard_map/ppermute | solution.py:752
  416.9 17.1 %collective-permute-start.24 = (bf16[4,64,1024]{2,1,0:T(8,128)(2,1)}, bf16[4,64,1024]{2,1,0:T(8,128)(2,1)S(1)}, u32[]{:S(2)}, u32[]{:S(2)}) collective-permute-start(bf16[4,64,1024]{2,1,0:T(8,128)(2,1)} %get-tuple-element.374), channel_id=1, source_target_pairs={{0,8},{8,0},{1,9},{9,1},{2,10},{10,2},{3,11},{11,3},{4,12},{12,4},... | collective-permute-start | bytes 1572872 | tf_op jit(solution)/shard_map/ppermute | solution.py:752
  438.2 31.7 %collective-permute-start.26 = (bf16[2,4,64,1024]{3,2,1,0:T(8,128)(2,1)}, bf16[2,4,64,1024]{3,2,1,0:T(8,128)(2,1)S(1)}, u32[]{:S(2)}, u32[]{:S(2)}) collective-permute-start(bf16[2,4,64,1024]{3,2,1,0:T(8,128)(2,1)} %get-tuple-element.388), channel_id=1, source_target_pairs={{0,8},{8,0},{1,9},{9,1},{2,10},{10,2},{3,11},{11,3},{4,12},{12,4},... | collective-permute-start | bytes 3145736 | tf_op jit(solution)/shard_map/ppermute | solution.py:752
  439.3 30.6 %collective-permute-start.27 = (bf16[2,4,64,1024]{3,2,1,0:T(8,128)(2,1)}, bf16[2,4,64,1024]{3,2,1,0:T(8,128)(2,1)S(1)}, u32[]{:S(2)}, u32[]{:S(2)}) collective-permute-start(bf16[2,4,64,1024]{3,2,1,0:T(8,128)(2,1)} %get-tuple-element.389), channel_id=1, source_target_pairs={{0,16},{16,0},{1,17},{17,1},{2,18},{18,2},{3,19},{19,3},{4,20},{20... | collective-permute-start | bytes 3145736 | tf_op jit(solution)/shard_map/ppermute | solution.py:752
  439.9 30.0 %collective-permute-start.28 = (bf16[2,128,1024]{2,1,0:T(8,128)(2,1)}, bf16[2,128,1024]{2,1,0:T(8,128)(2,1)}, u32[]{:S(2)}, u32[]{:S(2)}) collective-permute-start(bf16[2,128,1024]{2,1,0:T(8,128)(2,1)} %get-tuple-element.390), channel_id=1, source_target_pairs={{0,1},{1,0},{2,3},{3,2},{4,5},{5,4},{6,7},{7,6},{8,9},{9,8},{10,11... | collective-permute-start | bytes 1572872 | tf_op jit(solution)/shard_map/ppermute | solution.py:752
  478.0 17.8 %collective-permute-start.31 = (bf16[4,64,1024]{2,1,0:T(8,128)(2,1)}, bf16[4,64,1024]{2,1,0:T(8,128)(2,1)S(1)}, u32[]{:S(2)}, u32[]{:S(2)}) collective-permute-start(bf16[4,64,1024]{2,1,0:T(8,128)(2,1)} %get-tuple-element.413), channel_id=1, source_target_pairs={{0,16},{16,0},{1,17},{17,1},{2,18},{18,2},{3,19},{19,3},{4,20},{20... | collective-permute-start | bytes 1572872 | tf_op jit(solution)/shard_map/ppermute | solution.py:752
  479.5 16.4 %collective-permute-start.32 = (bf16[4,64,1024]{2,1,0:T(8,128)(2,1)}, bf16[4,64,1024]{2,1,0:T(8,128)(2,1)S(1)}, u32[]{:S(2)}, u32[]{:S(2)}) collective-permute-start(bf16[4,64,1024]{2,1,0:T(8,128)(2,1)} %get-tuple-element.414), channel_id=1, source_target_pairs={{0,8},{8,0},{1,9},{9,1},{2,10},{10,2},{3,11},{11,3},{4,12},{12,4},... | collective-permute-start | bytes 1572872 | tf_op jit(solution)/shard_map/ppermute | solution.py:752
  480.4 15.4 %collective-permute-start.33 = (bf16[128,1024]{1,0:T(8,128)(2,1)}, bf16[128,1024]{1,0:T(8,128)(2,1)S(1)}, u32[]{:S(2)}, u32[]{:S(2)}) collective-permute-start(bf16[128,1024]{1,0:T(8,128)(2,1)} %fusion.6), channel_id=1, source_target_pairs={{0,2},{2,0},{1,3},{3,1},{4,6},{6,4},{5,7},{7,5},{8,10},{10,8},{9,1... | collective-permute-start | bytes 786440 | tf_op jit(solution)/shard_map/ppermute | solution.py:752
  480.5 15.3 %collective-permute-start.34 = (f32[24,1024]{1,0:T(8,128)S(1)}, f32[24,1024]{1,0:T(8,128)S(1)}, u32[]{:S(2)}, u32[]{:S(2)}) collective-permute-start(f32[24,1024]{1,0:T(8,128)S(1)} %maximum_select_fusion.3), channel_id=1, source_target_pairs={{0,8},{8,0},{1,9},{9,1},{2,10},{10,2},{3,11},{11,3},{4,12},{12,4},... | collective-permute-start | bytes 294920 | tf_op jit(solution)/shard_map/ppermute | solution.py:752
  503.9 21.9 %collective-permute-start.37 = (bf16[128,1024]{1,0:T(8,128)(2,1)}, bf16[128,1024]{1,0:T(8,128)(2,1)S(1)}, u32[]{:S(2)}, u32[]{:S(2)}) collective-permute-start(bf16[128,1024]{1,0:T(8,128)(2,1)} %get-tuple-element.426), channel_id=1, source_target_pairs={{0,2},{1,3},{2,0},{3,1},{4,6},{5,7},{6,4},{7,5},{8,10},{9,11},{10,... | collective-permute-start | bytes 786440 | tf_op jit(solution)/shard_map/ppermute | solution.py:752
  (83 other events, 1186.2 us)
Sparse Core Ops, SparseCore 0:
  11.4 119.9 all-gather.4
  135.0 113.0 all-gather.6
  272.7 86.1 reduce-scatter.1

commit v4 on v3

--- a/solution.py
+++ b/solution.py
@@ -216,7 +216,7 @@
     return scores
 
 
-def attend_kernel(causal, valid, q_ref, k_ref, v_ref, o_ref, lse_ref, top_ref, held):
+def attend_kernel(causal, valid, q_ref, k_ref, v_ref, o_ref, exp_ref, inv_ref, top_ref, held):
     rows = q_ref.shape[0]
     query = masked_pair(q_ref[...] * jnp.asarray(HD**-0.5, BF))
     top = jnp.full((1, 2 * rows), -1e30, F32)
@@ -229,12 +229,14 @@
     for a, b in key_chunks(k_ref.shape[0]):
         probs = jnp.exp(held[a:b, :] - top)
         total += jnp.sum(probs, axis=0, keepdims=True)
-        mixed += dot_tn(v_ref[a:b, :], probs.astype(BF))
+        rounded = probs.astype(BF)
+        exp_ref[0, a:b, :] = rounded
+        mixed += dot_tn(v_ref[a:b, :], rounded)
+    inv_ref[0] = 1.0 / total
     o_ref[...] = pair_back(mixed * (1.0 / total), rows).astype(BF)
     lane = lax.broadcasted_iota(jnp.int32, (1, 2 * HD), 1)
     first, second = (jnp.max(part, axis=1, keepdims=True) for part in (top[:, :rows], top[:, rows:]))
     top_ref[0] = jnp.where(lane == 0, first, second)
-    lse_ref[0] = top + jnp.log(total)
 
 
 def attend(query, key, value, causal, valid):
@@ -249,9 +251,15 @@
     return pl.pallas_call(
         functools.partial(attend_kernel, causal, valid),
         grid=(pairs,),
-        out_shape=[shape((rows, width), BF), shape((pairs, 1, 2 * rows), F32), shape((pairs, 1, 2 * HD), F32)],
+        out_shape=[
+            shape((rows, width), BF), shape((pairs, keys, 2 * rows), BF), shape((pairs, 1, 2 * rows), F32),
+            shape((pairs, 1, 2 * HD), F32),
+        ],
         in_specs=[column(rows), column(keys), column(keys)],
-        out_specs=[column(rows), line, pl.BlockSpec((1, 1, 2 * HD), lambda h: (h, 0, 0))],
+        out_specs=[
+            column(rows), pl.BlockSpec((1, keys, 2 * rows), lambda h: (h, 0, 0)), line,
+            pl.BlockSpec((1, 1, 2 * HD), lambda h: (h, 0, 0)),
+        ],
         scratch_shapes=[pltpu.VMEM((keys, 2 * rows), F32)],
         compiler_params=params(48),
         cost_estimate=cost(16 * rows * keys * width, 4 * keys * width),
@@ -483,9 +491,7 @@
     )
 
 
-def attend_grad_kernel(
-    causal, valid, q_ref, k_ref, v_ref, o_ref, do_ref, lse_ref, dq_ref, dk_ref, dv_ref, sums_ref
-):
+def attend_grad_kernel(q_ref, k_ref, v_ref, o_ref, do_ref, exp_ref, inv_ref, dq_ref, dk_ref, dv_ref, sums_ref):
     rows = q_ref.shape[0]
     scale = jnp.asarray(HD**-0.5, BF)
     query = masked_pair(q_ref[...] * scale)
@@ -494,13 +500,12 @@
     delta = jnp.concatenate(
         [jnp.sum(product[:HD], axis=0, keepdims=True), jnp.sum(product[HD:], axis=0, keepdims=True)], axis=1
     )
-    lse = lse_ref[0]
+    inv = inv_ref[0]
     grad_query = jnp.zeros((2 * HD, 2 * rows), F32)
     value_sum = jnp.zeros((1, 2 * HD), F32)
     for a, b in key_chunks(k_ref.shape[0]):
         key = k_ref[a:b, :]
-        scores = exclude(dot_nt(key, query), a, rows, causal, valid)
-        probs = jnp.exp(scores - lse)
+        probs = exp_ref[0, a:b, :].astype(F32) * inv
         grad_probs = dot_nt(v_ref[a:b, :], grad_out)
         grad_scores = (probs * (grad_probs - delta)).astype(BF)
         grad_value = dot(probs.astype(BF), grad_out).astype(BF)
@@ -514,7 +519,7 @@
     sums_ref[1:2, :] = value_sum
 
 
-def attend_grad(query, key, value, mixed, grad_mixed, lse, causal, valid):
+def attend_grad(query, key, value, mixed, grad_mixed, saved):
     rows, width = query.shape
     keys = key.shape[0]
     pairs = width // (2 * HD)
@@ -524,15 +529,18 @@
 
     line = pl.BlockSpec((1, 1, 2 * rows), lambda h: (h, 0, 0))
     return pl.pallas_call(
-        functools.partial(attend_grad_kernel, causal, valid),
+        attend_grad_kernel,
         grid=(pairs,),
         out_shape=[shape((rows, width), BF)] + [shape((keys, width), BF)] * 2 + [shape((2, width), F32)],
-        in_specs=[column(rows), column(keys), column(keys), column(rows), column(rows), line],
+        in_specs=[
+            column(rows), column(keys), column(keys), column(rows), column(rows),
+            pl.BlockSpec((1, keys, 2 * rows), lambda h: (h, 0, 0)), line,
+        ],
         out_specs=[column(rows), column(keys), column(keys), column(2)],
         compiler_params=params(),
-        cost_estimate=cost(40 * rows * keys * width, 8 * keys * width),
-        name="attend_causal_grad" if causal else "attend_grad",
-    )(query, key, value, mixed, grad_mixed, lse)
+        cost_estimate=cost(32 * rows * keys * width, 8 * keys * width),
+        name="attend_grad",
+    )(query, key, value, mixed, grad_mixed, *saved)
 
 
 def cross_query_grad_kernel(
@@ -651,7 +659,7 @@
     )(place, *operands)
 
 
-def encoder_grad_kernel(frames, place_ref, dk_ref, dv_ref, one, two, out_ref, bufs, sems):
+def encoder_grad_kernel(place_ref, dk_ref, dv_ref, one, two, out_ref, bufs, held, sems):
     for n, part in enumerate((one, two)):
         weight_start(place_ref, part, 0, bufs.at[n], sems.at[n])
     for n in range(2):
@@ -666,21 +674,28 @@
         total += dot_nt(dv_ref[...], bufs[1, pl.ds(n * per, per)].reshape(TILE, width))
         for side in range(TILE // 128):
             start = n * (TILE // 128) + side
-            out_ref[pl.ds(start, frames, stride=lines), :] = total[:frames, side * 128 : (side + 1) * 128]
+            held[pl.ds(start, total.shape[0], stride=lines), :] = total[:, side * 128 : (side + 1) * 128]
+
+    copy = pltpu.make_async_copy(held.at[pl.ds(0, out_ref.shape[0]), :], out_ref, sems.at[2])
+    copy.start()
+    copy.wait()
 
 
 def encoder_grad(place, dk2, dv2, packs, frames):
-    width = dk2.shape[1]
+    padded, width = dk2.shape
+    lines = width // 128
     return call(
-        functools.partial(encoder_grad_kernel, frames),
+        encoder_grad_kernel,
         packs,
         [place, dk2, dv2],
-        out_shape=shape((frames * (width // 128), 128), F32),
+        out_shape=shape((frames * lines, 128), F32),
         in_specs=[smem()] + [vmem()] * 2,
-        out_specs=vmem(),
-        scratch_shapes=[pltpu.VMEM((2, 32, 32, width), BF), pltpu.SemaphoreType.DMA((2,))],
+        out_specs=hbm(),
+        scratch_shapes=[
+            pltpu.VMEM((2, 32, 32, width), BF), pltpu.VMEM((padded * lines, 128), F32), pltpu.SemaphoreType.DMA((3,)),
+        ],
         compiler_params=params(),
-        cost_estimate=cost(4 * frames * width * width, 16 * MIB),
+        cost_estimate=cost(4 * padded * width * width, 16 * MIB),
         name="encoder_grad",
     )
 
@@ -879,8 +894,10 @@
     for axis in ("c", "x", "y"):
         moved = yield [(table, axis, SWAP)]
         table = combine(table, moved[0])
-    moved = yield [(table, "z", turns()[k]) for k in (1, 3, 2)]
-    return functools.reduce(combine, moved, table)
+    for pairs in (NEAR, FAR):
+        moved = yield [(table, "z", pairs)]
+        table = combine(table, moved[0])
+    return table
 
 
 def vector_table(pack, row, rows, shard_cols):
@@ -888,10 +905,8 @@
     return table.reshape(rows, 32 * shard_cols).astype(F32)
 
 
-def feed_shard(expand, contract):
-    width = contract.shape[1]
-    pieces = [expand[:, n * width : (n + 1) * width] for n in range(expand.shape[1] // width)]
-    return jnp.concatenate(pieces + [contract], axis=0)
+def expand_shard(expand, width):
+    return jnp.concatenate([expand[:, n * width : (n + 1) * width] for n in range(expand.shape[1] // width)], axis=0)
 
 
 def gather_fast(attention, expand, contract, vectors):
@@ -899,7 +914,19 @@
     line = jnp.pad(vectors.reshape(1, -1), ((0, 7), (0, width - vectors.size)))
     shard = jnp.concatenate([attention[m] for group in MATRICES for m in group] + [line], axis=0)
     pack = lax.all_gather(shard, ALL, axis=0, tiled=False)
-    pack_f = lax.all_gather(feed_shard(expand, contract), ALL, axis=0, tiled=False)
+    parts = []
+    before = []
+    for part in (expand_shard(expand, width), contract):
+        moved = []
+        part, _ = lax.optimization_barrier((part, before))
+        for k in (3, 1, 2):
+            part, moved = lax.optimization_barrier((part, moved))
+            moved.append(lax.ppermute(part, "z", turns()[k]))
+        part, moved = lax.optimization_barrier((part, moved))
+        before = moved
+        line = jnp.stack([part, moved[0], moved[2], moved[1]] * 2)
+        parts.append(lax.dynamic_slice_in_dim(line, (4 - lax.axis_index("z")) % 4, 4, 0))
+    pack_f = lax.all_gather(jnp.concatenate(parts, axis=1), ("y", "x", "c"), axis=0, tiled=True)
     return parts_of(pack), pack_f, vector_table(pack, 256, *vectors.shape)
 
 
@@ -969,17 +996,17 @@
     rows, width = x.shape
     one_a, one_b, two_a, two_b = packs
     a1, q1, k1, v1 = self_in(place, x, vec, [one_a, one_b])
-    o1, lse1, top1 = attend(q1, k1, v1, True, rows)
+    o1, *saved1, top1 = attend(q1, k1, v1, True, rows)
     x1, a2, q2 = self_out(place, o1, x, vec, [two_a, one_b])
     k2, v2 = cross_in(place, enc, vec, [two_a, two_b])
-    o2, lse2, top2 = attend(q2, k2, v2, False, frames)
+    o2, *saved2, top2 = attend(q2, k2, v2, False, frames)
     x2, a3 = cross_out(place, o2, x1, vec, [two_b])
     result, df, gb1, gb2, grad2 = feed(a3, x2, cot, vec, pack_f)
     da3 = feed_grad(df, pack_f)
     dx2, do2, e2, sums3 = cross_out_grad(place, da3, x2, cot, vec, [two_b])
-    dq2, dk2, dv2, bias2 = attend_grad(q2, k2, v2, o2, do2, lse2, False, frames)
+    dq2, dk2, dv2, bias2 = attend_grad(q2, k2, v2, o2, do2, saved2)
     dx1, do1, e1, sums2 = cross_query_grad(place, dq2, x1, dx2, vec, [two_a, one_b])
-    dq1, dk1, dv1, bias1 = attend_grad(q1, k1, v1, o1, do1, lse1, True, rows)
+    dq1, dk1, dv1, bias1 = attend_grad(q1, k1, v1, o1, do1, saved1)
     grad_input, sums1 = self_in_grad(place, dq1, dk1, dv1, x, dx1, vec, [one_a, one_b])
     grad_encoder = encoder_grad(place, dk2, dv2, [two_a, two_b], frames).reshape(frames, width)
     table = vector_table_of(sums1, bias1, sums2, bias2, sums3, gb1, gb2, top1, top2)
@@ -1019,10 +1046,10 @@
     (one_a, one_b, two_a, two_b), pack_f, vec = gather_fast(*owned)
     enc = pad_frames(encoder[0])
     a1, q1, k1, v1 = self_in(place, x, vec, [one_a, one_b])
-    o1, lse1, top1 = attend(q1, k1, v1, True, rows)
+    o1, *saved1, top1 = attend(q1, k1, v1, True, rows)
     x1, a2, q2 = self_out(place, o1, x, vec, [two_a, one_b])
     k2, v2 = cross_in(place, enc, vec, [two_a, two_b])
-    o2, lse2, top2 = attend(q2, k2, v2, False, frames)
+    o2, *saved2, top2 = attend(q2, k2, v2, False, frames)
     x2, a3 = cross_out(place, o2, x1, vec, [two_b])
 
     acts = Unit(swap_chain([a3, a1, o1, a2, o2, enc]))
@@ -1039,7 +1066,7 @@
         dx2, do2, e2, sums3 = cross_out_grad(place, da3, x2, cot, vec, [two_b])
         swap = Unit(swap_chain([e2]))
         out = step(
-            lambda do2: attend_grad(q2, k2, v2, o2[0], do2, lse2, False, frames), [do2], start=[swap], finish=[swap]
+            lambda do2: attend_grad(q2, k2, v2, o2[0], do2, saved2), [do2], start=[swap], finish=[swap]
         )
         return dx2, swap.result, sums3, *out
 
@@ -1063,35 +1090,34 @@
     )
     r1 = Unit(reduce_chain(place, True, *blocks))
     f2 = Unit(z_halves(plane_2))
-    dq1, dk1, dv1, bias1 = step(
-        lambda do1: attend_grad(q1, k1, v1, o1[0], do1, lse1, True, rows),
-        [do1],
-        start=[r1, f1, f2],
-        finish=[r1, f1, f2],
-    )
+
+    def self_back(do1):
+        dq1, dk1, dv1, bias1 = attend_grad(q1, k1, v1, o1[0], do1, saved1)
+        grad_input, sums1 = self_in_grad(place, dq1, dk1, dv1, x, dx1, vec, [one_a, one_b])
+        return dq1, dk1, dv1, bias1, grad_input, sums1
+
+    dq1, dk1, dv1, bias1, grad_input, sums1 = step(self_back, [do1], start=[r1, f1, f2], finish=[r1, f1, f2])
+    table = Unit(table_chain(vector_table_of(sums1, bias1, sums2, bias2, sums3, gb1, gb2, top1, top2)))
     swap_1 = Unit(swap_chain([dq1, dk1, dv1]))
-    step(start=[swap_1], finish=[swap_1])
+    step(start=[swap_1, table], finish=[swap_1, table])
     rights = swap_e1.result + swap_1.result
     blocks = step(
         lambda *rights: weight_grads(
             place, [o1, a1], [rights[k : k + 2] for k in range(0, 8, 2)], ((0, 0, 0), (1, 1, 0), (1, 2, 0), (1, 3, 0))
         ),
         [value for pair in rights for value in pair],
-        start=[r1, f1],
-        finish=[r1, f1],
+        start=[r1, f1, table],
+        finish=[r1, f1, table],
     )
     r2 = Unit(reduce_chain(place, False, *blocks))
-
-    def last(dx1, dk2):
-        grad_input, sums1 = self_in_grad(place, dq1, dk1, dv1, x, dx1, vec, [one_a, one_b])
-        return grad_input, sums1, encoder_grad(place, dk2, dv2, [two_a, two_b], frames)
-
-    grad_input, sums1, grad_encoder = step(last, [dx1, dk2], start=[r2, r1, f2], finish=[r2, r1, f2])
-    table = Unit(table_chain(vector_table_of(sums1, bias1, sums2, bias2, sums3, gb1, gb2, top1, top2)))
-    step(start=[table], finish=[table])
+    grad_encoder = step(
+        lambda dk2: encoder_grad(place, dk2, dv2, [two_a, two_b], frames),
+        [dk2],
+        start=[r2, r1, f2, table],
+        finish=[r2, r1, f2, table],
+    )
     step(start=[r2, r1, table], finish=[r2, r1, table])
     step(start=[r2, table], finish=[r2, table])
-    step(start=[table], finish=[table])
     total = table.result
     shard_cols = vectors.shape[1]
     g_vectors = lax.dynamic_slice_in_dim(total[:VEC_ROWS], lax.axis_index(ALL) * shard_cols, shard_cols, 1)

time: 558 us -> 546 us (0.978)
  waiting for transfers between devices: 219 us -> 186 us
  starting transfers between devices: 34.2 us -> 51.9 us
    ppermute x0 -> x6, waiting for transfers between devices: none -> 78.9 us  [gather_fast(): moved.append(lax.ppermute(part, 'z', turns()[k]))]
    all_gather x1, waiting for transfers between devices: 116 us -> 46.3 us  [gather_fast(): pack = lax.all_gather(shard, ALL, axis=0, tiled=False)]
    all_gather x1, waiting for transfers between devices: 36.5 us -> 7.22 us  [gather_fast(): lax.all_gather(jnp.concatenate(parts, axis=1), ('y', 'x', 'c'), axis=0, t...]
    ppermute x42 -> x41, waiting for transfers between devices: 67.1 us -> 53.5 us  [step(): lax.ppermute(v, axis, pairs)]
    ppermute x0 -> x6, starting transfers between devices: none -> 13.1 us  [gather_fast(): moved.append(lax.ppermute(part, 'z', turns()[k]))]
    pallas_call x2, Pallas kernels: 45.5 us -> 39.4 us  [attend_grad(): pl.pallas_call(attend_grad_kernel, grid=(pairs,), out_shape=[shape((rows,...]
    ppermute x42 -> x41, starting transfers between devices: 34.1 us -> 38.7 us  [step(): lax.ppermute(v, axis, pairs)]
    unnamed x142 -> x160, local copies, waits for them, and re-layouts: 13.9 us -> 13.7 us
  transfers between devices with their start and end apart: 45 -> 50, of which waited for: 16 -> 18; matrix products, arithmetic and copies ran while one was open for 3% -> 3% of each run, Pallas kernels for 38% -> 38%
where the time goes in v4:
time: 546 us; the launch traced here: 535 us
  Pallas kernels  240 us (44%)
  waiting for transfers between devices  186 us (34%)
  starting transfers between devices  51.9 us (10%)
  other arithmetic  22.3 us (4%)
  local copies, waits for them, and re-layouts  19.1 us (3%)
  between operations  15.4 us (3%)
    ppermute x6, waiting for transfers between devices, gather_fast(): moved.append(lax.ppermute(part, 'z', turns()[k]))  78.9 us
    pallas_call x8, Pallas kernels, call(): pl.pallas_call(body, in_specs=specs, **settings)  72.5 us
    ppermute x41, waiting for transfers between devices, step(): lax.ppermute(v, axis, pairs)  53.5 us
    all_gather x1, waiting for transfers between devices, gather_fast(): pack = lax.all_gather(shard, ALL, axis=0, tiled=False)  46.3 us
    pallas_call x2, Pallas kernels, attend_grad(): pl.pallas_call(attend_grad_kernel, grid=(pairs,), out_shape=[shape((rows,...  39.4 us
    ppermute x41, starting transfers between devices, step(): lax.ppermute(v, axis, pairs)  38.7 us
    pallas_call x3, Pallas kernels, weight_grads(): pl.pallas_call(functools.partial(weight_grads_kernel, jobs, len(lefts), l...  37.1 us
    pallas_call x2, Pallas kernels, attend(): pl.pallas_call(functools.partial(attend_kernel, causal, valid), grid=(pai...  34.1 us
  transfers between devices with their start and end apart: 50, of which 18 were waited for; matrix products, arithmetic and copies ran while one was open for 3% of the time, Pallas kernels for 38%

profile of v4, /device:TPU:0, one launch (start us, length us, event | category | flops | bytes accessed | tf_op | source)
XLA Modules:
  0.0 534.8 jit_solution(15049835714648409811)
XLA Ops:
  21.0 14.1 %collective-permute-done.7 = bf16[128,1024]{1,0:T(8,128)(2,1)S(1)} collective-permute-done((bf16[128,1024]{1,0:T(8,128)(2,1)S(1)}, bf16[128,1024]{1,0:T(8,128)(2,1)S(1)}, u32[]{:S(2)}, u32[]{:S(2)}) %collective-permute-start.7) | collective-permute-done | bytes 262176 | tf_op jit(solution)/shard_map/ppermute | solution.py:924
  38.6 14.8 %collective-permute-done.8 = bf16[128,1024]{1,0:T(8,128)(2,1)S(1)} collective-permute-done((bf16[128,1024]{1,0:T(8,128)(2,1)S(1)}, bf16[128,1024]{1,0:T(8,128)(2,1)S(1)}, u32[]{:S(2)}, u32[]{:S(2)}) %collective-permute-start.8) | collective-permute-done | bytes 262176 | tf_op jit(solution)/shard_map/ppermute | solution.py:924
  53.4 23.1 %collective-permute-done.9 = bf16[128,1024]{1,0:T(8,128)(2,1)S(1)} collective-permute-done((bf16[128,1024]{1,0:T(8,128)(2,1)S(1)}, bf16[128,1024]{1,0:T(8,128)(2,1)S(1)}, u32[]{:S(2)}, u32[]{:S(2)}) %collective-permute-start.9) | collective-permute-done | bytes 262176 | tf_op jit(solution)/shard_map/ppermute | solution.py:924
  76.6 13.6 %collective-permute-done.10 = bf16[128,1024]{1,0:T(8,128)(2,1)S(1)} collective-permute-done((bf16[128,1024]{1,0:T(8,128)(2,1)S(1)}, bf16[128,1024]{1,0:T(8,128)(2,1)S(1)}, u32[]{:S(2)}, u32[]{:S(2)}) %collective-permute-start.10) | collective-permute-done | bytes 262176 | tf_op jit(solution)/shard_map/ppermute | solution.py:924
  94.8 7.3 %collective-permute-done.11 = bf16[128,1024]{1,0:T(8,128)(2,1)S(1)} collective-permute-done((bf16[128,1024]{1,0:T(8,128)(2,1)S(1)}, bf16[128,1024]{1,0:T(8,128)(2,1)S(1)}, u32[]{:S(2)}, u32[]{:S(2)}) %collective-permute-start.11) | collective-permute-done | bytes 262176 | tf_op jit(solution)/shard_map/ppermute | solution.py:924
  107.2 46.3 %all-gather.6.cloned.1.call-done = bf16[8448,1024]{1,0:T(8,128)(2,1)} async-done(((bf16[264,1024]{1,0:T(8,128)(2,1)}), bf16[8448,1024]{1,0:T(8,128)(2,1)}) %all-gather.6.cloned.1.call-update) | async-done | bytes 17301520 | tf_op jit(solution)/shard_map/all_gather | solution.py:916
  155.0 6.4 %self_in.1 = (bf16[448,1024]{1,0:T(8,128)(2,1)}, bf16[448,1024]{1,0:T(8,128)(2,1)S(1)}, bf16[448,1024]{1,0:T(8,128)(2,1)S(1)}, bf16[448,1024]{1,0:T(8,128)(2,1)S(1)}) custom-call(s32[2]{0:T(128)S(1)} %pad_add_fusion.refs_0_.place_ref, bf16[448,1024]{1,0:T(8,128)(2,1)S(1)} %bitcast.122, ...), custom_call_target="tpu_custom_call" | custom-call | flops 2818572288 | bytes 10485760 | tf_op jit(solution)/shard_map/self_in/pallas_call | solution.py:86
  161.4 9.0 %attend_causal.1 = (bf16[448,1024]{1,0:T(8,128)(2,1)}, bf16[8,448,896]{2,1,0:T(8,128)(2,1)}, f32[8,1,896]{2,1,0:T(1,128)S(1)}, f32[8,1,128]{2,1,0:T(1,128)S(1)}) custom-call(bf16[448,1024]{1,0:T(8,128)(2,1)S(1)} %get-tuple-element.250.q_ref, bf16[448,1024]{1,0:T(8,128)(2,1)S(1)} %get-tuple-element.251.k_ref, bf16[448,1024]{1,0:T(8,128)(2,1)S(1)} %get-tuple-element.252.v_ref), custom_call_target="tpu_custom_call" | custom-call | flops 3288334336 | bytes 1835008 | tf_op jit(solution)/shard_map/attend_causal/pallas_call | solution.py:251
  177.9 13.3 %cross_in.1 = (bf16[1504,1024]{1,0:T(8,128)(2,1)S(1)}, bf16[1504,1024]{1,0:T(8,128)(2,1)}) custom-call(s32[2]{0:T(128)S(1)} %pad_add_fusion.refs_0_.place_ref, bf16[1504,1024]{1,0:T(8,128)(2,1)} %pad.9.refs_1_.refs_0_, f32[17,1024]{1,0:T(8,128)S(1)} %convert_element_type.134.refs_2_.refs_3_.vec_ref.refs_4_.refs_6_, bf16[32,264,1024]{2,1,0:T(8,128)(2,1)} %bitcast.129, ...), custom_call_target="tpu_custom_call" | custom-call | flops 6308233216 | bytes 14680064 | tf_op jit(solution)/shard_map/cross_in/pallas_call | solution.py:86
  191.3 25.2 %attend.1 = (bf16[448,1024]{1,0:T(8,128)(2,1)S(1)}, bf16[8,1504,896]{2,1,0:T(8,128)(2,1)}, f32[8,1,896]{2,1,0:T(1,128)S(1)}, f32[8,1,128]{2,1,0:T(1,128)S(1)}) custom-call(bf16[448,1024]{1,0:T(8,128)(2,1)S(1)} %get-tuple-element.254.q_ref, bf16[1504,1024]{1,0:T(8,128)(2,1)S(1)} %get-tuple-element.255.k_ref, bf16[1504,1024]{1,0:T(8,128)(2,1)} %get-tuple-element.256.v_ref), custom_call_target="tpu_custom_call" | custom-call | flops 11039408128 | bytes 6160384 | tf_op jit(solution)/shard_map/attend/pallas_call | solution.py:251
  236.8 7.2 %all-gather.4.cloned.1.call-done.w1_ref.w2_ref = bf16[32,256,1024]{2,1,0:T(8,128)(2,1)} async-done(((bf16[4,256,1024]{2,1,0:T(8,128)(2,1)}), bf16[32,256,1024]{2,1,0:T(8,128)(2,1)}) %all-gather.4.cloned.1.call-update) | async-done | bytes 16777232 | tf_op jit(solution)/shard_map/all_gather | solution.py:929
  244.0 24.6 %feed.1 = (bf16[448,1024]{1,0:T(8,128)(2,1)}, bf16[448,4096]{1,0:T(8,128)(2,1)}, f32[8,1,512]{2,1,0:T(1,128)}, f32[1,1024]{1,0:T(1,128)}, bf16[8,4,128,1024]{3,2,1,0:T(8,128)(2,1)}) custom-call(bf16[448,1024]{1,0:T(8,128)(2,1)} %copy-done.13, f32[448,1024]{1,0:T(8,128)} %copy-done.3, bf16[448,1024]{1,0:T(8,128)(2,1)} %bitcast.148, f32[17,1024]{1,0:T(8,128)} %copy-done.2, ...), custom_call_target="tpu_custom_call" | custom-call | flops 15032385536 | bytes 31457280 | tf_op jit(solution)/shard_map/feed/pallas_call | solution.py:401
  269.0 9.4 %feed_grad.1.refs_1_ = f32[448,1024]{1,0:T(8,128)} custom-call(bf16[448,4096]{1,0:T(8,128)(2,1)} %get-tuple-element.293.df_ref.refs_2_, bf16[32,256,1024]{2,1,0:T(8,128)(2,1)} %all-gather.4.cloned.1.call-done.w1_ref.w2_ref), custom_call_target="tpu_custom_call" | custom-call | flops 3758096384 | bytes 12582912 | tf_op jit(solution)/shard_map/feed_grad/pallas_call | solution.py:442
  280.4 11.3 %weight_grads.3 = (bf16[2,4,64,1024]{3,2,1,0:T(8,128)(2,1)}, bf16[2,4,64,1024]{3,2,1,0:T(8,128)(2,1)}, bf16[2,4,64,1024]{3,2,1,0:T(8,128)(2,1)}, bf16[2,4,64,1024]{3,2,1,0:T(8,128)(2,1)}) custom-call(s32[2]{0:T(128)} %copy-done.5, bf16[448,1024]{1,0:T(8,128)(2,1)} %copy-done.13, bf16[448,1024]{1,0:T(8,128)(2,1)} %copy-done.64, ...), custom_call_target="tpu_custom_call" | custom-call | flops 3758096384 | bytes 12582912 | tf_op jit(solution)/shard_map/weight_grads/pallas_call | solution.py:647
  291.7 6.8 %cross_out_grad.1 = (f32[448,1024]{1,0:T(8,128)}, bf16[448,1024]{1,0:T(8,128)(2,1)}, bf16[448,1024]{1,0:T(8,128)(2,1)}, f32[3,1024]{1,0:T(4,128)}) custom-call(s32[2]{0:T(128)} %copy-done.5, f32[448,1024]{1,0:T(8,128)} %feed_grad.1.refs_1_, f32[448,1024]{1,0:T(8,128)} %copy-done.3, bf16[448,1024]{1,0:T(8,128)(2,1)} %bitcast.149, f32[17,1024]{1,0:T(8,128)} %copy-done.2, ...), custom_call_target="tpu_custom_call" | custom-call | flops 939524096 | bytes 10485760 | tf_op jit(solution)/shard_map/cross_out_grad/pallas_call | solution.py:86
  300.7 27.2 %attend_grad.2 = (bf16[448,1024]{1,0:T(8,128)(2,1)}, bf16[1504,1024]{1,0:T(8,128)(2,1)}, bf16[1504,1024]{1,0:T(8,128)(2,1)}, f32[2,1024]{1,0:T(2,128)}) custom-call(bf16[448,1024]{1,0:T(8,128)(2,1)} %copy-done.12, bf16[1504,1024]{1,0:T(8,128)(2,1)} %copy-done.8, bf16[1504,1024]{1,0:T(8,128)(2,1)} %get-tuple-element.256.v_ref, bf16[448,1024]{1,0:T(8,128)(2,1)} %copy-done.4, ...), custom_call_target="tpu_custom_call" | custom-call | flops 22078816256 | bytes 12320768 | tf_op jit(solution)/shard_map/attend_grad/pallas_call | solution.py:531
  327.9 13.0 %collective-permute-done.14.refs_2_ = bf16[2,4,64,1024]{3,2,1,0:T(8,128)(2,1)S(1)} collective-permute-done((bf16[2,4,64,1024]{3,2,1,0:T(8,128)(2,1)}, bf16[2,4,64,1024]{3,2,1,0:T(8,128)(2,1)S(1)}, u32[]{:S(2)}, u32[]{:S(2)}) %collective-permute-start.14) | collective-permute-done | bytes 1048608 | tf_op jit(solution)/shard_map/ppermute | solution.py:767
  346.1 9.6 %cross_query_grad.1 = (f32[448,1024]{1,0:T(8,128)}, bf16[448,1024]{1,0:T(8,128)(2,1)}, bf16[448,1024]{1,0:T(8,128)(2,1)}, f32[3,1024]{1,0:T(4,128)}) custom-call(s32[2]{0:T(128)} %copy-done.5, bf16[448,1024]{1,0:T(8,128)(2,1)} %get-tuple-element.347.refs_1_.refs_6_, f32[448,1024]{1,0:T(8,128)} %copy-done.1, f32[448,1024]{1,0:T(8,128)} %get-tuple-element.323.refs_3_, ...), custom_call_target="tpu_custom_call" | custom-call | flops 1879048192 | bytes 14680064 | tf_op jit(solution)/shard_map/cross_query_grad/pallas_call | solution.py:86
  358.7 16.6 %weight_grads.4 = (bf16[2,4,64,1024]{3,2,1,0:T(8,128)(2,1)}, bf16[2,4,64,1024]{3,2,1,0:T(8,128)(2,1)}, bf16[2,4,64,1024]{3,2,1,0:T(8,128)(2,1)}, bf16[2,4,64,1024]{3,2,1,0:T(8,128)(2,1)}) custom-call(s32[2]{0:T(128)} %copy-done.5, bf16[1504,1024]{1,0:T(8,128)(2,1)} %pad.9.refs_1_.refs_0_, bf16[1504,1024]{1,0:T(8,128)(2,1)} %collective-permute-done.5.refs_1_, ...), custom_call_target="tpu_custom_call" | custom-call | flops 8187281408 | bytes 12582912 | tf_op jit(solution)/shard_map/weight_grads/pallas_call | solution.py:647
  384.7 12.1 %attend_grad.3 = (bf16[448,1024]{1,0:T(8,128)(2,1)}, bf16[448,1024]{1,0:T(8,128)(2,1)}, bf16[448,1024]{1,0:T(8,128)(2,1)}, f32[2,1024]{1,0:T(2,128)}) custom-call(bf16[448,1024]{1,0:T(8,128)(2,1)} %copy-done.9, bf16[448,1024]{1,0:T(8,128)(2,1)} %copy-done.10, bf16[448,1024]{1,0:T(8,128)(2,1)} %copy-done.11, ...), custom_call_target="tpu_custom_call" | custom-call | flops 6576668672 | bytes 3670016 | tf_op jit(solution)/shard_map/attend_grad/pallas_call | solution.py:531
  396.8 11.2 %self_in_grad.1 = (f32[448,1024]{1,0:T(8,128)}, f32[2,1024]{1,0:T(2,128)}) custom-call(s32[2]{0:T(128)} %copy-done.5, bf16[448,1024]{1,0:T(8,128)(2,1)} %get-tuple-element.418.refs_1_.refs_6_, bf16[448,1024]{1,0:T(8,128)(2,1)} %get-tuple-element.420.refs_2_.refs_8_, bf16[448,1024]{1,0:T(8,128)(2,1)} %get-tuple-element.422.refs_3_.refs_10_, ...), custom_call_target="tpu_custom_call" | custom-call | flops 2818572288 | bytes 14680064 | tf_op jit(solution)/shard_map/self_in_grad/pallas_call | solution.py:86
  424.7 9.3 %weight_grads.5 = (bf16[2,4,64,1024]{3,2,1,0:T(8,128)(2,1)}, bf16[2,4,64,1024]{3,2,1,0:T(8,128)(2,1)}, bf16[2,4,64,1024]{3,2,1,0:T(8,128)(2,1)}, bf16[2,4,64,1024]{3,2,1,0:T(8,128)(2,1)}) custom-call(s32[2]{0:T(128)} %copy-done.5, bf16[448,1024]{1,0:T(8,128)(2,1)} %get-tuple-element.266.refs_1_.o_ref.refs_0_, bf16[448,1024]{1,0:T(8,128)(2,1)} %copy-done.61, ...), custom_call_target="tpu_custom_call" | custom-call | flops 3758096384 | bytes 12582912 | tf_op jit(solution)/shard_map/weight_grads/pallas_call | solution.py:647
  445.4 14.8 %encoder_grad.1 = f32[12000,128]{1,0:T(8,128)} custom-call(s32[2]{0:T(128)} %copy-done.5, bf16[1504,1024]{1,0:T(8,128)(2,1)} %get-tuple-element.441.refs_8_.refs_1_, bf16[1504,1024]{1,0:T(8,128)(2,1)} %get-tuple-element.351.refs_10_.refs_2_, bf16[32,264,1024]{2,1,0:T(8,128)(2,1)} %bitcast.137, bf16[32,264,1024]{2,1,0:T(8,128)(2,1)} %bitcast.138), custom_call_target="tpu_custom_call" | custom-call | flops 6308233216 | bytes 16777216 | tf_op jit(solution)/shard_map/encoder_grad/pallas_call | solution.py:86
  502.6 18.8 %collective-permute-done.46 = f32[24,1024]{1,0:T(8,128)S(1)} collective-permute-done((f32[24,1024]{1,0:T(8,128)S(1)}, f32[24,1024]{1,0:T(8,128)S(1)}, u32[]{:S(2)}, u32[]{:S(2)}) %collective-permute-start.46) | collective-permute-done | bytes 98336 | tf_op jit(solution)/shard_map/ppermute | solution.py:767
  (322 shorter events, 154.4 us)
Async XLA Ops:
  7.2 146.3 %all-gather.6.cloned.1.call-start = ((), (), s32[]{:S(2)}) async-start(), calls=%async_computation.3 | async-start | bytes 17842176 | tf_op jit(solution)/shard_map/all_gather | solution.py:916
  9.7 234.3 %all-gather.4.cloned.1.call-start = ((), (), s32[]{:S(2)}) async-start(), calls=%async_computation.1 | async-start | bytes 18874368 | tf_op jit(solution)/shard_map/all_gather | solution.py:929
  35.0 18.3 %collective-permute-start.8 = (bf16[128,1024]{1,0:T(8,128)(2,1)S(1)}, bf16[128,1024]{1,0:T(8,128)(2,1)S(1)}, u32[]{:S(2)}, u32[]{:S(2)}) collective-permute-start(bf16[128,1024]{1,0:T(8,128)(2,1)S(1)} %pad_maximum_fusion.2), channel_id=1, source_target_pairs={{0,2},{1,3},{2,0},{3,1},{4,6},{5,7},{6,4},{7,5},{8,10},{9,11},{10,... | collective-permute-start | bytes 786440 | tf_op jit(solution)/shard_map/ppermute | solution.py:924
  53.3 23.2 %collective-permute-start.9 = (bf16[128,1024]{1,0:T(8,128)(2,1)S(1)}, bf16[128,1024]{1,0:T(8,128)(2,1)S(1)}, u32[]{:S(2)}, u32[]{:S(2)}) collective-permute-start(bf16[128,1024]{1,0:T(8,128)(2,1)S(1)} %convert_element_type.136), channel_id=1, source_target_pairs={{0,3},{1,0},{2,1},{3,2},{4,7},{5,4},{6,5},{7,6},{8,11},{9,8},{10,9... | collective-permute-start | bytes 786440 | tf_op jit(solution)/shard_map/ppermute | solution.py:924
  104.1 275.4 %reduce-scatter.2.cloned.1.call-start = ((), (), s32[]{:S(2)}) async-start(), calls=%async_computation.2 | async-start | bytes 9437184 | tf_op jit(solution)/shard_map/reduce_scatter | solution.py:1060
  298.5 29.4 %collective-permute-start.13 = (bf16[448,1024]{1,0:T(8,128)(2,1)}, bf16[448,1024]{1,0:T(8,128)(2,1)S(1)}, u32[]{:S(2)}, u32[]{:S(2)}) collective-permute-start(bf16[448,1024]{1,0:T(8,128)(2,1)} %get-tuple-element.353.refs_12_), channel_id=1, source_target_pairs={{0,4},{4,0},{1,5},{5,1},{2,6},{6,2},{3,7},{7,3},{8,12},{12,8},{9,1... | collective-permute-start | bytes 2752520 | tf_op jit(solution)/shard_map/ppermute | solution.py:767
  298.8 42.1 %collective-permute-start.14 = (bf16[2,4,64,1024]{3,2,1,0:T(8,128)(2,1)}, bf16[2,4,64,1024]{3,2,1,0:T(8,128)(2,1)S(1)}, u32[]{:S(2)}, u32[]{:S(2)}) collective-permute-start(bf16[2,4,64,1024]{3,2,1,0:T(8,128)(2,1)} %get-tuple-element.317), channel_id=1, source_target_pairs={{0,8},{8,0},{1,9},{9,1},{2,10},{10,2},{3,11},{11,3},{4,12},{12,4},... | collective-permute-start | bytes 3145736 | tf_op jit(solution)/shard_map/ppermute | solution.py:767
  300.2 40.7 %collective-permute-start.15 = (bf16[2,4,64,1024]{3,2,1,0:T(8,128)(2,1)S(1)}, bf16[2,4,64,1024]{3,2,1,0:T(8,128)(2,1)S(1)}, u32[]{:S(2)}, u32[]{:S(2)}) collective-permute-start(bf16[2,4,64,1024]{3,2,1,0:T(8,128)(2,1)S(1)} %copy-done.59), channel_id=1, source_target_pairs={{0,16},{16,0},{1,17},{17,1},{2,18},{18,2},{3,19},{19,3},{4,20},{20... | collective-permute-start | bytes 3145736 | tf_op jit(solution)/shard_map/ppermute | solution.py:767
  355.8 19.5 %collective-permute-start.19 = (bf16[448,1024]{1,0:T(8,128)(2,1)}, bf16[448,1024]{1,0:T(8,128)(2,1)S(1)}, u32[]{:S(2)}, u32[]{:S(2)}) collective-permute-start(bf16[448,1024]{1,0:T(8,128)(2,1)} %get-tuple-element.416.refs_4_), channel_id=1, source_target_pairs={{0,4},{4,0},{1,5},{5,1},{2,6},{6,2},{3,7},{7,3},{8,12},{12,8},{9,1... | collective-permute-start | bytes 2752520 | tf_op jit(solution)/shard_map/ppermute | solution.py:767
  355.9 19.4 %collective-permute-start.20 = (bf16[4,64,1024]{2,1,0:T(8,128)(2,1)}, bf16[4,64,1024]{2,1,0:T(8,128)(2,1)S(1)}, u32[]{:S(2)}, u32[]{:S(2)}) collective-permute-start(bf16[4,64,1024]{2,1,0:T(8,128)(2,1)} %get-tuple-element.360), channel_id=1, source_target_pairs={{0,16},{16,0},{1,17},{17,1},{2,18},{18,2},{3,19},{19,3},{4,20},{20... | collective-permute-start | bytes 1572872 | tf_op jit(solution)/shard_map/ppermute | solution.py:767
  357.7 17.6 %collective-permute-start.21 = (bf16[4,64,1024]{2,1,0:T(8,128)(2,1)}, bf16[4,64,1024]{2,1,0:T(8,128)(2,1)S(1)}, u32[]{:S(2)}, u32[]{:S(2)}) collective-permute-start(bf16[4,64,1024]{2,1,0:T(8,128)(2,1)} %get-tuple-element.361), channel_id=1, source_target_pairs={{0,8},{8,0},{1,9},{9,1},{2,10},{10,2},{3,11},{11,3},{4,12},{12,4},... | collective-permute-start | bytes 1572872 | tf_op jit(solution)/shard_map/ppermute | solution.py:767
  381.3 26.7 %collective-permute-start.22 = (bf16[2,4,64,1024]{3,2,1,0:T(8,128)(2,1)}, bf16[2,4,64,1024]{3,2,1,0:T(8,128)(2,1)S(1)}, u32[]{:S(2)}, u32[]{:S(2)}) collective-permute-start(bf16[2,4,64,1024]{3,2,1,0:T(8,128)(2,1)} %get-tuple-element.380), channel_id=1, source_target_pairs={{0,8},{8,0},{1,9},{9,1},{2,10},{10,2},{3,11},{11,3},{4,12},{12,4},... | collective-permute-start | bytes 3145736 | tf_op jit(solution)/shard_map/ppermute | solution.py:767
  382.3 25.7 %collective-permute-start.23 = (bf16[2,4,64,1024]{3,2,1,0:T(8,128)(2,1)}, bf16[2,4,64,1024]{3,2,1,0:T(8,128)(2,1)S(1)}, u32[]{:S(2)}, u32[]{:S(2)}) collective-permute-start(bf16[2,4,64,1024]{3,2,1,0:T(8,128)(2,1)} %get-tuple-element.381), channel_id=1, source_target_pairs={{0,16},{16,0},{1,17},{17,1},{2,18},{18,2},{3,19},{19,3},{4,20},{20... | collective-permute-start | bytes 3145736 | tf_op jit(solution)/shard_map/ppermute | solution.py:767
  382.6 25.4 %collective-permute-start.24 = (bf16[2,128,1024]{2,1,0:T(8,128)(2,1)}, bf16[2,128,1024]{2,1,0:T(8,128)(2,1)S(1)}, u32[]{:S(2)}, u32[]{:S(2)}) collective-permute-start(bf16[2,128,1024]{2,1,0:T(8,128)(2,1)} %get-tuple-element.382), channel_id=1, source_target_pairs={{0,1},{1,0},{2,3},{3,2},{4,5},{5,4},{6,7},{7,6},{8,9},{9,8},{10,11... | collective-permute-start | bytes 1572872 | tf_op jit(solution)/shard_map/ppermute | solution.py:767
  384.4 23.7 %collective-permute-start.25 = (bf16[2,128,1024]{2,1,0:T(8,128)(2,1)}, bf16[2,128,1024]{2,1,0:T(8,128)(2,1)}, u32[]{:S(2)}, u32[]{:S(2)}) collective-permute-start(bf16[2,128,1024]{2,1,0:T(8,128)(2,1)} %pad_maximum_fusion.1), channel_id=1, source_target_pairs={{0,1},{1,0},{2,3},{3,2},{4,5},{5,4},{6,7},{7,6},{8,9},{9,8},{10,11... | collective-permute-start | bytes 1572872 | tf_op jit(solution)/shard_map/ppermute | solution.py:767
  416.7 19.0 %collective-permute-start.30 = (bf16[4,64,1024]{2,1,0:T(8,128)(2,1)}, bf16[4,64,1024]{2,1,0:T(8,128)(2,1)S(1)}, u32[]{:S(2)}, u32[]{:S(2)}) collective-permute-start(bf16[4,64,1024]{2,1,0:T(8,128)(2,1)} %get-tuple-element.428), channel_id=1, source_target_pairs={{0,16},{16,0},{1,17},{17,1},{2,18},{18,2},{3,19},{19,3},{4,20},{20... | collective-permute-start | bytes 1572872 | tf_op jit(solution)/shard_map/ppermute | solution.py:767
  439.9 27.2 %collective-permute-start.34 = (bf16[2,4,64,1024]{3,2,1,0:T(8,128)(2,1)}, bf16[2,4,64,1024]{3,2,1,0:T(8,128)(2,1)S(1)}, u32[]{:S(2)}, u32[]{:S(2)}) collective-permute-start(bf16[2,4,64,1024]{3,2,1,0:T(8,128)(2,1)} %get-tuple-element.442), channel_id=1, source_target_pairs={{0,8},{8,0},{1,9},{9,1},{2,10},{10,2},{3,11},{11,3},{4,12},{12,4},... | collective-permute-start | bytes 3145736 | tf_op jit(solution)/shard_map/ppermute | solution.py:767
  441.0 26.2 %collective-permute-start.35 = (bf16[2,4,64,1024]{3,2,1,0:T(8,128)(2,1)}, bf16[2,4,64,1024]{3,2,1,0:T(8,128)(2,1)S(1)}, u32[]{:S(2)}, u32[]{:S(2)}) collective-permute-start(bf16[2,4,64,1024]{3,2,1,0:T(8,128)(2,1)} %get-tuple-element.443), channel_id=1, source_target_pairs={{0,16},{16,0},{1,17},{17,1},{2,18},{18,2},{3,19},{19,3},{4,20},{20... | collective-permute-start | bytes 3145736 | tf_op jit(solution)/shard_map/ppermute | solution.py:767
  441.4 25.8 %collective-permute-start.36 = (bf16[2,128,1024]{2,1,0:T(8,128)(2,1)}, bf16[2,128,1024]{2,1,0:T(8,128)(2,1)}, u32[]{:S(2)}, u32[]{:S(2)}) collective-permute-start(bf16[2,128,1024]{2,1,0:T(8,128)(2,1)} %get-tuple-element.444), channel_id=1, source_target_pairs={{0,1},{1,0},{2,3},{3,2},{4,5},{5,4},{6,7},{7,6},{8,9},{9,8},{10,11... | collective-permute-start | bytes 1572872 | tf_op jit(solution)/shard_map/ppermute | solution.py:767
  442.2 25.0 %collective-permute-start.37 = (bf16[128,1024]{1,0:T(8,128)(2,1)}, bf16[128,1024]{1,0:T(8,128)(2,1)S(1)}, u32[]{:S(2)}, u32[]{:S(2)}) collective-permute-start(bf16[128,1024]{1,0:T(8,128)(2,1)} %fusion.4), channel_id=1, source_target_pairs={{0,2},{2,0},{1,3},{3,1},{4,6},{6,4},{5,7},{7,5},{8,10},{10,8},{9,1... | collective-permute-start | bytes 786440 | tf_op jit(solution)/shard_map/ppermute | solution.py:767
  492.2 29.3 %collective-permute-start.43 = (bf16[128,1024]{1,0:T(8,128)(2,1)}, bf16[128,1024]{1,0:T(8,128)(2,1)S(1)}, u32[]{:S(2)}, u32[]{:S(2)}) collective-permute-start(bf16[128,1024]{1,0:T(8,128)(2,1)} %get-tuple-element.470), channel_id=1, source_target_pairs={{0,1},{1,2},{2,3},{3,0},{4,5},{5,6},{6,7},{7,4},{8,9},{9,10},{10,1... | collective-permute-start | bytes 786440 | tf_op jit(solution)/shard_map/ppermute | solution.py:767
  492.4 29.1 %collective-permute-start.44 = (bf16[128,1024]{1,0:T(8,128)(2,1)}, bf16[128,1024]{1,0:T(8,128)(2,1)S(1)}, u32[]{:S(2)}, u32[]{:S(2)}) collective-permute-start(bf16[128,1024]{1,0:T(8,128)(2,1)} %get-tuple-element.471), channel_id=1, source_target_pairs={{0,3},{1,0},{2,1},{3,2},{4,7},{5,4},{6,5},{7,6},{8,11},{9,8},{10,9... | collective-permute-start | bytes 786440 | tf_op jit(solution)/shard_map/ppermute | solution.py:767
  496.1 25.4 %collective-permute-start.45 = (bf16[128,1024]{1,0:T(8,128)(2,1)}, bf16[128,1024]{1,0:T(8,128)(2,1)S(1)}, u32[]{:S(2)}, u32[]{:S(2)}) collective-permute-start(bf16[128,1024]{1,0:T(8,128)(2,1)} %get-tuple-element.472), channel_id=1, source_target_pairs={{0,2},{1,3},{2,0},{3,1},{4,6},{5,7},{6,4},{7,5},{8,10},{9,11},{10,... | collective-permute-start | bytes 786440 | tf_op jit(solution)/shard_map/ppermute | solution.py:767
  498.6 22.8 %collective-permute-start.46 = (f32[24,1024]{1,0:T(8,128)S(1)}, f32[24,1024]{1,0:T(8,128)S(1)}, u32[]{:S(2)}, u32[]{:S(2)}) collective-permute-start(f32[24,1024]{1,0:T(8,128)S(1)} %maximum_select_fusion.1), channel_id=1, source_target_pairs={{0,2},{2,0},{1,3},{3,1},{4,6},{6,4},{5,7},{7,5},{8,10},{10,8},{9,1... | collective-permute-start | bytes 294920 | tf_op jit(solution)/shard_map/ppermute | solution.py:767
  (92 other events, 1038.8 us)
Sparse Core Ops, SparseCore 0:
  11.4 142.0 all-gather.5
  155.9 88.0 all-gather.3
  268.8 88.6 reduce-scatter.1

commit v5 on v4

--- a/solution.py
+++ b/solution.py
@@ -491,56 +491,31 @@
     )
 
 
-def attend_grad_kernel(q_ref, k_ref, v_ref, o_ref, do_ref, exp_ref, inv_ref, dq_ref, dk_ref, dv_ref, sums_ref):
-    rows = q_ref.shape[0]
-    scale = jnp.asarray(HD**-0.5, BF)
-    query = masked_pair(q_ref[...] * scale)
-    grad_out = masked_pair(do_ref[...])
-    product = (do_ref[...].astype(F32) * o_ref[...].astype(F32)).T
-    delta = jnp.concatenate(
-        [jnp.sum(product[:HD], axis=0, keepdims=True), jnp.sum(product[HD:], axis=0, keepdims=True)], axis=1
-    )
-    inv = inv_ref[0]
-    grad_query = jnp.zeros((2 * HD, 2 * rows), F32)
-    value_sum = jnp.zeros((1, 2 * HD), F32)
-    for a, b in key_chunks(k_ref.shape[0]):
-        key = k_ref[a:b, :]
-        probs = exp_ref[0, a:b, :].astype(F32) * inv
-        grad_probs = dot_nt(v_ref[a:b, :], grad_out)
-        grad_scores = (probs * (grad_probs - delta)).astype(BF)
-        grad_value = dot(probs.astype(BF), grad_out).astype(BF)
-        dv_ref[a:b, :] = grad_value
-        value_sum += jnp.sum(grad_value.astype(F32), axis=0, keepdims=True)
-        dk_ref[a:b, :] = dot(grad_scores, query).astype(BF)
-        grad_query += dot_tn(key, grad_scores)
-    grad_query = (pair_back(grad_query, rows) * HD**-0.5).astype(BF)
-    dq_ref[...] = grad_query
-    sums_ref[0:1, :] = jnp.sum(grad_query.astype(F32), axis=0, keepdims=True)
-    sums_ref[1:2, :] = value_sum
-
-
 def attend_grad(query, key, value, mixed, grad_mixed, saved):
     rows, width = query.shape
     keys = key.shape[0]
-    pairs = width // (2 * HD)
-
-    def column(count):
-        return pl.BlockSpec((count, 2 * HD), lambda h: (0, h))
-
-    line = pl.BlockSpec((1, 1, 2 * rows), lambda h: (h, 0, 0))
-    return pl.pallas_call(
-        attend_grad_kernel,
-        grid=(pairs,),
-        out_shape=[shape((rows, width), BF)] + [shape((keys, width), BF)] * 2 + [shape((2, width), F32)],
-        in_specs=[
-            column(rows), column(keys), column(keys), column(rows), column(rows),
-            pl.BlockSpec((1, keys, 2 * rows), lambda h: (h, 0, 0)), line,
-        ],
-        out_specs=[column(rows), column(keys), column(keys), column(2)],
-        compiler_params=params(),
-        cost_estimate=cost(32 * rows * keys * width, 8 * keys * width),
-        name="attend_grad",
-    )(query, key, value, mixed, grad_mixed, *saved)
+
+    def pairs(array):
+        return array.reshape(array.shape[0], -1, 2, HD).transpose(1, 2, 0, 3)
+
+    def back(array):
+        return array.transpose(2, 0, 1, 3).reshape(array.shape[2], width)
+
+    def one(inputs):
+        q, k, v, o, grad_o, exps, inv = inputs
+        probs = exps.reshape(keys, 2, rows).swapaxes(0, 1).astype(F32) * inv.reshape(2, 1, rows)
+        grad_probs = jnp.einsum("hkd,hqd->hkq", v, grad_o, preferred_element_type=F32)
+        delta = jnp.sum(o.astype(F32) * grad_o.astype(F32), axis=-1)[:, None, :]
+        grad_scores = (probs * (grad_probs - delta)).astype(BF)
+        grad_q = jnp.einsum("hkq,hkd->hqd", grad_scores, k, preferred_element_type=F32) * HD**-0.5
+        grad_k = jnp.einsum("hkq,hqd->hkd", grad_scores, q, preferred_element_type=F32) * HD**-0.5
+        grad_v = jnp.einsum("hkq,hqd->hkd", probs.astype(BF), grad_o, preferred_element_type=F32)
+        return grad_q.astype(BF), grad_k.astype(BF), grad_v.astype(BF)
+
+    grads = lax.map(one, (*[pairs(a) for a in (query, key, value, mixed, grad_mixed)], *saved))
+    grads = [back(g) for g in grads]
+    sums = jnp.stack([jnp.sum(grads[n].astype(F32), axis=0) for n in (0, 2)])
+    return *grads, sums
 
 
 def cross_query_grad_kernel(

time: 546 us -> 795 us (1.46)
  matrix products: 0 us -> 135 us
  local copies, waits for them, and re-layouts: 19.1 us -> 141 us
  Pallas kernels: 240 us -> 200 us
  other arithmetic: 22.3 us -> 54.5 us
    dot_general x0 -> x64, matrix products: none -> 135 us  [the longest x16 36.5 us: one(): jnp.einsum('hkd,hqd->hkq', v, grad_o, preferred_element_type=F32)]
    dynamic_slice x0 -> x32, local copies, waits for them, and re-layouts: none -> 46.2 us  [attend_grad(): lax.map(one, (*[pairs(a) for a in (query, key, value, mixed, grad_mixed)]...]
    pallas_call x2 -> x0, Pallas kernels: 39.4 us -> none  [attend_grad(): pl.pallas_call(attend_grad_kernel, grid=(pairs,), out_shape=[shape((rows,...]
    optimization_barrier x0 -> x17, local copies, waits for them, and re-layouts: none -> 38.7 us  [the longest x15 34.6 us: step(): inputs, operands = lax.optimization_barrier((tuple(inputs), operands))]
    reduce_sum x0 -> x20, other arithmetic: none -> 21.1 us  [the longest x16 16.8 us: one(): delta = jnp.sum(o.astype(F32) * grad_o.astype(F32), axis=-1)[:, None, :]]
    pallas_call x0 -> x8, local copies, waits for them, and re-layouts: none -> 16.6 us  [the longest x6 13.1 us: call(): pl.pallas_call(body, in_specs=specs, **settings)]
    convert_element_type x0 -> x8, local copies, waits for them, and re-layouts: none -> 13.9 us  [one(): exps.reshape(keys, 2, rows).swapaxes(0, 1).astype(F32)]
    convert_element_type x0 -> x8, other arithmetic: none -> 10 us  [one(): exps.reshape(keys, 2, rows).swapaxes(0, 1).astype(F32)]
  transfers between devices with their start and end apart: 50 -> 50, of which waited for: 18 -> 18; matrix products, arithmetic and copies ran while one was open for 3% -> 39% of each run, Pallas kernels for 38% -> 21%
where the time goes in v5:
time: 795 us; the launch traced here: 782 us
  Pallas kernels  200 us (25%)
  waiting for transfers between devices  187 us (24%)
  local copies, waits for them, and re-layouts  141 us (18%)
  matrix products  135 us (17%)
  other arithmetic  54.5 us (7%)
  starting transfers between devices  48.3 us (6%)
  between operations  15.5 us (2%)
    ppermute x6, waiting for transfers between devices, gather_fast(): moved.append(lax.ppermute(part, 'z', turns()[k]))  78.9 us
    pallas_call x8, Pallas kernels, call(): pl.pallas_call(body, in_specs=specs, **settings)  71.5 us
    ppermute x41, waiting for transfers between devices, step(): lax.ppermute(v, axis, pairs)  51.8 us
    all_gather x1, waiting for transfers between devices, gather_fast(): pack = lax.all_gather(shard, ALL, axis=0, tiled=False)  46.3 us
    dynamic_slice x32, local copies, waits for them, and re-layouts, attend_grad(): lax.map(one, (*[pairs(a) for a in (query, key, value, mixed, grad_mixed)]...  46.2 us
    pallas_call x3, Pallas kernels, weight_grads(): pl.pallas_call(functools.partial(weight_grads_kernel, jobs, len(lefts), l...  37.7 us
    dot_general x16, matrix products, one(): jnp.einsum('hkd,hqd->hkq', v, grad_o, preferred_element_type=F32)  36.5 us
    dot_general x16, matrix products, one(): jnp.einsum('hkq,hkd->hqd', grad_scores, k, preferred_element_type=F32)  36.3 us
  transfers between devices with their start and end apart: 50, of which 18 were waited for; matrix products, arithmetic and copies ran while one was open for 39% of the time, Pallas kernels for 21%

profile of v5, /device:TPU:0, one launch (start us, length us, event | category | flops | bytes accessed | tf_op | source)
XLA Modules:
  0.0 782.2 jit_solution(10646260729894208937)
XLA Ops:
  21.0 14.1 %collective-permute-done.7 = bf16[128,1024]{1,0:T(8,128)(2,1)S(1)} collective-permute-done((bf16[128,1024]{1,0:T(8,128)(2,1)S(1)}, bf16[128,1024]{1,0:T(8,128)(2,1)S(1)}, u32[]{:S(2)}, u32[]{:S(2)}) %collective-permute-start.7) | collective-permute-done | bytes 262176 | tf_op jit(solution)/shard_map/ppermute | solution.py:899
  38.6 14.8 %collective-permute-done.8 = bf16[128,1024]{1,0:T(8,128)(2,1)S(1)} collective-permute-done((bf16[128,1024]{1,0:T(8,128)(2,1)S(1)}, bf16[128,1024]{1,0:T(8,128)(2,1)S(1)}, u32[]{:S(2)}, u32[]{:S(2)}) %collective-permute-start.8) | collective-permute-done | bytes 262176 | tf_op jit(solution)/shard_map/ppermute | solution.py:899
  53.4 23.1 %collective-permute-done.9 = bf16[128,1024]{1,0:T(8,128)(2,1)S(1)} collective-permute-done((bf16[128,1024]{1,0:T(8,128)(2,1)S(1)}, bf16[128,1024]{1,0:T(8,128)(2,1)S(1)}, u32[]{:S(2)}, u32[]{:S(2)}) %collective-permute-start.9) | collective-permute-done | bytes 262176 | tf_op jit(solution)/shard_map/ppermute | solution.py:899
  76.6 13.6 %collective-permute-done.10 = bf16[128,1024]{1,0:T(8,128)(2,1)S(1)} collective-permute-done((bf16[128,1024]{1,0:T(8,128)(2,1)S(1)}, bf16[128,1024]{1,0:T(8,128)(2,1)S(1)}, u32[]{:S(2)}, u32[]{:S(2)}) %collective-permute-start.10) | collective-permute-done | bytes 262176 | tf_op jit(solution)/shard_map/ppermute | solution.py:899
  94.8 7.3 collective-permute-done.11
  107.2 46.3 %all-gather.6.cloned.1.call-done = bf16[8448,1024]{1,0:T(8,128)(2,1)} async-done(((bf16[264,1024]{1,0:T(8,128)(2,1)}), bf16[8448,1024]{1,0:T(8,128)(2,1)}) %all-gather.6.cloned.1.call-update) | async-done | bytes 17301520 | tf_op jit(solution)/shard_map/all_gather | solution.py:891
  161.4 9.0 %attend_causal.1 = (bf16[448,1024]{1,0:T(8,128)(2,1)}, bf16[8,448,896]{2,1,0:T(8,128)(2,1)}, f32[8,1,896]{2,1,0:T(1,128)}, f32[8,1,128]{2,1,0:T(1,128)S(1)}) custom-call(bf16[448,1024]{1,0:T(8,128)(2,1)S(1)} %get-tuple-element.360.q_ref, bf16[448,1024]{1,0:T(8,128)(2,1)S(1)} %get-tuple-element.361.k_ref, bf16[448,1024]{1,0:T(8,128)(2,1)S(1)} %get-tuple-element.362.v_ref), custom_call_target="tpu_custom_call" | custom-call | flops 3288334336 | bytes 1835008 | tf_op jit(solution)/shard_map/attend_causal/pallas_call | solution.py:251
  176.8 13.3 %cross_in.1 = (bf16[1504,1024]{1,0:T(8,128)(2,1)S(1)}, bf16[1504,1024]{1,0:T(8,128)(2,1)}) custom-call(s32[2]{0:T(128)S(1)} %pad_add_fusion.refs_0_.place_ref, bf16[1504,1024]{1,0:T(8,128)(2,1)} %pad.9.refs_1_.refs_0_, f32[17,1024]{1,0:T(8,128)S(1)} %convert_element_type.212.refs_2_.refs_3_.vec_ref.refs_4_.refs_6_, bf16[32,264,1024]{2,1,0:T(8,128)(2,1)} %bitcast.326, ...), custom_call_target="tpu_custom_call" | custom-call | flops 6308233216 | bytes 14680064 | tf_op jit(solution)/shard_map/cross_in/pallas_call | solution.py:86
  190.1 25.2 %attend.1 = (bf16[448,1024]{1,0:T(8,128)(2,1)S(1)}, bf16[8,1504,896]{2,1,0:T(8,128)(2,1)}, f32[8,1,896]{2,1,0:T(1,128)S(1)}, f32[8,1,128]{2,1,0:T(1,128)S(1)}) custom-call(bf16[448,1024]{1,0:T(8,128)(2,1)S(1)} %get-tuple-element.364.q_ref, bf16[1504,1024]{1,0:T(8,128)(2,1)S(1)} %get-tuple-element.365.k_ref, bf16[1504,1024]{1,0:T(8,128)(2,1)} %get-tuple-element.366.v_ref), custom_call_target="tpu_custom_call" | custom-call | flops 11039408128 | bytes 6160384 | tf_op jit(solution)/shard_map/attend/pallas_call | solution.py:251
  234.5 9.5 %all-gather.4.cloned.1.call-done.w1_ref.w2_ref = bf16[32,256,1024]{2,1,0:T(8,128)(2,1)} async-done(((bf16[4,256,1024]{2,1,0:T(8,128)(2,1)}), bf16[32,256,1024]{2,1,0:T(8,128)(2,1)}) %all-gather.4.cloned.1.call-update) | async-done | bytes 16777232 | tf_op jit(solution)/shard_map/all_gather | solution.py:904
  244.0 24.6 %feed.1 = (bf16[448,1024]{1,0:T(8,128)(2,1)}, bf16[448,4096]{1,0:T(8,128)(2,1)}, f32[8,1,512]{2,1,0:T(1,128)}, f32[1,1024]{1,0:T(1,128)}, bf16[8,4,128,1024]{3,2,1,0:T(8,128)(2,1)}) custom-call(bf16[448,1024]{1,0:T(8,128)(2,1)} %copy-done.18, f32[448,1024]{1,0:T(8,128)} %copy-done.6, bf16[448,1024]{1,0:T(8,128)(2,1)} %bitcast.373, f32[17,1024]{1,0:T(8,128)} %copy-done.2, ...), custom_call_target="tpu_custom_call" | custom-call | flops 15032385536 | bytes 31457280 | tf_op jit(solution)/shard_map/feed/pallas_call | solution.py:401
  279.4 9.4 %feed_grad.1.refs_1_ = f32[448,1024]{1,0:T(8,128)} custom-call(bf16[448,4096]{1,0:T(8,128)(2,1)} %get-tuple-element.405.df_ref.refs_2_, bf16[32,256,1024]{2,1,0:T(8,128)(2,1)} %all-gather.4.cloned.1.call-done.w1_ref.w2_ref), custom_call_target="tpu_custom_call" | custom-call | flops 3758096384 | bytes 12582912 | tf_op jit(solution)/shard_map/feed_grad/pallas_call | solution.py:442
  288.8 11.5 %weight_grads.3 = (bf16[2,4,64,1024]{3,2,1,0:T(8,128)(2,1)}, bf16[2,4,64,1024]{3,2,1,0:T(8,128)(2,1)}, bf16[2,4,64,1024]{3,2,1,0:T(8,128)(2,1)}, bf16[2,4,64,1024]{3,2,1,0:T(8,128)(2,1)}) custom-call(s32[2]{0:T(128)} %copy-done.15, bf16[448,1024]{1,0:T(8,128)(2,1)} %copy-done.18, bf16[448,1024]{1,0:T(8,128)(2,1)} %copy-done.63, ...), custom_call_target="tpu_custom_call" | custom-call | flops 3758096384 | bytes 12582912 | tf_op jit(solution)/shard_map/weight_grads/pallas_call | solution.py:622
  300.4 6.5 cross_out_grad.1
  311.2 128.1 %while.28 = (s32[]{:T(128)}, bf16[8,2,448,64]{2,3,1,0:T(8,128)(2,1)}, bf16[8,2,1504,64]{2,3,1,0:T(8,128)(2,1)}, bf16[8,2,1504,64]{2,3,1,0:T(8,128)(2,1)}, bf16[8...) while((s32[]{:T(128)}, ...), condition=%wide.region_2.3_spmd, body=%wide.region_0.2_spmd.sunk | while | flops 701664384 | bytes 44851924 | solution.py:515
  458.9 9.4 %cross_query_grad.1 = (f32[448,1024]{1,0:T(8,128)}, bf16[448,1024]{1,0:T(8,128)(2,1)}, bf16[448,1024]{1,0:T(8,128)(2,1)}, f32[3,1024]{1,0:T(4,128)}) custom-call(s32[2]{0:T(128)} %copy-done.15, bf16[448,1024]{1,0:T(8,128)(2,1)} %copy.99.refs_1_, f32[448,1024]{1,0:T(8,128)} %copy-done.1, f32[448,1024]{1,0:T(8,128)} %get-tuple-element.434.refs_3_, ...), custom_call_target="tpu_custom_call" | custom-call | flops 1879048192 | bytes 14680064 | tf_op jit(solution)/shard_map/cross_query_grad/pallas_call | solution.py:86
  487.7 16.6 %weight_grads.4 = (bf16[2,4,64,1024]{3,2,1,0:T(8,128)(2,1)}, bf16[2,4,64,1024]{3,2,1,0:T(8,128)(2,1)}, bf16[2,4,64,1024]{3,2,1,0:T(8,128)(2,1)}, bf16[2,4,64,1024]{3,2,1,0:T(8,128)(2,1)}) custom-call(s32[2]{0:T(128)} %copy-done.15, bf16[1504,1024]{1,0:T(8,128)(2,1)} %pad.9.refs_1_.refs_0_, bf16[1504,1024]{1,0:T(8,128)(2,1)} %collective-permute-done.5.refs_1_, ...), custom_call_target="tpu_custom_call" | custom-call | flops 8187281408 | bytes 12582912 | tf_op jit(solution)/shard_map/weight_grads/pallas_call | solution.py:622
  516.5 96.7 %while.29 = (s32[]{:T(128)}, bf16[8,2,448,64]{2,3,1,0:T(8,128)(2,1)}, bf16[8,2,448,64]{2,3,1,0:T(8,128)(2,1)}, bf16[8,2,448,64]{2,3,1,0:T(8,128)(2,1)}, bf16[8,4...) while((s32[]{:T(128)}, ...), condition=%wide.region_8.9_spmd, body=%wide.region_6.8_spmd.sunk | while | flops 208845952 | bytes 12550273 | solution.py:515
  622.3 10.9 %self_in_grad.1 = (f32[448,1024]{1,0:T(8,128)}, f32[2,1024]{1,0:T(2,128)}) custom-call(s32[2]{0:T(128)} %copy-done.15, bf16[448,1024]{1,0:T(8,128)(2,1)} %copy.110.refs_1_, bf16[448,1024]{1,0:T(8,128)(2,1)} %copy.111.refs_2_, bf16[448,1024]{1,0:T(8,128)(2,1)} %copy.112.refs_3_, bf16[448,1024]{1,0:T(8,128)(2,1)} %bitcast.318, ...), custom_call_target="tpu_custom_call" | custom-call | flops 2818572288 | bytes 14680064 | tf_op jit(solution)/shard_map/self_in_grad/pallas_call | solution.py:86
  634.6 9.2 %collective-permute-done.25 = bf16[2,128,1024]{2,1,0:T(8,128)(2,1)} collective-permute-done((bf16[2,128,1024]{2,1,0:T(8,128)(2,1)}, bf16[2,128,1024]{2,1,0:T(8,128)(2,1)}, u32[]{:S(2)}, u32[]{:S(2)}) %collective-permute-start.25) | collective-permute-done | bytes 524320 | tf_op jit(solution)/shard_map/ppermute | solution.py:742
  667.9 9.5 %weight_grads.5 = (bf16[2,4,64,1024]{3,2,1,0:T(8,128)(2,1)}, bf16[2,4,64,1024]{3,2,1,0:T(8,128)(2,1)}, bf16[2,4,64,1024]{3,2,1,0:T(8,128)(2,1)}, bf16[2,4,64,1024]{3,2,1,0:T(8,128)(2,1)}) custom-call(s32[2]{0:T(128)} %copy-done.15, bf16[448,1024]{1,0:T(8,128)(2,1)} %get-tuple-element.376.refs_1_.refs_0_, bf16[448,1024]{1,0:T(8,128)(2,1)} %collective-permute-done.2.refs_1_, ...), custom_call_target="tpu_custom_call" | custom-call | flops 3758096384 | bytes 12582912 | tf_op jit(solution)/shard_map/weight_grads/pallas_call | solution.py:622
  697.6 14.8 %encoder_grad.1 = f32[12000,128]{1,0:T(8,128)} custom-call(s32[2]{0:T(128)} %copy-done.15, bf16[1504,1024]{1,0:T(8,128)(2,1)} %copy.119.refs_1_, bf16[1504,1024]{1,0:T(8,128)(2,1)} %copy.120.refs_2_, bf16[32,264,1024]{2,1,0:T(8,128)(2,1)} %bitcast.334, bf16[32,264,1024]{2,1,0:T(8,128)(2,1)} %bitcast.335), custom_call_target="tpu_custom_call" | custom-call | flops 6308233216 | bytes 16777216 | tf_op jit(solution)/shard_map/encoder_grad/pallas_call | solution.py:86
  727.0 6.5 collective-permute-done.41
  747.4 19.8 %collective-permute-done.46 = f32[24,1024]{1,0:T(8,128)S(1)} collective-permute-done((f32[24,1024]{1,0:T(8,128)S(1)}, f32[24,1024]{1,0:T(8,128)S(1)}, u32[]{:S(2)}, u32[]{:S(2)}) %collective-permute-start.46) | collective-permute-done | bytes 98336 | tf_op jit(solution)/shard_map/ppermute | solution.py:742
  (550 shorter events, 440.6 us)
Async XLA Ops:
  7.2 146.3 %all-gather.6.cloned.1.call-start = ((), (), s32[]{:S(2)}) async-start(), calls=%async_computation.3 | async-start | bytes 17842176 | tf_op jit(solution)/shard_map/all_gather | solution.py:891
  9.7 234.3 %all-gather.4.cloned.1.call-start = ((), (), s32[]{:S(2)}) async-start(), calls=%async_computation.1 | async-start | bytes 18874368 | tf_op jit(solution)/shard_map/all_gather | solution.py:904
  53.3 23.2 %collective-permute-start.9 = (bf16[128,1024]{1,0:T(8,128)(2,1)S(1)}, bf16[128,1024]{1,0:T(8,128)(2,1)S(1)}, u32[]{:S(2)}, u32[]{:S(2)}) collective-permute-start(bf16[128,1024]{1,0:T(8,128)(2,1)S(1)} %convert_element_type.214), channel_id=1, source_target_pairs={{0,3},{1,0},{2,1},{3,2},{4,7},{5,4},{6,5},{7,6},{8,11},{9,8},{10,9... | collective-permute-start | bytes 786440 | tf_op jit(solution)/shard_map/ppermute | solution.py:899
  104.1 404.5 %reduce-scatter.2.cloned.1.call-start = ((), (), s32[]{:S(2)}) async-start(), calls=%async_computation.2 | async-start | bytes 9437184 | tf_op jit(solution)/shard_map/reduce_scatter | solution.py:1035
  268.6 20.3 %collective-permute-start.12 = (bf16[448,4096]{1,0:T(8,128)(2,1)}, bf16[448,4096]{1,0:T(8,128)(2,1)}, u32[]{:S(2)}, u32[]{:S(2)}) collective-permute-start(bf16[448,4096]{1,0:T(8,128)(2,1)} %get-tuple-element.405.df_ref.refs_2_), channel_id=1, source_target_pairs={{0,4},{4,0},{1,5},{5,1},{2,6},{6,2},{3,7},{7,3},{8,12},{12,8},{9,1... | collective-permute-start | bytes 11010056 | tf_op jit(solution)/shard_map/ppermute | solution.py:742
  308.3 135.6 %collective-permute-start.13 = (bf16[448,1024]{1,0:T(8,128)(2,1)}, bf16[448,1024]{1,0:T(8,128)(2,1)}, u32[]{:S(2)}, u32[]{:S(2)}) collective-permute-start(bf16[448,1024]{1,0:T(8,128)(2,1)} %get-tuple-element.464.refs_12_), channel_id=1, source_target_pairs={{0,4},{4,0},{1,5},{5,1},{2,6},{6,2},{3,7},{7,3},{8,12},{12,8},{9,1... | collective-permute-start | bytes 2752520 | tf_op jit(solution)/shard_map/ppermute | solution.py:742
  308.6 135.3 %collective-permute-start.14 = (bf16[2,4,64,1024]{3,2,1,0:T(8,128)(2,1)}, bf16[2,4,64,1024]{3,2,1,0:T(8,128)(2,1)}, u32[]{:S(2)}, u32[]{:S(2)}) collective-permute-start(bf16[2,4,64,1024]{3,2,1,0:T(8,128)(2,1)} %get-tuple-element.428), channel_id=1, source_target_pairs={{0,8},{8,0},{1,9},{9,1},{2,10},{10,2},{3,11},{11,3},{4,12},{12,4},... | collective-permute-start | bytes 3145736 | tf_op jit(solution)/shard_map/ppermute | solution.py:742
  309.8 134.2 %collective-permute-start.15 = (bf16[2,4,64,1024]{3,2,1,0:T(8,128)(2,1)}, bf16[2,4,64,1024]{3,2,1,0:T(8,128)(2,1)}, u32[]{:S(2)}, u32[]{:S(2)}) collective-permute-start(bf16[2,4,64,1024]{3,2,1,0:T(8,128)(2,1)} %get-tuple-element.429), channel_id=1, source_target_pairs={{0,16},{16,0},{1,17},{17,1},{2,18},{18,2},{3,19},{19,3},{4,20},{20... | collective-permute-start | bytes 3145736 | tf_op jit(solution)/shard_map/ppermute | solution.py:742
  448.7 19.6 %collective-permute-start.17 = (bf16[1504,1024]{1,0:T(8,128)(2,1)}, bf16[1504,1024]{1,0:T(8,128)(2,1)}, u32[]{:S(2)}, u32[]{:S(2)}) collective-permute-start(bf16[1504,1024]{1,0:T(8,128)(2,1)} %copy.101), channel_id=1, source_target_pairs={{0,4},{4,0},{1,5},{5,1},{2,6},{6,2},{3,7},{7,3},{8,12},{12,8},{9,1... | collective-permute-start | bytes 9240584 | tf_op jit(solution)/shard_map/ppermute | solution.py:742
  468.3 36.0 %collective-permute-start.19 = (bf16[448,1024]{1,0:T(8,128)(2,1)}, bf16[448,1024]{1,0:T(8,128)(2,1)}, u32[]{:S(2)}, u32[]{:S(2)}) collective-permute-start(bf16[448,1024]{1,0:T(8,128)(2,1)} %get-tuple-element.524.refs_4_), channel_id=1, source_target_pairs={{0,4},{4,0},{1,5},{5,1},{2,6},{6,2},{3,7},{7,3},{8,12},{12,8},{9,1... | collective-permute-start | bytes 2752520 | tf_op jit(solution)/shard_map/ppermute | solution.py:742
  485.1 19.2 %collective-permute-start.20 = (bf16[4,64,1024]{2,1,0:T(8,128)(2,1)}, bf16[4,64,1024]{2,1,0:T(8,128)(2,1)S(1)}, u32[]{:S(2)}, u32[]{:S(2)}) collective-permute-start(bf16[4,64,1024]{2,1,0:T(8,128)(2,1)} %get-tuple-element.471), channel_id=1, source_target_pairs={{0,16},{16,0},{1,17},{17,1},{2,18},{18,2},{3,19},{19,3},{4,20},{20... | collective-permute-start | bytes 1572872 | tf_op jit(solution)/shard_map/ppermute | solution.py:742
  511.8 132.0 %collective-permute-start.22 = (bf16[2,4,64,1024]{3,2,1,0:T(8,128)(2,1)}, bf16[2,4,64,1024]{3,2,1,0:T(8,128)(2,1)}, u32[]{:S(2)}, u32[]{:S(2)}) collective-permute-start(bf16[2,4,64,1024]{3,2,1,0:T(8,128)(2,1)} %get-tuple-element.488), channel_id=1, source_target_pairs={{0,8},{8,0},{1,9},{9,1},{2,10},{10,2},{3,11},{11,3},{4,12},{12,4},... | collective-permute-start | bytes 3145736 | tf_op jit(solution)/shard_map/ppermute | solution.py:742
  512.9 130.9 %collective-permute-start.23 = (bf16[2,4,64,1024]{3,2,1,0:T(8,128)(2,1)}, bf16[2,4,64,1024]{3,2,1,0:T(8,128)(2,1)}, u32[]{:S(2)}, u32[]{:S(2)}) collective-permute-start(bf16[2,4,64,1024]{3,2,1,0:T(8,128)(2,1)} %get-tuple-element.489), channel_id=1, source_target_pairs={{0,16},{16,0},{1,17},{17,1},{2,18},{18,2},{3,19},{19,3},{4,20},{20... | collective-permute-start | bytes 3145736 | tf_op jit(solution)/shard_map/ppermute | solution.py:742
  620.9 22.9 %collective-permute-start.25 = (bf16[2,128,1024]{2,1,0:T(8,128)(2,1)}, bf16[2,128,1024]{2,1,0:T(8,128)(2,1)}, u32[]{:S(2)}, u32[]{:S(2)}) collective-permute-start(bf16[2,128,1024]{2,1,0:T(8,128)(2,1)} %pad_maximum_fusion.1), channel_id=1, source_target_pairs={{0,1},{1,0},{2,3},{3,2},{4,5},{5,4},{6,7},{7,6},{8,9},{9,8},{10,11... | collective-permute-start | bytes 1572872 | tf_op jit(solution)/shard_map/ppermute | solution.py:742
  655.8 23.0 %collective-permute-start.30 = (bf16[4,64,1024]{2,1,0:T(8,128)(2,1)}, bf16[4,64,1024]{2,1,0:T(8,128)(2,1)}, u32[]{:S(2)}, u32[]{:S(2)}) collective-permute-start(bf16[4,64,1024]{2,1,0:T(8,128)(2,1)} %get-tuple-element.536), channel_id=1, source_target_pairs={{0,16},{16,0},{1,17},{17,1},{2,18},{18,2},{3,19},{19,3},{4,20},{20... | collective-permute-start | bytes 1572872 | tf_op jit(solution)/shard_map/ppermute | solution.py:742
  657.5 21.4 %collective-permute-start.31 = (bf16[4,64,1024]{2,1,0:T(8,128)(2,1)}, bf16[4,64,1024]{2,1,0:T(8,128)(2,1)}, u32[]{:S(2)}, u32[]{:S(2)}) collective-permute-start(bf16[4,64,1024]{2,1,0:T(8,128)(2,1)} %get-tuple-element.537), channel_id=1, source_target_pairs={{0,8},{8,0},{1,9},{9,1},{2,10},{10,2},{3,11},{11,3},{4,12},{12,4},... | collective-permute-start | bytes 1572872 | tf_op jit(solution)/shard_map/ppermute | solution.py:742
  682.8 30.9 %collective-permute-start.34 = (bf16[2,4,64,1024]{3,2,1,0:T(8,128)(2,1)}, bf16[2,4,64,1024]{3,2,1,0:T(8,128)(2,1)}, u32[]{:S(2)}, u32[]{:S(2)}) collective-permute-start(bf16[2,4,64,1024]{3,2,1,0:T(8,128)(2,1)} %get-tuple-element.550), channel_id=1, source_target_pairs={{0,8},{8,0},{1,9},{9,1},{2,10},{10,2},{3,11},{11,3},{4,12},{12,4},... | collective-permute-start | bytes 3145736 | tf_op jit(solution)/shard_map/ppermute | solution.py:742
  683.9 29.8 %collective-permute-start.35 = (bf16[2,4,64,1024]{3,2,1,0:T(8,128)(2,1)}, bf16[2,4,64,1024]{3,2,1,0:T(8,128)(2,1)}, u32[]{:S(2)}, u32[]{:S(2)}) collective-permute-start(bf16[2,4,64,1024]{3,2,1,0:T(8,128)(2,1)} %get-tuple-element.551), channel_id=1, source_target_pairs={{0,16},{16,0},{1,17},{17,1},{2,18},{18,2},{3,19},{19,3},{4,20},{20... | collective-permute-start | bytes 3145736 | tf_op jit(solution)/shard_map/ppermute | solution.py:742
  692.0 21.7 %collective-permute-start.36 = (bf16[2,128,1024]{2,1,0:T(8,128)(2,1)S(1)}, bf16[2,128,1024]{2,1,0:T(8,128)(2,1)S(1)}, u32[]{:S(2)}, u32[]{:S(2)}) collective-permute-start(bf16[2,128,1024]{2,1,0:T(8,128)(2,1)S(1)} %copy-done.64), channel_id=1, source_target_pairs={{0,1},{1,0},{2,3},{3,2},{4,5},{5,4},{6,7},{7,6},{8,9},{9,8},{10,11... | collective-permute-start | bytes 1572872 | tf_op jit(solution)/shard_map/ppermute | solution.py:742
  692.7 21.0 %collective-permute-start.37 = (bf16[128,1024]{1,0:T(8,128)(2,1)S(1)}, bf16[128,1024]{1,0:T(8,128)(2,1)S(1)}, u32[]{:S(2)}, u32[]{:S(2)}) collective-permute-start(bf16[128,1024]{1,0:T(8,128)(2,1)S(1)} %copy-done.54), channel_id=1, source_target_pairs={{0,2},{2,0},{1,3},{3,1},{4,6},{6,4},{5,7},{7,5},{8,10},{10,8},{9,1... | collective-permute-start | bytes 786440 | tf_op jit(solution)/shard_map/ppermute | solution.py:742
  737.6 29.6 %collective-permute-start.43 = (bf16[128,1024]{1,0:T(8,128)(2,1)}, bf16[128,1024]{1,0:T(8,128)(2,1)S(1)}, u32[]{:S(2)}, u32[]{:S(2)}) collective-permute-start(bf16[128,1024]{1,0:T(8,128)(2,1)} %get-tuple-element.578), channel_id=1, source_target_pairs={{0,1},{1,2},{2,3},{3,0},{4,5},{5,6},{6,7},{7,4},{8,9},{9,10},{10,1... | collective-permute-start | bytes 786440 | tf_op jit(solution)/shard_map/ppermute | solution.py:742
  737.6 29.5 %collective-permute-start.44 = (bf16[128,1024]{1,0:T(8,128)(2,1)}, bf16[128,1024]{1,0:T(8,128)(2,1)S(1)}, u32[]{:S(2)}, u32[]{:S(2)}) collective-permute-start(bf16[128,1024]{1,0:T(8,128)(2,1)} %get-tuple-element.579), channel_id=1, source_target_pairs={{0,3},{1,0},{2,1},{3,2},{4,7},{5,4},{6,5},{7,6},{8,11},{9,8},{10,9... | collective-permute-start | bytes 786440 | tf_op jit(solution)/shard_map/ppermute | solution.py:742
  741.7 25.4 %collective-permute-start.45 = (bf16[128,1024]{1,0:T(8,128)(2,1)}, bf16[128,1024]{1,0:T(8,128)(2,1)S(1)}, u32[]{:S(2)}, u32[]{:S(2)}) collective-permute-start(bf16[128,1024]{1,0:T(8,128)(2,1)} %get-tuple-element.580), channel_id=1, source_target_pairs={{0,2},{1,3},{2,0},{3,1},{4,6},{5,7},{6,4},{7,5},{8,10},{9,11},{10,... | collective-permute-start | bytes 786440 | tf_op jit(solution)/shard_map/ppermute | solution.py:742
  744.3 22.8 %collective-permute-start.46 = (f32[24,1024]{1,0:T(8,128)S(1)}, f32[24,1024]{1,0:T(8,128)S(1)}, u32[]{:S(2)}, u32[]{:S(2)}) collective-permute-start(f32[24,1024]{1,0:T(8,128)S(1)} %maximum_select_fusion.1), channel_id=1, source_target_pairs={{0,2},{2,0},{1,3},{3,1},{4,6},{6,4},{5,7},{7,5},{8,10},{10,8},{9,1... | collective-permute-start | bytes 294920 | tf_op jit(solution)/shard_map/ppermute | solution.py:742
  (112 other events, 1076.1 us)
Sparse Core Ops, SparseCore 0:
  11.4 142.0 all-gather.5
  155.9 88.0 all-gather.3
  279.5 89.7 reduce-scatter.1
